TPU v7x, 512 devices: a whole 4x4x16 slice. The times are simulated.
512 devices in a mesh: wide: 64 (over z, y), narrow: 8 (over x, core).
Axes of the slice: x: 4, y: 4, z: 16, core: 2. Of those that a mesh axis runs over, the one named last changes fastest.
Arguments:
- rhs_field: float32 [512, 64, 512], P('wide', 'narrow'), may hold values from -6 to 6
- beta_cells: float32 [512, 64, 512], P('wide', 'narrow'), may hold values from 0.25 to 4
Outputs:
- solution_field: float32 [512, 64, 512], P('wide', 'narrow')
All inputs are finite; a program needn't handle non-finite values.
Results may differ from a plain program's by a relative error of at most 0.0001.
Values sent between devices are 32-bit elements; how exact they have to be, the bound alone decides.
No kernel may reach another device: no remote copies, remote signals or barrier semaphores. Data moves between devices by JAX's collectives and lax.ppermute only.
A program may use at most 64 MiB of HBM per device.

v0:
```python
import jax
import jax.numpy as jnp
from jax import lax
from jax.sharding import PartitionSpec as P

SWEEPS = 2
COARSE_SWEEPS = 8


LOW_BOUND = 0.25
HIGH_BOUND = 2.0


def padded_2(array, sides, width):
    for axis, dim in sides:
        count, length = (lax.axis_size(axis), array.shape[dim])
        up = [(i, (i + 1) % count) for i in range(count - 1)]
        down = [(j, i) for i, j in up]
        last = lax.slice_in_dim(array, length - width, length, axis=dim)
        initial = lax.slice_in_dim(array, 0, width, axis=dim)
        before = lax.ppermute(last, axis, up)
        after = lax.ppermute(initial, axis, down)
        array = jnp.concatenate([before, array, after], axis=dim)
    return array


def face_terms(padded, scale):
    face_x = scale * 0.5 * (padded[:-1, 1:-1, 1:-1] + padded[1:, 1:-1, 1:-1])
    face_y = scale * 0.5 * (padded[1:-1, :-1, 1:-1] + padded[1:-1, 1:, 1:-1])
    face_z = scale * 0.5 * (padded[1:-1, 1:-1, :-1] + padded[1:-1, 1:-1, 1:])
    diagonal = (
        face_x[1:]
        + face_x[:-1]
        + face_y[:, 1:]
        + face_y[:, :-1]
        + face_z[:, :, 1:]
        + face_z[:, :, :-1]
    )
    return (face_x, face_y, face_z, diagonal)


def apply_operator(padded, faces):
    face_x, face_y, face_z, diagonal = faces
    center = padded[1:-1, 1:-1, 1:-1]
    result = diagonal * center
    result = result - face_x[1:] * padded[2:, 1:-1, 1:-1] - face_x[:-1] * padded[:-2, 1:-1, 1:-1]
    result = (
        result - face_y[:, 1:] * padded[1:-1, 2:, 1:-1] - face_y[:, :-1] * padded[1:-1, :-2, 1:-1]
    )
    result = (
        result
        - face_z[:, :, 1:] * padded[1:-1, 1:-1, 2:]
        - face_z[:, :, :-1] * padded[1:-1, 1:-1, :-2]
    )
    return result


def chebyshev(source, start, sweeps, pad_fn, faces, from_zero):
    center_value = 0.5 * (HIGH_BOUND + LOW_BOUND)
    half_width = 0.5 * (HIGH_BOUND - LOW_BOUND)
    sigma_value = center_value / half_width
    rho_now = 1.0 / sigma_value
    iterate = start
    direction = start
    for sweep_index in range(sweeps):
        if sweep_index == 0 and from_zero:
            defect = source
        else:
            defect = source - apply_operator(pad_fn(iterate), faces)
        scaled = defect / faces[3]
        if sweep_index == 0:
            direction = scaled / center_value
        else:
            rho_next = 1.0 / (2.0 * sigma_value - rho_now)
            direction = rho_next * rho_now * direction + 2.0 * rho_next / half_width * scaled
            rho_now = rho_next
        iterate = iterate + direction
    return iterate


def conjugate(source, iterations, pad_fn, faces):
    iterate = jnp.zeros_like(source)
    remainder = source
    direction = source
    norm_now = jnp.sum(remainder * remainder)
    for step_index in range(iterations):
        image = apply_operator(pad_fn(direction), faces)
        alpha = norm_now / jnp.sum(direction * image)
        iterate = iterate + alpha * direction
        remainder = remainder - alpha * image
        norm_next = jnp.sum(remainder * remainder)
        direction = remainder + norm_next / norm_now * direction
        norm_now = norm_next
    return iterate


def restrict(values):
    first, second, third = values.shape
    return values.reshape(first // 2, 2, second // 2, 2, third // 2, 2).mean(axis=(1, 3, 5))


def prolong(values):
    return jnp.repeat(jnp.repeat(jnp.repeat(values, 2, axis=0), 2, axis=1), 2, axis=2)


def pad_depth(values):
    return jnp.pad(values, ((0, 0), (0, 0), (1, 1)))


def pad_bricks(values):
    return pad_depth(padded_2(values, (("wide", 0), ("narrow", 1)), 1))


def pad_groups(values):
    extended = padded_2(values, (("wide", 0),), 1)
    return pad_depth(jnp.pad(extended, ((0, 0), (1, 1), (0, 0))))


def pad_local(values):
    return jnp.pad(values, 1)


def descend(source, cells, level, pad_fn):
    faces = face_terms(pad_fn(cells), 0.25**level)
    iterate = chebyshev(source, jnp.zeros_like(source), SWEEPS, pad_fn, faces, True)
    residual = source - apply_operator(pad_fn(iterate), faces)
    return (faces, iterate, restrict(residual), restrict(cells))


def shards(rhs_field, beta_cells):
    faces_zero, iterate_zero, source_one, cells_one = descend(rhs_field, beta_cells, 0, pad_bricks)
    faces_one, iterate_one, source_two, cells_two = descend(source_one, cells_one, 1, pad_bricks)
    group_source, group_cells = (
        lax.all_gather(source_two, "narrow", axis=1, tiled=True),
        lax.all_gather(cells_two, "narrow", axis=1, tiled=True),
    )
    faces_two, iterate_two, source_three, cells_three = descend(
        group_source, group_cells, 2, pad_groups
    )
    coarse_source, coarse_cells = (
        lax.all_gather(source_three, "wide", axis=0, tiled=True),
        lax.all_gather(cells_three, "wide", axis=0, tiled=True),
    )
    coarse_faces = face_terms(pad_local(coarse_cells), 0.25**3)
    coarse_iterate = conjugate(coarse_source, COARSE_SWEEPS, pad_local, coarse_faces)
    group_width = source_three.shape[0]
    group_piece = lax.dynamic_slice_in_dim(
        coarse_iterate, lax.axis_index("wide") * group_width, group_width, 0
    )
    brick_rows = source_two.shape[1]
    level_two = chebyshev(
        group_source, iterate_two + prolong(group_piece), SWEEPS, pad_groups, faces_two, False
    )
    brick_two = lax.dynamic_slice_in_dim(
        level_two, lax.axis_index("narrow") * brick_rows, brick_rows, 1
    )
    level_one = chebyshev(
        source_one, iterate_one + prolong(brick_two), SWEEPS, pad_bricks, faces_one, False
    )
    return chebyshev(
        rhs_field, iterate_zero + prolong(level_one), SWEEPS, pad_bricks, faces_zero, False
    )


def solution(mesh):
    return jax.shard_map(
        shards,
        mesh=mesh,
        in_specs=(P("wide", "narrow", None), P("wide", "narrow", None)),
        out_specs=P("wide", "narrow", None),
        check_vma=False,
    )
```

profile of v0, /device:TPU:130, one launch (start us, length us, event | category | flops | bytes accessed | tf_op | source)
XLA Modules:
  0.0 494.6 jit_solution(11182286559199135034)
XLA Ops:
  0.7 3.5 collective-permute-start
  4.2 5.7 %collective-permute-start.1 = (f32[1,8,512]{2,1,0:T(8,128)S(1)}, f32[1,8,512]{2,1,0:T(8,128)S(1)}, u32[]{:S(2)}, u32[]{:S(2)}) collective-permute-start(f32[1,8,512]{2,1,0:T(8,128)S(1)} %get-tuple-element.64), channel_id=1, source_target_pairs={{8,0},{16,8},{24,16},{32,24},{40,32},{48,40},{56,48},{64,56},{72,6... | collective-permute-start | bytes 49160 | tf_op jit(solution)/shard_map/ppermute | solution.py:22
  9.9 10.5 %reshape.64 = f32[4,2,4,2,256,2]{5,4,3,2,1,0:T(8,128)} reshape(f32[8,8,512]{2,1,0:T(8,128)} %param.3) | data formatting | bytes 262144 | tf_op jit(solution)/shard_map/reshape | solution.py:99
  20.4 4.1 reduce_sum.213
  26.5 7.2 %collective-permute-start.13 = (f32[1,4,256]{2,1,0:T(4,128)S(1)}, f32[1,4,256]{2,1,0:T(4,128)S(1)}, u32[]{:S(2)}, u32[]{:S(2)}) collective-permute-start(f32[1,4,256]{2,1,0:T(4,128)S(1)} %get-tuple-element.97), channel_id=1, source_target_pairs={{8,0},{16,8},{24,16},{32,24},{40,32},{48,40},{56,48},{64,56},{72,6... | collective-permute-start | bytes 12296 | tf_op jit(solution)/shard_map/ppermute | solution.py:22
  34.9 11.6 %all_gather.13 = f32[2,16,128]{2,0,1:T(2,128)S(1)} all-gather(f32[2,2,128]{2,0,1:T(2,128)S(1)} %copy.516), channel_id=1, replica_groups=mesh['wide'=64,'narrow'=8] {'narrow'}, dimensions={1}, use_global_device_ids=true | all-gather | bytes 18432 | tf_op jit(solution)/shard_map/all_gather | solution.py:135
  49.2 83.8 %all-gather.1 = f32[512,64]{1,0:T(8,128)S(1)} all-gather(f32[8,64]{1,0:T(8,128)S(1)} %broadcast_multiply_fusion.5), channel_id=3, replica_groups=mesh['wide'=64,'narrow'=8] {'wide'}, dimensions={0}, use_global_device_ids=true | all-gather | bytes 133120 | tf_op jit(solution)/shard_map/all_gather | solution.py:142
  133.1 4.5 collective-permute-start.25
  139.7 2.8 collective-permute-start.2
  142.5 2.7 collective-permute-start.3
  147.3 4.0 collective-permute-start.4
  153.3 3.4 collective-permute-start.15
  156.6 3.6 collective-permute-done.5
  164.8 2.8 collective-permute-done.7
  168.2 3.1 collective-permute-start.8
  171.3 2.8 collective-permute-start.9
  174.1 6.1 %collective-permute-done.9 = f32[1,8,512]{2,1,0:T(8,128)S(1)} collective-permute-done((f32[1,8,512]{2,1,0:T(8,128)S(1)}, f32[1,8,512]{2,1,0:T(8,128)S(1)}, u32[]{:S(2)}, u32[]{:S(2)}) %collective-permute-start.9) | collective-permute-done | bytes 16416 | tf_op jit(solution)/shard_map/ppermute | solution.py:21
  184.6 2.6 collective-permute-done.11
  187.8 9.8 %reshape.63 = f32[4,2,4,2,256,2]{5,4,3,2,1,0:T(8,128)} reshape(f32[8,8,512]{2,1,0:T(8,128)S(1)} %fusion.137) | data formatting | bytes 262144 | tf_op jit(solution)/shard_map/reshape | solution.py:99
  197.6 4.0 reduce_sum.212
  203.6 3.9 collective-permute-start.17
  207.6 4.8 collective-permute-done.17
  216.8 2.5 collective-permute-done.19
  221.5 3.9 collective-permute-start.21
  225.6 4.8 collective-permute-done.21
  234.8 2.5 collective-permute-done.23
  238.7 11.0 %all_gather.12 = f32[2,16,128]{2,0,1:T(2,128)S(1)} all-gather(f32[2,2,128]{2,0,1:T(2,128)S(1)} %copy.515), channel_id=1, replica_groups=mesh['wide'=64,'narrow'=8] {'narrow'}, dimensions={1}, use_global_device_ids=true | all-gather | bytes 18432 | tf_op jit(solution)/shard_map/all_gather | solution.py:134
  251.7 4.1 collective-permute-start.27
  255.9 4.7 collective-permute-done.27
  262.7 3.9 collective-permute-start.29
  266.8 4.8 collective-permute-done.29
  272.4 78.6 %all-gather = f32[512,64]{1,0:T(8,128)S(1)} all-gather(f32[8,64]{1,0:T(8,128)S(1)} %broadcast_multiply_fusion.6), channel_id=2, replica_groups=mesh['wide'=64,'narrow'=8] {'wide'}, dimensions={0}, use_global_device_ids=true | all-gather | bytes 133120 | tf_op jit(solution)/shard_map/all_gather | solution.py:141
  387.7 4.6 collective-permute-start.30
  394.3 6.9 %collective-permute-done.31 = f32[1,16,128]{2,0,1:T(1,128)S(1)} collective-permute-done((f32[1,16,128]{2,0,1:T(1,128)S(1)}, f32[1,16,128]{2,0,1:T(1,128)S(1)}, u32[]{:S(2)}, u32[]{:S(2)}) %collective-permute-start.31) | collective-permute-done | bytes 8224 | tf_op jit(solution)/shard_map/ppermute | solution.py:21
  404.2 3.9 collective-permute-start.33
  408.1 4.9 collective-permute-done.33
  418.0 3.9 collective-permute-start.35
  421.9 4.9 collective-permute-done.35
  431.2 2.5 collective-permute-done.37
  436.7 3.9 collective-permute-start.39
  440.6 4.9 collective-permute-done.39
  449.9 2.5 collective-permute-done.41
  458.9 3.9 collective-permute-start.43
  462.8 5.0 %collective-permute-done.43 = f32[1,8,512]{2,1,0:T(8,128)S(1)} collective-permute-done((f32[1,8,512]{2,1,0:T(8,128)S(1)}, f32[1,8,512]{2,1,0:T(8,128)S(1)}, u32[]{:S(2)}, u32[]{:S(2)}) %collective-permute-start.43) | collective-permute-done | bytes 16416 | tf_op jit(solution)/shard_map/ppermute | solution.py:21
  472.2 2.7 collective-permute-done.45
  477.4 3.9 collective-permute-start.47
  481.3 5.0 %collective-permute-done.47 = f32[1,8,512]{2,1,0:T(8,128)S(1)} collective-permute-done((f32[1,8,512]{2,1,0:T(8,128)S(1)}, f32[1,8,512]{2,1,0:T(8,128)S(1)}, u32[]{:S(2)}, u32[]{:S(2)}) %collective-permute-start.47) | collective-permute-done | bytes 16416 | tf_op jit(solution)/shard_map/ppermute | solution.py:21
  490.7 2.7 collective-permute-done.49
  (210 shorter events, 99.1 us)
Async XLA Ops:
  0.7 138.8 %collective-permute-start = (f32[1,8,512]{2,1,0:T(8,128)S(1)}, f32[1,8,512]{2,1,0:T(8,128)S(1)}, u32[]{:S(2)}, u32[]{:S(2)}) collective-permute-start(f32[1,8,512]{2,1,0:T(8,128)S(1)} %get-tuple-element.65), channel_id=1, source_target_pairs={{0,8},{8,16},{16,24},{24,32},{32,40},{40,48},{48,56},{56,64},{64,7... | collective-permute-start | bytes 49160 | tf_op jit(solution)/shard_map/ppermute | solution.py:21
  4.2 135.4 %collective-permute-start.1 = (f32[1,8,512]{2,1,0:T(8,128)S(1)}, f32[1,8,512]{2,1,0:T(8,128)S(1)}, u32[]{:S(2)}, u32[]{:S(2)}) collective-permute-start(f32[1,8,512]{2,1,0:T(8,128)S(1)} %get-tuple-element.64), channel_id=1, source_target_pairs={{8,0},{16,8},{24,16},{32,24},{40,32},{48,40},{56,48},{64,56},{72,6... | collective-permute-start | bytes 49160 | tf_op jit(solution)/shard_map/ppermute | solution.py:22
  24.5 108.5 %collective-permute-start.12 = (f32[1,4,256]{2,1,0:T(4,128)S(1)}, f32[1,4,256]{2,1,0:T(4,128)S(1)}, u32[]{:S(2)}, u32[]{:S(2)}) collective-permute-start(f32[1,4,256]{2,1,0:T(4,128)S(1)} %get-tuple-element.96), channel_id=1, source_target_pairs={{0,8},{8,16},{16,24},{24,32},{32,40},{40,48},{48,56},{56,64},{64,7... | collective-permute-start | bytes 12296 | tf_op jit(solution)/shard_map/ppermute | solution.py:21
  26.5 111.1 %collective-permute-start.13 = (f32[1,4,256]{2,1,0:T(4,128)S(1)}, f32[1,4,256]{2,1,0:T(4,128)S(1)}, u32[]{:S(2)}, u32[]{:S(2)}) collective-permute-start(f32[1,4,256]{2,1,0:T(4,128)S(1)} %get-tuple-element.97), channel_id=1, source_target_pairs={{8,0},{16,8},{24,16},{32,24},{40,32},{48,40},{56,48},{64,56},{72,6... | collective-permute-start | bytes 12296 | tf_op jit(solution)/shard_map/ppermute | solution.py:22
  46.6 161.0 %collective-permute-start.24 = (f32[1,16,128]{2,0,1:T(1,128)S(1)}, f32[1,16,128]{2,0,1:T(1,128)S(1)}, u32[]{:S(2)}, u32[]{:S(2)}) collective-permute-start(f32[1,16,128]{2,0,1:T(1,128)S(1)} %get-tuple-element.90), channel_id=1, source_target_pairs={{0,8},{8,16},{16,24},{24,32},{32,40},{40,48},{48,56},{56,64},{64,7... | collective-permute-start | bytes 24584 | tf_op jit(solution)/shard_map/ppermute | solution.py:21
  133.1 74.5 %collective-permute-start.25 = (f32[1,16,128]{2,0,1:T(1,128)S(1)}, f32[1,16,128]{2,0,1:T(1,128)S(1)}, u32[]{:S(2)}, u32[]{:S(2)}) collective-permute-start(f32[1,16,128]{2,0,1:T(1,128)S(1)} %get-tuple-element.91), channel_id=1, source_target_pairs={{8,0},{16,8},{24,16},{32,24},{40,32},{48,40},{56,48},{64,56},{72,6... | collective-permute-start | bytes 24584 | tf_op jit(solution)/shard_map/ppermute | solution.py:22
  137.6 24.9 %collective-permute-start.14 = (f32[6,1,256]{2,1,0:T(1,128)S(1)}, f32[6,1,256]{2,1,0:T(1,128)S(1)}, u32[]{:S(2)}, u32[]{:S(2)}) collective-permute-start(f32[6,1,256]{2,1,0:T(1,128)S(1)} %get-tuple-element.76), channel_id=1, source_target_pairs={{0,1},{1,2},{2,3},{3,4},{4,5},{5,6},{6,7},{8,9},{9,10},{10,11},{11... | collective-permute-start | bytes 18440 | tf_op jit(solution)/shard_map/ppermute | solution.py:21
  139.7 5.6 %collective-permute-start.2 = (f32[10,1,512]{2,1,0:T(1,128)S(1)}, f32[10,1,512]{2,1,0:T(1,128)S(1)}, u32[]{:S(2)}, u32[]{:S(2)}) collective-permute-start(f32[10,1,512]{2,1,0:T(1,128)S(1)} %get-tuple-element.54), channel_id=1, source_target_pairs={{0,1},{1,2},{2,3},{3,4},{4,5},{5,6},{6,7},{8,9},{9,10},{10,11},{11... | collective-permute-start | bytes 61448 | tf_op jit(solution)/shard_map/ppermute | solution.py:21
  147.3 5.9 %collective-permute-start.4 = (f32[1,8,512]{2,1,0:T(8,128)S(1)}, f32[1,8,512]{2,1,0:T(8,128)S(1)}, u32[]{:S(2)}, u32[]{:S(2)}) collective-permute-start(f32[1,8,512]{2,1,0:T(8,128)S(1)} %get-tuple-element.63), channel_id=1, source_target_pairs={{8,0},{16,8},{24,16},{32,24},{40,32},{48,40},{56,48},{64,56},{72,6... | collective-permute-start | bytes 49160 | tf_op jit(solution)/shard_map/ppermute | solution.py:22
  151.3 9.0 %collective-permute-start.5 = (f32[1,8,512]{2,1,0:T(8,128)S(1)}, f32[1,8,512]{2,1,0:T(8,128)S(1)}, u32[]{:S(2)}, u32[]{:S(2)}) collective-permute-start(f32[1,8,512]{2,1,0:T(8,128)S(1)} %get-tuple-element.62), channel_id=1, source_target_pairs={{0,8},{8,16},{16,24},{24,32},{32,40},{40,48},{48,56},{56,64},{64,7... | collective-permute-start | bytes 49160 | tf_op jit(solution)/shard_map/ppermute | solution.py:21
  153.3 11.4 %collective-permute-start.15 = (f32[6,1,256]{2,1,0:T(1,128)S(1)}, f32[6,1,256]{2,1,0:T(1,128)S(1)}, u32[]{:S(2)}, u32[]{:S(2)}) collective-permute-start(f32[6,1,256]{2,1,0:T(1,128)S(1)} %get-tuple-element.77), channel_id=1, source_target_pairs={{1,0},{2,1},{3,2},{4,3},{5,4},{6,5},{7,6},{9,8},{10,9},{11,10},{12... | collective-permute-start | bytes 18440 | tf_op jit(solution)/shard_map/ppermute | solution.py:22
  160.3 4.5 collective-permute-start.6
  162.5 5.1 %collective-permute-start.7 = (f32[10,1,512]{2,1,0:T(1,128)S(1)}, f32[10,1,512]{2,1,0:T(1,128)S(1)}, u32[]{:S(2)}, u32[]{:S(2)}) collective-permute-start(f32[10,1,512]{2,1,0:T(1,128)S(1)} %get-tuple-element.52), channel_id=1, source_target_pairs={{0,1},{1,2},{2,3},{3,4},{4,5},{5,6},{6,7},{8,9},{9,10},{10,11},{11... | collective-permute-start | bytes 61448 | tf_op jit(solution)/shard_map/ppermute | solution.py:21
  168.2 6.0 %collective-permute-start.8 = (f32[1,8,512]{2,1,0:T(8,128)S(1)}, f32[1,8,512]{2,1,0:T(8,128)S(1)}, u32[]{:S(2)}, u32[]{:S(2)}) collective-permute-start(f32[1,8,512]{2,1,0:T(8,128)S(1)} %get-tuple-element.61), channel_id=1, source_target_pairs={{8,0},{16,8},{24,16},{32,24},{40,32},{48,40},{56,48},{64,56},{72,6... | collective-permute-start | bytes 49160 | tf_op jit(solution)/shard_map/ppermute | solution.py:22
  171.3 9.0 %collective-permute-start.9 = (f32[1,8,512]{2,1,0:T(8,128)S(1)}, f32[1,8,512]{2,1,0:T(8,128)S(1)}, u32[]{:S(2)}, u32[]{:S(2)}) collective-permute-start(f32[1,8,512]{2,1,0:T(8,128)S(1)} %get-tuple-element.60), channel_id=1, source_target_pairs={{0,8},{8,16},{16,24},{24,32},{32,40},{40,48},{48,56},{56,64},{64,7... | collective-permute-start | bytes 49160 | tf_op jit(solution)/shard_map/ppermute | solution.py:21
  180.2 4.4 collective-permute-start.10
  182.2 5.1 %collective-permute-start.11 = (f32[10,1,512]{2,1,0:T(1,128)S(1)}, f32[10,1,512]{2,1,0:T(1,128)S(1)}, u32[]{:S(2)}, u32[]{:S(2)}) collective-permute-start(f32[10,1,512]{2,1,0:T(1,128)S(1)} %get-tuple-element.50), channel_id=1, source_target_pairs={{0,1},{1,2},{2,3},{3,4},{4,5},{5,6},{6,7},{8,9},{9,10},{10,11},{11... | collective-permute-start | bytes 61448 | tf_op jit(solution)/shard_map/ppermute | solution.py:21
  201.7 5.9 %collective-permute-start.16 = (f32[1,4,256]{2,1,0:T(4,128)S(1)}, f32[1,4,256]{2,1,0:T(4,128)S(1)}, u32[]{:S(2)}, u32[]{:S(2)}) collective-permute-start(f32[1,4,256]{2,1,0:T(4,128)S(1)} %get-tuple-element.95), channel_id=1, source_target_pairs={{8,0},{16,8},{24,16},{32,24},{40,32},{48,40},{56,48},{64,56},{72,6... | collective-permute-start | bytes 12296 | tf_op jit(solution)/shard_map/ppermute | solution.py:22
  203.6 8.8 %collective-permute-start.17 = (f32[1,4,256]{2,1,0:T(4,128)S(1)}, f32[1,4,256]{2,1,0:T(4,128)S(1)}, u32[]{:S(2)}, u32[]{:S(2)}) collective-permute-start(f32[1,4,256]{2,1,0:T(4,128)S(1)} %get-tuple-element.94), channel_id=1, source_target_pairs={{0,8},{8,16},{16,24},{24,32},{32,40},{40,48},{48,56},{56,64},{64,7... | collective-permute-start | bytes 12296 | tf_op jit(solution)/shard_map/ppermute | solution.py:21
  212.5 4.4 collective-permute-start.18
  214.4 4.9 %collective-permute-start.19 = (f32[6,1,256]{2,1,0:T(1,128)S(1)}, f32[6,1,256]{2,1,0:T(1,128)S(1)}, u32[]{:S(2)}, u32[]{:S(2)}) collective-permute-start(f32[6,1,256]{2,1,0:T(1,128)S(1)} %get-tuple-element.74), channel_id=1, source_target_pairs={{0,1},{1,2},{2,3},{3,4},{4,5},{5,6},{6,7},{8,9},{9,10},{10,11},{11... | collective-permute-start | bytes 18440 | tf_op jit(solution)/shard_map/ppermute | solution.py:21
  219.6 6.0 %collective-permute-start.20 = (f32[1,4,256]{2,1,0:T(4,128)S(1)}, f32[1,4,256]{2,1,0:T(4,128)S(1)}, u32[]{:S(2)}, u32[]{:S(2)}) collective-permute-start(f32[1,4,256]{2,1,0:T(4,128)S(1)} %get-tuple-element.93), channel_id=1, source_target_pairs={{8,0},{16,8},{24,16},{32,24},{40,32},{48,40},{56,48},{64,56},{72,6... | collective-permute-start | bytes 12296 | tf_op jit(solution)/shard_map/ppermute | solution.py:22
  221.5 8.8 %collective-permute-start.21 = (f32[1,4,256]{2,1,0:T(4,128)S(1)}, f32[1,4,256]{2,1,0:T(4,128)S(1)}, u32[]{:S(2)}, u32[]{:S(2)}) collective-permute-start(f32[1,4,256]{2,1,0:T(4,128)S(1)} %get-tuple-element.92), channel_id=1, source_target_pairs={{0,8},{8,16},{16,24},{24,32},{32,40},{40,48},{48,56},{56,64},{64,7... | collective-permute-start | bytes 12296 | tf_op jit(solution)/shard_map/ppermute | solution.py:21
  230.4 4.4 collective-permute-start.22
  232.3 4.9 %collective-permute-start.23 = (f32[6,1,256]{2,1,0:T(1,128)S(1)}, f32[6,1,256]{2,1,0:T(1,128)S(1)}, u32[]{:S(2)}, u32[]{:S(2)}) collective-permute-start(f32[6,1,256]{2,1,0:T(1,128)S(1)} %get-tuple-element.72), channel_id=1, source_target_pairs={{0,1},{1,2},{2,3},{3,4},{4,5},{5,6},{6,7},{8,9},{9,10},{10,11},{11... | collective-permute-start | bytes 18440 | tf_op jit(solution)/shard_map/ppermute | solution.py:21
  249.8 6.1 %collective-permute-start.26 = (f32[1,16,128]{2,0,1:T(1,128)S(1)}, f32[1,16,128]{2,0,1:T(1,128)S(1)}, u32[]{:S(2)}, u32[]{:S(2)}) collective-permute-start(f32[1,16,128]{2,0,1:T(1,128)S(1)} %get-tuple-element.89), channel_id=1, source_target_pairs={{8,0},{16,8},{24,16},{32,24},{40,32},{48,40},{56,48},{64,56},{72,6... | collective-permute-start | bytes 24584 | tf_op jit(solution)/shard_map/ppermute | solution.py:22
  251.7 8.9 %collective-permute-start.27 = (f32[1,16,128]{2,0,1:T(1,128)S(1)}, f32[1,16,128]{2,0,1:T(1,128)S(1)}, u32[]{:S(2)}, u32[]{:S(2)}) collective-permute-start(f32[1,16,128]{2,0,1:T(1,128)S(1)} %get-tuple-element.88), channel_id=1, source_target_pairs={{0,8},{8,16},{16,24},{24,32},{32,40},{40,48},{48,56},{56,64},{64,7... | collective-permute-start | bytes 24584 | tf_op jit(solution)/shard_map/ppermute | solution.py:21
  260.8 6.0 %collective-permute-start.28 = (f32[1,16,128]{2,0,1:T(1,128)S(1)}, f32[1,16,128]{2,0,1:T(1,128)S(1)}, u32[]{:S(2)}, u32[]{:S(2)}) collective-permute-start(f32[1,16,128]{2,0,1:T(1,128)S(1)} %get-tuple-element.87), channel_id=1, source_target_pairs={{8,0},{16,8},{24,16},{32,24},{40,32},{48,40},{56,48},{64,56},{72,6... | collective-permute-start | bytes 24584 | tf_op jit(solution)/shard_map/ppermute | solution.py:22
  262.7 8.9 %collective-permute-start.29 = (f32[1,16,128]{2,0,1:T(1,128)S(1)}, f32[1,16,128]{2,0,1:T(1,128)S(1)}, u32[]{:S(2)}, u32[]{:S(2)}) collective-permute-start(f32[1,16,128]{2,0,1:T(1,128)S(1)} %get-tuple-element.86), channel_id=1, source_target_pairs={{0,8},{8,16},{16,24},{24,32},{32,40},{40,48},{48,56},{56,64},{64,7... | collective-permute-start | bytes 24584 | tf_op jit(solution)/shard_map/ppermute | solution.py:21
  387.7 6.6 %collective-permute-start.30 = (f32[1,16,128]{2,0,1:T(1,128)S(1)}, f32[1,16,128]{2,0,1:T(1,128)S(1)}, u32[]{:S(2)}, u32[]{:S(2)}) collective-permute-start(f32[1,16,128]{2,0,1:T(1,128)S(1)} %get-tuple-element.85), channel_id=1, source_target_pairs={{8,0},{16,8},{24,16},{32,24},{40,32},{48,40},{56,48},{64,56},{72,6... | collective-permute-start | bytes 24584 | tf_op jit(solution)/shard_map/ppermute | solution.py:22
  392.4 8.9 %collective-permute-start.31 = (f32[1,16,128]{2,0,1:T(1,128)S(1)}, f32[1,16,128]{2,0,1:T(1,128)S(1)}, u32[]{:S(2)}, u32[]{:S(2)}) collective-permute-start(f32[1,16,128]{2,0,1:T(1,128)S(1)} %get-tuple-element.84), channel_id=1, source_target_pairs={{0,8},{8,16},{16,24},{24,32},{32,40},{40,48},{48,56},{56,64},{64,7... | collective-permute-start | bytes 24584 | tf_op jit(solution)/shard_map/ppermute | solution.py:21
  402.3 5.9 %collective-permute-start.32 = (f32[1,16,128]{2,0,1:T(1,128)S(1)}, f32[1,16,128]{2,0,1:T(1,128)S(1)}, u32[]{:S(2)}, u32[]{:S(2)}) collective-permute-start(f32[1,16,128]{2,0,1:T(1,128)S(1)} %get-tuple-element.83), channel_id=1, source_target_pairs={{8,0},{16,8},{24,16},{32,24},{40,32},{48,40},{56,48},{64,56},{72,6... | collective-permute-start | bytes 24584 | tf_op jit(solution)/shard_map/ppermute | solution.py:22
  404.2 8.9 %collective-permute-start.33 = (f32[1,16,128]{2,0,1:T(1,128)S(1)}, f32[1,16,128]{2,0,1:T(1,128)S(1)}, u32[]{:S(2)}, u32[]{:S(2)}) collective-permute-start(f32[1,16,128]{2,0,1:T(1,128)S(1)} %get-tuple-element.82), channel_id=1, source_target_pairs={{0,8},{8,16},{16,24},{24,32},{32,40},{40,48},{48,56},{56,64},{64,7... | collective-permute-start | bytes 24584 | tf_op jit(solution)/shard_map/ppermute | solution.py:21
  416.1 5.8 %collective-permute-start.34 = (f32[1,4,256]{2,1,0:T(4,128)S(1)}, f32[1,4,256]{2,1,0:T(4,128)S(1)}, u32[]{:S(2)}, u32[]{:S(2)}) collective-permute-start(f32[1,4,256]{2,1,0:T(4,128)S(1)} %get-tuple-element.81), channel_id=1, source_target_pairs={{8,0},{16,8},{24,16},{32,24},{40,32},{48,40},{56,48},{64,56},{72,6... | collective-permute-start | bytes 12296 | tf_op jit(solution)/shard_map/ppermute | solution.py:22
  418.0 8.8 %collective-permute-start.35 = (f32[1,4,256]{2,1,0:T(4,128)S(1)}, f32[1,4,256]{2,1,0:T(4,128)S(1)}, u32[]{:S(2)}, u32[]{:S(2)}) collective-permute-start(f32[1,4,256]{2,1,0:T(4,128)S(1)} %get-tuple-element.80), channel_id=1, source_target_pairs={{0,8},{8,16},{16,24},{24,32},{32,40},{40,48},{48,56},{56,64},{64,7... | collective-permute-start | bytes 12296 | tf_op jit(solution)/shard_map/ppermute | solution.py:21
  426.8 4.3 collective-permute-start.36
  428.7 4.9 %collective-permute-start.37 = (f32[6,1,256]{2,1,0:T(1,128)S(1)}, f32[6,1,256]{2,1,0:T(1,128)S(1)}, u32[]{:S(2)}, u32[]{:S(2)}) collective-permute-start(f32[6,1,256]{2,1,0:T(1,128)S(1)} %get-tuple-element.70), channel_id=1, source_target_pairs={{0,1},{1,2},{2,3},{3,4},{4,5},{5,6},{6,7},{8,9},{9,10},{10,11},{11... | collective-permute-start | bytes 18440 | tf_op jit(solution)/shard_map/ppermute | solution.py:21
  434.8 5.9 %collective-permute-start.38 = (f32[1,4,256]{2,1,0:T(4,128)S(1)}, f32[1,4,256]{2,1,0:T(4,128)S(1)}, u32[]{:S(2)}, u32[]{:S(2)}) collective-permute-start(f32[1,4,256]{2,1,0:T(4,128)S(1)} %get-tuple-element.79), channel_id=1, source_target_pairs={{8,0},{16,8},{24,16},{32,24},{40,32},{48,40},{56,48},{64,56},{72,6... | collective-permute-start | bytes 12296 | tf_op jit(solution)/shard_map/ppermute | solution.py:22
  436.7 8.8 %collective-permute-start.39 = (f32[1,4,256]{2,1,0:T(4,128)S(1)}, f32[1,4,256]{2,1,0:T(4,128)S(1)}, u32[]{:S(2)}, u32[]{:S(2)}) collective-permute-start(f32[1,4,256]{2,1,0:T(4,128)S(1)} %get-tuple-element.78), channel_id=1, source_target_pairs={{0,8},{8,16},{16,24},{24,32},{32,40},{40,48},{48,56},{56,64},{64,7... | collective-permute-start | bytes 12296 | tf_op jit(solution)/shard_map/ppermute | solution.py:21
  445.5 4.3 collective-permute-start.40
  447.5 4.9 %collective-permute-start.41 = (f32[6,1,256]{2,1,0:T(1,128)S(1)}, f32[6,1,256]{2,1,0:T(1,128)S(1)}, u32[]{:S(2)}, u32[]{:S(2)}) collective-permute-start(f32[6,1,256]{2,1,0:T(1,128)S(1)} %get-tuple-element.68), channel_id=1, source_target_pairs={{0,1},{1,2},{2,3},{3,4},{4,5},{5,6},{6,7},{8,9},{9,10},{10,11},{11... | collective-permute-start | bytes 18440 | tf_op jit(solution)/shard_map/ppermute | solution.py:21
  457.0 5.9 %collective-permute-start.42 = (f32[1,8,512]{2,1,0:T(8,128)S(1)}, f32[1,8,512]{2,1,0:T(8,128)S(1)}, u32[]{:S(2)}, u32[]{:S(2)}) collective-permute-start(f32[1,8,512]{2,1,0:T(8,128)S(1)} %get-tuple-element.59), channel_id=1, source_target_pairs={{8,0},{16,8},{24,16},{32,24},{40,32},{48,40},{56,48},{64,56},{72,6... | collective-permute-start | bytes 49160 | tf_op jit(solution)/shard_map/ppermute | solution.py:22
  458.9 9.0 %collective-permute-start.43 = (f32[1,8,512]{2,1,0:T(8,128)S(1)}, f32[1,8,512]{2,1,0:T(8,128)S(1)}, u32[]{:S(2)}, u32[]{:S(2)}) collective-permute-start(f32[1,8,512]{2,1,0:T(8,128)S(1)} %get-tuple-element.58), channel_id=1, source_target_pairs={{0,8},{8,16},{16,24},{24,32},{32,40},{40,48},{48,56},{56,64},{64,7... | collective-permute-start | bytes 49160 | tf_op jit(solution)/shard_map/ppermute | solution.py:21
  467.9 4.3 collective-permute-start.44
  469.8 5.1 %collective-permute-start.45 = (f32[10,1,512]{2,1,0:T(1,128)S(1)}, f32[10,1,512]{2,1,0:T(1,128)S(1)}, u32[]{:S(2)}, u32[]{:S(2)}) collective-permute-start(f32[10,1,512]{2,1,0:T(1,128)S(1)} %get-tuple-element.48), channel_id=1, source_target_pairs={{0,1},{1,2},{2,3},{3,4},{4,5},{5,6},{6,7},{8,9},{9,10},{10,11},{11... | collective-permute-start | bytes 61448 | tf_op jit(solution)/shard_map/ppermute | solution.py:21
  475.4 5.9 %collective-permute-start.46 = (f32[1,8,512]{2,1,0:T(8,128)S(1)}, f32[1,8,512]{2,1,0:T(8,128)S(1)}, u32[]{:S(2)}, u32[]{:S(2)}) collective-permute-start(f32[1,8,512]{2,1,0:T(8,128)S(1)} %get-tuple-element.57), channel_id=1, source_target_pairs={{8,0},{16,8},{24,16},{32,24},{40,32},{48,40},{56,48},{64,56},{72,6... | collective-permute-start | bytes 49160 | tf_op jit(solution)/shard_map/ppermute | solution.py:22
  477.4 9.0 %collective-permute-start.47 = (f32[1,8,512]{2,1,0:T(8,128)S(1)}, f32[1,8,512]{2,1,0:T(8,128)S(1)}, u32[]{:S(2)}, u32[]{:S(2)}) collective-permute-start(f32[1,8,512]{2,1,0:T(8,128)S(1)} %get-tuple-element.56), channel_id=1, source_target_pairs={{0,8},{8,16},{16,24},{24,32},{32,40},{40,48},{48,56},{56,64},{64,7... | collective-permute-start | bytes 49160 | tf_op jit(solution)/shard_map/ppermute | solution.py:21
  488.3 5.1 %collective-permute-start.49 = (f32[10,1,512]{2,1,0:T(1,128)S(1)}, f32[10,1,512]{2,1,0:T(1,128)S(1)}, u32[]{:S(2)}, u32[]{:S(2)}) collective-permute-start(f32[10,1,512]{2,1,0:T(1,128)S(1)} %get-tuple-element.46), channel_id=1, source_target_pairs={{0,1},{1,2},{2,3},{3,4},{4,5},{5,6},{6,7},{8,9},{9,10},{10,11},{11... | collective-permute-start | bytes 61448 | tf_op jit(solution)/shard_map/ppermute | solution.py:21
  (12 other events, 1055.2 us)
where the time goes:
time: 497 us; the launch traced here: 495 us
  blocking collectives  185 us (37%)
  starting transfers between devices  141 us (28%)
  waiting for transfers between devices  82.7 us (17%)
  other arithmetic  35.6 us (7%)
  local copies, waits for them, and re-layouts  29 us (6%)
  between operations  21 us (4%)
    all_gather x1, blocking collectives, shards(): lax.all_gather(cells_three, 'wide', axis=0, tiled=True)  83.8 us
    ppermute x25, waiting for transfers between devices, padded_2(): before = lax.ppermute(last, axis, up)  81.2 us
    all_gather x1, blocking collectives, shards(): lax.all_gather(source_three, 'wide', axis=0, tiled=True)  78.6 us
    ppermute x25, starting transfers between devices, padded_2(): before = lax.ppermute(last, axis, up)  73.1 us
    ppermute x25, starting transfers between devices, padded_2(): after = lax.ppermute(initial, axis, down)  68.1 us
    reshape x3, local copies, waits for them, and re-layouts, restrict(): values.reshape(first // 2, 2, second // 2, 2, third // 2, 2)  21.3 us
    all_gather x1, blocking collectives, shards(): lax.all_gather(cells_two, 'narrow', axis=1, tiled=True)  11.6 us
    all_gather x1, blocking collectives, shards(): lax.all_gather(source_two, 'narrow', axis=1, tiled=True)  11 us
  transfers between devices with their start and end apart: 50, of which 21 were waited for; matrix products, arithmetic and copies ran while one was open for 7% of the time, Pallas kernels for 0%

commit v1 on v0

v1 whole, which is shorter than its diff:
```python
import functools

import jax
import jax.numpy as jnp
from jax import lax
from jax.experimental import pallas as pl
from jax.experimental.pallas import tpu as pltpu
from jax.sharding import Mesh, PartitionSpec as P

F32 = jnp.float32
BF16 = jnp.bfloat16

THETA = 0.5 * (2.0 + 0.25)
DELTA = 0.5 * (2.0 - 0.25)
SIGMA = THETA / DELTA
RHO_0 = 1.0 / SIGMA
RHO_1 = 1.0 / (2.0 * SIGMA - RHO_0)
KEEP = RHO_1 * RHO_0
GAIN = 2.0 * RHO_1 / DELTA
COARSE_SWEEPS = 8


def dot_exact(values, chooser):
    high = values.astype(BF16)
    rest = values - high.astype(F32)
    middle = rest.astype(BF16)
    low = (rest - middle.astype(F32)).astype(BF16)
    out = jnp.dot(high, chooser, preferred_element_type=F32)
    out = out + jnp.dot(middle, chooser, preferred_element_type=F32)
    return out + jnp.dot(low, chooser, preferred_element_type=F32)


def chosen_dot(chooser, values):
    high = values.astype(BF16)
    rest = values - high.astype(F32)
    middle = rest.astype(BF16)
    low = (rest - middle.astype(F32)).astype(BF16)
    out = jnp.dot(chooser, high, preferred_element_type=F32)
    out = out + jnp.dot(chooser, middle, preferred_element_type=F32)
    return out + jnp.dot(chooser, low, preferred_element_type=F32)


def iota(shape, dim):
    return lax.broadcasted_iota(jnp.int32, shape, dim)


def ones_where(mask, value=1.0):
    return jnp.where(mask, value, 0.0).astype(BF16)


def shift(values, step, axis):
    size = values.shape[axis]
    return pltpu.roll(values, (-step) % size, axis)


def plane_faces(c, c_next, fx_before, scale, axis, last, first, last_b=None, first_b=None):
    count, other = len(c), 1 - axis
    fx = [scale * (c[q] + c_next[q]) for q in range(count)]
    after = [c[q + 1] if q + 1 < count else jnp.where(last, 0.0, shift(c[0], 1, axis)) for q in range(count)]
    fa = [scale * (c[q] + after[q]) for q in range(count)]
    lowest = jnp.where(first, scale * c[0], shift(fa[-1], -1, axis))
    fb, diagonal = [], []
    for q in range(count):
        beside = shift(c[q], 1, other)
        if last_b is not None:
            beside = jnp.where(last_b, 0.0, beside)
        face = scale * (c[q] + beside)
        face_before = shift(face, -1, other)
        if first_b is not None:
            face_before = jnp.where(first_b, scale * c[q], face_before)
        diagonal.append(fx[q] + fx_before[q] + face + face_before + fa[q] + (fa[q - 1] if q else lowest))
        fb.append(face if last_b is None else jnp.where(last_b, 0.0, face))
    fa[-1] = jnp.where(last, 0.0, fa[-1])
    return fx, fa, fb, diagonal


def neighbours(u, fx, fa, fb, p, count, axis):
    other = 1 - axis
    here = [u[p, q] for q in range(count)]
    faces = [fa[p, q] for q in range(count)]
    out = []
    for q in range(count):
        face = fb[p, q]
        total = fx[p, q] * u[p + 1, q] + fx[p - 1, q] * u[p - 1, q]
        total = total + face * shift(here[q], 1, other) + shift(face * here[q], -1, other)
        if q + 1 < count:
            total = total + faces[q] * here[q + 1]
        else:
            total = total + faces[q] * shift(here[0], 1, axis)
        if q > 0:
            total = total + faces[q - 1] * here[q - 1]
        else:
            total = total + shift(faces[-1] * here[-1], -1, axis)
        out.append(total)
    return out


def loop(low, high, body):
    def step(i, carry):
        body(i)
        return carry

    lax.fori_loop(low, high, step, 0)


def inverse(c, diagonal):
    return jnp.where(c > 0.0, 1.0 / diagonal, 0.0)


C_LOW, B_LOW = 7, 6
C_PLANES, B_PLANES = 8 + 2 * C_LOW, 8 + 2 * B_LOW
SENT = C_LOW + B_LOW
WIDE_PLANES = C_PLANES + B_PLANES


def split_kernel(rhs, beta, own, up, down):
    z = iota((512, 512), 0)
    k = iota((512, 512), 1)
    chooser = ones_where(z == 4 * (k % 128) + k // 128)
    for field, source in enumerate((beta, rhs)):
        out = dot_exact(source[...].reshape(64, 512), chooser)
        for x in range(8):
            for q in range(4):
                tile = out[8 * x : 8 * x + 8, 128 * q : 128 * q + 128]
                own[8 * field + x, q] = tile
                width = (C_LOW, B_LOW)[field]
                start = (0, C_LOW)[field]
                if x >= 8 - width:
                    up[start + x - (8 - width), q] = tile
                if x < width:
                    down[start + x, q] = tile


def widen_kernel(own, below, above, out, *, wide):
    index = lax.axis_index("z") * lax.axis_size("y") + lax.axis_index("y")
    keep_low = jnp.where(index > 0, 1.0, 0.0).astype(F32)
    keep_high = jnp.where(index < wide - 1, 1.0, 0.0).astype(F32)
    for j in range(C_LOW):
        out[j] = below[j] * keep_low
        out[C_LOW + 8 + j] = above[j] * keep_high
    for j in range(8):
        out[C_LOW + j] = own[j]
        out[C_PLANES + B_LOW + j] = own[8 + j]
    for j in range(B_LOW):
        out[C_PLANES + j] = below[C_LOW + j]
        out[C_PLANES + B_LOW + 8 + j] = above[C_LOW + j]


def down_kernel(mid, left, right, packed, x0, b0, fx, fy, fz, dinv, c1, b1, fx1, fy1, fz1, dinv1, diag, first, sums, diag1, first1, x1, *, group):
    n = lax.axis_index("n")
    keep_left = jnp.where(n > 0, 1.0, 0.0).astype(F32)
    keep_right = jnp.where(n < lax.axis_size("n") - 1, 1.0, 0.0).astype(F32)
    lane = iota((24, 128), 1)
    last, begin = lane == 127, lane == 0

    def cells(p):
        j = p - 1
        return [jnp.concatenate([left[j, q] * keep_left, mid[j, q], right[j, q] * keep_right], axis=0) for q in range(4)]

    def source(p):
        j = p - 2 + C_PLANES
        return [jnp.concatenate([left[j, q], mid[j, q], right[j, q]], axis=0) for q in range(4)]

    before, after = cells(1), cells(2)
    for q in range(4):
        fx[1, q] = 0.5 * (before[q] + after[q])

    def faces_0(p):
        c, c_next, b = cells(p), cells(p + 1), source(p)
        gx, gz, gy, d = plane_faces(c, c_next, [fx[p - 1, q] for q in range(4)], 0.5, 1, last, begin)
        for q in range(4):
            fx[p, q], fy[p, q], fz[p, q], diag[p, q] = gx[q], gy[q], gz[q], d[q]
            inv = inverse(c[q], d[q])
            dinv[p, q] = inv
            b0[p, q] = b[q]
            first[p, q] = b[q] * inv * (1.0 / THETA)

    loop(2, 22, faces_0)

    def second_0(p):
        near = neighbours(first, fx, fz, fy, p, 4, 1)
        for q in range(4):
            x0[p, q] = (1.0 + KEEP - GAIN) * first[p, q] + GAIN * (b0[p, q] + near[q]) * dinv[p, q]

    loop(3, 21, second_0)

    def residual_0(k):
        total = [jnp.zeros((24, 128), F32)] * 2
        for p in (4 + 2 * k, 5 + 2 * k):
            near = neighbours(x0, fx, fz, fy, p, 4, 1)
            for q in range(4):
                total[q // 2] = total[q // 2] + (b0[p, q] + near[q] - diag[p, q] * x0[p, q])
        for q in range(2):
            sums[k, q, 0:24] = total[q]
            sums[k, q, 24:32] = jnp.zeros((8, 128), F32)

    loop(0, 8, residual_0)

    def cells_1(k):
        one, two = cells(2 + 2 * k), cells(3 + 2 * k)
        for q in range(2):
            sums[8 + k, q, 0:24] = (one[2 * q] + one[2 * q + 1]) + (two[2 * q] + two[2 * q + 1])
            sums[8 + k, q, 24:32] = jnp.zeros((8, 128), F32)

    loop(0, 10, cells_1)

    def halve(k, q):
        return 0.125 * (sums[k, q, pl.ds(0, 16, stride=2), :] + sums[k, q, pl.ds(1, 16, stride=2), :])

    for q in range(2):
        loop(0, 8, lambda k, q=q: b1.__setitem__((k + 1, q), halve(k, q)))
        loop(0, 10, lambda k, q=q: c1.__setitem__((k, q), halve(8 + k, q)))

    lane = iota((16, 128), 1)
    last_1, begin_1 = lane == 127, lane == 0
    for q in range(2):
        fx1[0, q] = 0.125 * (c1[0, q] + c1[1, q])

    def faces_1(p):
        c, c_next = [c1[p, q] for q in range(2)], [c1[p + 1, q] for q in range(2)]
        gx, gz, gy, d = plane_faces(c, c_next, [fx1[p - 1, q] for q in range(2)], 0.125, 1, last_1, begin_1)
        for q in range(2):
            fx1[p, q], fy1[p, q], fz1[p, q], diag1[p, q] = gx[q], gy[q], gz[q], d[q]
            inv = inverse(c[q], d[q])
            dinv1[p, q] = inv
            first1[p, q] = b1[p, q] * inv * (1.0 / THETA)

    loop(1, 9, faces_1)

    def second_1(p):
        near = neighbours(first1, fx1, fz1, fy1, p, 2, 1)
        for q in range(2):
            x1[p, q] = (1.0 + KEEP - GAIN) * first1[p, q] + GAIN * (b1[p, q] + near[q]) * dinv1[p, q]

    loop(2, 8, second_1)

    for x in range(4):
        for q in range(2):
            packed[0, x, 4 * q : 4 * q + 4] = x1[3 + x, q, 4:8]
    for x in range(2):
        total = jnp.zeros((16, 128), F32)
        cell = jnp.zeros((16, 128), F32)
        for p in (3 + 2 * x, 4 + 2 * x):
            near = neighbours(x1, fx1, fz1, fy1, p, 2, 1)
            for q in range(2):
                total = total + (b1[p, q] + near[q] - diag1[p, q] * x1[p, q])
                cell = cell + c1[p, q]
        total = 0.125 * (total + shift(total, 1, 0))
        cell = 0.125 * (cell + shift(cell, 1, 0))
        for yy in range(2):
            packed[0, 4, 2 * x + yy : 2 * x + yy + 1] = total[4 + 2 * yy : 5 + 2 * yy]
            packed[0, 4, 4 + 2 * x + yy : 5 + 2 * x + yy] = cell[4 + 2 * yy : 5 + 2 * yy]

    def copy(s):
        packed[s] = packed[0]

    loop(1, group, copy)


def edge_kernel(plane, up, down, *, depth):
    n = lax.axis_index("n")
    size = lax.axis_size("n")

    def slab(s):
        tile = plane[s, 4]
        up[s] = tile
        down[s] = tile

    loop(0, depth * size, slab)
    for k in range(3):
        place = jnp.clip(n + (k - 1), 0, size - 1)
        for x in range(4):
            up[depth * size + 4 * k + x] = plane[(depth - 1) * size + place, x]
            down[depth * size + 4 * k + x] = plane[place, x]


def middle_kernel(plane, below, above, sent, x2, b2, fx, fy, fz, dinv, x1, c2, diag, first, *, depth, tall):
    z, y, n = lax.axis_index("z"), lax.axis_index("y"), lax.axis_index("n")
    size = lax.axis_size("n")
    keep_low = jnp.where(z > 0, 1.0, 0.0).astype(F32)
    keep_high = jnp.where(z < tall - 1, 1.0, 0.0).astype(F32)
    width = 2 * depth
    for yb in range(depth):
        for x in range(2):
            for yy in range(2):
                r = 2 * x + yy
                place = 2 * yb + x
                own = yb * size * 40 + 32 + r
                edge = yb * size * 8 + r
                b2[place, yy] = below[pl.ds(edge, 8, stride=8), :]
                b2[width + place, yy] = plane[pl.ds(own, 8, stride=40), :]
                b2[2 * width + place, yy] = above[pl.ds(edge, 8, stride=8), :]
                c2[place, yy] = below[pl.ds(edge + 4, 8, stride=8), :] * keep_low
                c2[width + place, yy] = plane[pl.ds(own + 4, 8, stride=40), :]
                c2[2 * width + place, yy] = above[pl.ds(edge + 4, 8, stride=8), :] * keep_high

    scale = 0.5 / 16.0
    shape = (8, 128)
    row, lane = iota(shape, 0), iota(shape, 1)
    last, begin, last_b, begin_b = row == 7, row == 0, lane == 127, lane == 0
    for q in range(2):
        fx[0, q] = scale * (c2[0, q] + c2[1, q])

    def faces_2(p):
        c, c_next = [c2[p, q] for q in range(2)], [c2[p + 1, q] for q in range(2)]
        gx, gy, gz, d = plane_faces(c, c_next, [fx[p - 1, q] for q in range(2)], scale, 0, last, begin, last_b, begin_b)
        for q in range(2):
            fx[p, q], fy[p, q], fz[p, q], diag[p, q] = gx[q], gy[q], gz[q], d[q]
            inv = inverse(c[q], d[q])
            dinv[p, q] = inv
            first[p, q] = b2[p, q] * inv * (1.0 / THETA)

    loop(1, 3 * width - 1, faces_2)

    def second_2(p):
        near = neighbours(first, fx, fy, fz, p, 2, 0)
        for q in range(2):
            x2[p, q] = (1.0 + KEEP - GAIN) * first[p, q] + GAIN * (b2[p, q] + near[q]) * dinv[p, q]

    loop(2, 3 * width - 2, second_2)

    totals, cell_sums = [], []
    for j in range(depth):
        total = jnp.zeros(shape, F32)
        cell = jnp.zeros(shape, F32)
        for p in (width + 2 * j, width + 2 * j + 1):
            near = neighbours(x2, fx, fy, fz, p, 2, 0)
            for q in range(2):
                total = total + (b2[p, q] + near[q] - diag[p, q] * x2[p, q])
                cell = cell + c2[p, q]
        totals.append(total)
        cell_sums.append(cell)
    zz, k = iota((128, 128), 0), iota((128, 128), 1)
    low_half = ones_where(k == zz // 2, 0.125)
    high_half = ones_where(k == zz // 2 + 64, 0.125)
    coarse = dot_exact(jnp.concatenate(totals, axis=0), low_half) + dot_exact(jnp.concatenate(cell_sums, axis=0), high_half)
    coarse = coarse.reshape(depth, 8, 128)
    for s in range(tall):
        sent[s] = coarse

    for x in range(4):
        for k in range(3):
            place = jnp.clip(n + (k - 1), 0, size - 1)

            def block(yb):
                start = pl.multiple_of((yb * size + place) * 40 + 8 * x, 8)
                return plane[pl.ds(start, 8), :]

            edge = 8 * (depth * size + 4 * k + x)
            tiles = {
                -1: jnp.where(y == 0, below[edge : edge + 8], block(jnp.maximum(y - 1, 0))),
                0: block(y),
                1: jnp.where(y == depth - 1, above[edge : edge + 8], block(jnp.minimum(y + 1, depth - 1))),
            }
            for dx, tile in tiles.items():
                p = 3 + 4 * dx + x
                if 0 <= p < 10:
                    for q in range(2):
                        x1[p, q, 4 * k : 4 * k + 4] = tile[4 * q : 4 * q + 4]
    for p in range(10):
        for q in range(2):
            x1[p, q, 12:16] = jnp.zeros((4, 128), F32)


def sweeps(start, mid, out, source, fx, fa, fb, dinv, low, high, count, axis):
    def one(p):
        near = neighbours(start, fx, fa, fb, p, count, axis)
        for q in range(count):
            mid[p, q] = (1.0 - 1.0 / THETA) * start[p, q] + (1.0 / THETA) * ((source[p, q] + near[q]) * dinv[p, q])

    loop(low - 1, high + 1, one)

    def two(p):
        near = neighbours(mid, fx, fa, fb, p, count, axis)
        for q in range(count):
            value = (1.0 - GAIN + KEEP) * mid[p, q] - KEEP * start[p, q]
            out(p, q, value + GAIN * ((source[p, q] + near[q]) * dinv[p, q]))

    loop(low, high, two)


def up_kernel(gathered, x1h, x2, b2, fx2, fy2, fz2, dinv2, c1, b1, fx1, fy1, fz1, dinv1, x0, b0, fx, fy, fz, dinv, result,
              c3, p3, r3, x3, i3, fx3, fy3, fz3, d3, s2, m2, f2, s1, m1, f1, s0, m0, f0, *, depth, tall):
    z, y, n = lax.axis_index("z"), lax.axis_index("y"), lax.axis_index("n")
    half = depth * tall // 2
    shape = (8, 128)
    row, lane = iota(shape, 0), iota(shape, 1)
    upper = lane >= 64

    def unpack(i):
        one, two = gathered[i], gathered[i + half]
        b = jnp.where(upper, pltpu.roll(two, 64, 1), one)
        c3[i + 1, 0] = jnp.where(upper, two, pltpu.roll(one, 64, 1))
        r3[i + 1, 0] = b
        p3[i + 1, 0] = b
        x3[i + 1, 0] = jnp.zeros(shape, F32)

    loop(0, half, unpack)

    def wrap(ref):
        ref[0, 0] = jnp.where(upper, pltpu.roll(ref[half, 0], 64, 1), 0.0)
        ref[half + 1, 0] = jnp.where(upper, 0.0, pltpu.roll(ref[1, 0], 64, 1))

    wrap(c3)
    scale = 0.5 / 64.0
    fx3[0, 0] = scale * (c3[0, 0] + c3[1, 0])

    def faces_3(p):
        gx, gy, gz, d = plane_faces([c3[p, 0]], [c3[p + 1, 0]], [fx3[p - 1, 0]], scale, 0, row == 7, row == 0, lane % 64 == 63, lane % 64 == 0)
        fx3[p, 0], fy3[p, 0], fz3[p, 0], d3[p, 0] = gx[0], gy[0], gz[0], d[0]

    loop(1, half + 1, faces_3)

    def whole(parts):
        total = functools.reduce(lambda a, b: a + b, parts)
        return jnp.sum(jnp.sum(total, axis=0, keepdims=True), axis=1, keepdims=True)

    def spread(values):
        parts = [jnp.zeros(shape, F32)] * 4
        for i, value in enumerate(values):
            parts[i % 4] = parts[i % 4] + value
        return whole(parts)

    start_norm = spread([r3[i + 1, 0] * r3[i + 1, 0] for i in range(half)])

    def iterate(_, norm):
        wrap(p3)
        products = []
        for p in range(1, half + 1):
            here = p3[p, 0]
            image = d3[p, 0] * here - neighbours(p3, fx3, fy3, fz3, p, 1, 0)[0]
            i3[p, 0] = image
            products.append(here * image)
        alpha = norm / spread(products)
        squares = []
        for p in range(1, half + 1):
            x3[p, 0] = x3[p, 0] + alpha * p3[p, 0]
            rest = r3[p, 0] - alpha * i3[p, 0]
            r3[p, 0] = rest
            squares.append(rest * rest)
        new = spread(squares)
        beta = new / norm
        for p in range(1, half + 1):
            p3[p, 0] = r3[p, 0] + beta * p3[p, 0]
        return new

    lax.fori_loop(0, COARSE_SWEEPS, iterate, start_norm)

    base = 2 * depth + 2 * y - 4
    tiles = []
    for j in range(5):
        place = jnp.clip(depth * z + y - 2 + j, 0, 2 * half - 1)
        high = place >= half
        tile = x3[jnp.where(high, place - half, place) + 1, 0]
        tiles.append(jnp.where(high, pltpu.roll(tile, 64, 1), tile))
    k, zz = iota((128, 128), 0), iota((128, 128), 1)
    fine = dot_exact(jnp.concatenate(tiles, axis=0), ones_where(k == zz // 2))
    for j in range(5):
        add = fine[8 * j : 8 * j + 8]
        for p in (base + 2 * j, base + 2 * j + 1):
            for q in range(2):
                s2[p, q] = jnp.where(dinv2[p, q] > 0.0, x2[p, q] + add, 0.0)

    def keep_2(p, q, value):
        f2[p, q] = value

    sweeps(s2, m2, keep_2, b2, fx2, fy2, fz2, dinv2, base + 2, base + 8, 2, 0)

    wide = jnp.concatenate([jnp.concatenate([f2[base + 2 + k, 0], f2[base + 2 + k, 1]], axis=0) for k in range(6)], axis=1)
    r, k = iota((16, 16), 0), iota((16, 16), 1)
    from_n = n + r // 4 - 1
    pick = ones_where((k == (r // 2) % 2 * 8 + from_n) & (from_n >= 0) & (from_n < 8))
    fine = chosen_dot(pick, wide)
    for p in range(10):
        k = (p + 1) // 2
        for q in range(2):
            s1[p, q] = jnp.where(c1[p, q] > 0.0, x1h[p, q] + fine[:, 128 * k : 128 * k + 128], 0.0)

    def keep_1(p, q, value):
        f1[p, q] = value

    sweeps(s1, m1, keep_1, b1, fx1, fz1, fy1, dinv1, 2, 8, 2, 1)

    wide = jnp.concatenate([f1[p, q] for p in range(2, 8) for q in range(2)], axis=1)
    r, k = iota((24, 16), 0), iota((24, 16), 1)
    fine = chosen_dot(ones_where(k == r // 2), wide)
    for p in range(6, 18):
        for q in range(4):
            j = 2 * (p // 2 - 3) + q // 2
            s0[p, q] = jnp.where(dinv[p, q] > 0.0, x0[p, q] + fine[:, 128 * j : 128 * j + 128], 0.0)

    def keep_0(p, q, value):
        start = (p - 8) * 8
        if not isinstance(start, int):
            start = pl.multiple_of(start, 8)
        f0[pl.ds(start, 8), 128 * q : 128 * q + 128] = value[8:16]

    sweeps(s0, m0, keep_0, b0, fx, fz, fy, dinv, 8, 16, 4, 1)
    k, z0 = iota((512, 512), 0), iota((512, 512), 1)
    back = ones_where(z0 == 4 * (k % 128) + k // 128)
    result[...] = dot_exact(f0[...], back).reshape(8, 8, 512)


def call(kernel, outs, *operands, scratch=(), limit=40):
    shapes = [jax.ShapeDtypeStruct(shape, F32) for shape in outs]
    return pl.pallas_call(
        kernel,
        out_shape=shapes,
        in_specs=[pl.BlockSpec(memory_space=pltpu.VMEM)] * len(operands),
        out_specs=[pl.BlockSpec(memory_space=pltpu.VMEM)] * len(outs),
        scratch_shapes=[pltpu.VMEM(shape, F32) for shape in scratch],
        compiler_params=pltpu.CompilerParams(vmem_limit_bytes=limit * 2**20),
    )(*operands)


def ring(axis_size, step):
    return [(i, (i + step) % axis_size) for i in range(axis_size)]


def shards(rhs_field, beta_cells):
    tall, depth, size = lax.axis_size("z"), lax.axis_size("y"), lax.axis_size("n")
    wide, group = tall * depth, depth * size
    own, up, down = call(
        split_kernel, [(16, 4, 8, 128), (SENT, 4, 8, 128), (SENT, 4, 8, 128)], rhs_field, beta_cells
    )
    below = lax.ppermute(up, ("z", "y"), ring(wide, 1))
    above = lax.ppermute(down, ("z", "y"), ring(wide, -1))
    (mid,) = call(functools.partial(widen_kernel, wide=wide), [(WIDE_PLANES, 4, 8, 128)], own, below, above)
    left = lax.ppermute(mid, "n", ring(size, 1))
    right = lax.ppermute(mid, "n", ring(size, -1))
    fine, coarse = (24, 4, 24, 128), (10, 2, 16, 128)
    outs = call(
        functools.partial(down_kernel, group=group),
        [(group, 5, 8, 128)] + [fine] * 6 + [coarse] * 6,
        mid, left, right,
        scratch=[fine, fine, (18, 2, 32, 128), coarse, coarse, coarse],
    )
    packed, level_zero, level_one = outs[0], outs[1:7], outs[7:13]
    plane = lax.all_to_all(packed, ("y", "n"), 0, 0)
    edge = group + 12
    up, down = call(functools.partial(edge_kernel, depth=depth), [(edge, 8, 128)] * 2, plane)
    below = lax.ppermute(up, "z", ring(tall, 1))
    above = lax.ppermute(down, "z", ring(tall, -1))
    slab = (6 * depth, 2, 8, 128)
    outs = call(
        functools.partial(middle_kernel, depth=depth, tall=tall),
        [(tall, depth, 8, 128)] + [slab] * 6 + [coarse],
        plane.reshape(group * 40, 128), below.reshape(edge * 8, 128), above.reshape(edge * 8, 128),
        scratch=[slab, slab, slab],
    )
    sent, level_two, x1h = outs[0], outs[1:7], outs[7]
    gathered = lax.all_to_all(sent, "z", 0, 0)
    packed_3 = (wide // 2 + 2, 1, 8, 128)
    (result,) = call(
        functools.partial(up_kernel, depth=depth, tall=tall),
        [(8, 8, 512)],
        gathered.reshape(wide, 8, 128), x1h, *level_two, *level_one, *level_zero,
        scratch=[packed_3] * 9 + [slab] * 3 + [coarse] * 3 + [fine] * 2 + [(64, 512)],
    )
    return result


def solution(mesh):
    wide, size = mesh.shape["wide"], mesh.shape["narrow"]
    inner = Mesh(mesh.devices.reshape(wide // 4, 4, size), ("z", "y", "n"))
    spec = P(("z", "y"), "n", None)
    return jax.shard_map(shards, mesh=inner, in_specs=(spec, spec), out_specs=spec, check_vma=False)
```

time: 497 us -> 120 us (0.24)
  the two profiles are of different devices: /device:TPU:130 before, /device:TPU:32 now
where the time goes in v1:
time: 120 us
  blocking collectives  49.4 us (41%)
  Pallas kernels  29.3 us (24%)
  waiting for transfers between devices  21.7 us (18%)
  starting transfers between devices  17.5 us (15%)
  local copies, waits for them, and re-layouts  1.81 us (2%)
    all_to_all x1, blocking collectives, shards(): gathered = lax.all_to_all(sent, 'z', 0, 0)  29.4 us
    pallas_call x6, Pallas kernels, call(): pl.pallas_call(kernel, out_shape=shapes, in_specs=[pl.BlockSpec(memory_sp...  29.3 us
    all_to_all x1, blocking collectives, shards(): plane = lax.all_to_all(packed, ('y', 'n'), 0, 0)  20 us
    ppermute x1, waiting for transfers between devices, shards(): right = lax.ppermute(mid, 'n', ring(size, -1))  8.45 us
    ppermute x1, starting transfers between devices, shards(): above = lax.ppermute(down, 'z', ring(tall, -1))  4.75 us
    ppermute x1, starting transfers between devices, shards(): above = lax.ppermute(down, ('z', 'y'), ring(wide, -1))  4.47 us
    ppermute x1, starting transfers between devices, shards(): below = lax.ppermute(up, 'z', ring(tall, 1))  3.82 us
    ppermute x1, starting transfers between devices, shards(): below = lax.ppermute(up, ('z', 'y'), ring(wide, 1))  3.48 us
  transfers between devices with their start and end apart: 6, of which 6 were waited for; matrix products, arithmetic and copies ran while one was open for 0% of the time, Pallas kernels for 0%

profile of v1, /device:TPU:32, one launch (start us, length us, event | category | flops | bytes accessed | tf_op | source)
XLA Modules:
  0.0 119.7 jit_solution(18442534648064748593)
XLA Ops:
  0.0 0.0 copy-start
  0.0 0.9 copy-done
  0.9 0.0 copy-start.1
  0.9 0.9 copy-done.1
  1.8 0.7 shard_map.28
  2.5 3.5 %collective-permute-start = (f32[13,4,8,128]{3,2,1,0:T(8,128)S(1)}, f32[13,4,8,128]{3,2,1,0:T(8,128)S(1)}, u32[]{:S(2)}, u32[]{:S(2)}) collective-permute-start(f32[13,4,8,128]{3,2,1,0:T(8,128)S(1)} %get-tuple-element.32), channel_id=1, source_target_pairs={{0,8},{8,16},{16,24},{24,32},{32,40},{40,48},{48,56},{56,64},{64,7... | collective-permute-start | bytes 638984 | tf_op jit(solution)/shard_map/ppermute | solution.py:526
  6.0 4.5 %collective-permute-start.1 = (f32[13,4,8,128]{3,2,1,0:T(8,128)S(1)}, f32[13,4,8,128]{3,2,1,0:T(8,128)S(1)}, u32[]{:S(2)}, u32[]{:S(2)}) collective-permute-start(f32[13,4,8,128]{3,2,1,0:T(8,128)S(1)} %get-tuple-element.33), channel_id=1, source_target_pairs={{0,504},{8,0},{16,8},{24,16},{32,24},{40,32},{48,40},{56,48},{64,5... | collective-permute-start | bytes 638984 | tf_op jit(solution)/shard_map/ppermute | solution.py:527
  10.5 3.0 %collective-permute-done.below = f32[13,4,8,128]{3,2,1,0:T(8,128)S(1)} collective-permute-done((f32[13,4,8,128]{3,2,1,0:T(8,128)S(1)}, f32[13,4,8,128]{3,2,1,0:T(8,128)S(1)}, u32[]{:S(2)}, u32[]{:S(2)}) %collective-permute-start) | collective-permute-done | bytes 213024 | tf_op jit(solution)/shard_map/ppermute | solution.py:526
  13.5 1.2 collective-permute-done.1.above
  14.7 0.1 shard_map.29.mid
  14.7 1.0 collective-permute-start.3
  15.8 0.0 collective-permute-start.2
  15.8 8.5 %collective-permute-done.3.right = f32[42,4,8,128]{3,2,1,0:T(8,128)S(1)} collective-permute-done((f32[42,4,8,128]{3,2,1,0:T(8,128)S(1)}, f32[42,4,8,128]{3,2,1,0:T(8,128)S(1)}, u32[]{:S(2)}, u32[]{:S(2)}) %collective-permute-start.3) | collective-permute-done | bytes 688160 | tf_op jit(solution)/shard_map/ppermute | solution.py:530
  24.2 3.1 %collective-permute-done.2.left = f32[42,4,8,128]{3,2,1,0:T(8,128)S(1)} collective-permute-done((f32[42,4,8,128]{3,2,1,0:T(8,128)S(1)}, f32[42,4,8,128]{3,2,1,0:T(8,128)S(1)}, u32[]{:S(2)}, u32[]{:S(2)}) %collective-permute-start.2) | collective-permute-done | bytes 688160 | tf_op jit(solution)/shard_map/ppermute | solution.py:529
  27.3 7.5 %shard_map.30 = (f32[32,5,8,128]{3,2,1,0:T(8,128)S(1)}, f32[24,4,24,128]{3,2,1,0:T(8,128)S(1)}, f32[24,4,24,128]{3,2,1,0:T(8,128)S(1)}, f32[24,4,24,128]{3,2,1,0...) custom-call(f32[42,4,8,128]{3,2,1,0:T(8,128)S(1)} %shard_map.29.mid,, ...), custom_call_target="tpu_custom_call" | custom-call | tf_op jit(solution)/shard_map/pallas_call | solution.py:506
  34.9 20.0 %all_to_all.10.plane = f32[32,5,8,128]{3,2,1,0:T(8,128)S(1)} all-to-all(f32[32,5,8,128]{3,2,1,0:T(8,128)S(1)} %get-tuple-element.34), channel_id=1, replica_groups=mesh['z'=16,'y'=4,'n'=8] {'y','n'}, dimensions={0} | all-to-all | bytes 1310720 | tf_op jit(solution)/shard_map/all_to_all | solution.py:539
  54.9 0.2 shard_map.31
  55.0 3.8 %collective-permute-start.4 = (f32[44,8,128]{2,1,0:T(8,128)S(1)}, f32[44,8,128]{2,1,0:T(8,128)S(1)}, u32[]{:S(2)}, u32[]{:S(2)}) collective-permute-start(f32[44,8,128]{2,1,0:T(8,128)S(1)} %get-tuple-element.35), channel_id=1, source_target_pairs={{0,32},{32,64},{64,96},{96,128},{128,160},{160,192},{192,224},{224... | collective-permute-start | bytes 540680 | tf_op jit(solution)/shard_map/ppermute | solution.py:542
  58.9 4.7 %collective-permute-start.5 = (f32[44,8,128]{2,1,0:T(8,128)S(1)}, f32[44,8,128]{2,1,0:T(8,128)S(1)}, u32[]{:S(2)}, u32[]{:S(2)}) collective-permute-start(f32[44,8,128]{2,1,0:T(8,128)S(1)} %get-tuple-element.36), channel_id=1, source_target_pairs={{0,480},{32,0},{64,32},{96,64},{128,96},{160,128},{192,160},{224,1... | collective-permute-start | bytes 540680 | tf_op jit(solution)/shard_map/ppermute | solution.py:543
  63.6 2.7 %collective-permute-done.4 = f32[44,8,128]{2,1,0:T(8,128)S(1)} collective-permute-done((f32[44,8,128]{2,1,0:T(8,128)S(1)}, f32[44,8,128]{2,1,0:T(8,128)S(1)}, u32[]{:S(2)}, u32[]{:S(2)}) %collective-permute-start.4) | collective-permute-done | bytes 180256 | tf_op jit(solution)/shard_map/ppermute | solution.py:542
  66.4 3.1 %collective-permute-done.5 = f32[44,8,128]{2,1,0:T(8,128)S(1)} collective-permute-done((f32[44,8,128]{2,1,0:T(8,128)S(1)}, f32[44,8,128]{2,1,0:T(8,128)S(1)}, u32[]{:S(2)}, u32[]{:S(2)}) %collective-permute-start.5) | collective-permute-done | bytes 180256 | tf_op jit(solution)/shard_map/ppermute | solution.py:543
  69.5 5.4 %shard_map.32 = (f32[16,4,8,128]{3,2,1,0:T(8,128)S(1)}, f32[24,2,8,128]{3,2,1,0:T(8,128)S(1)}, f32[24,2,8,128]{3,2,1,0:T(8,128)S(1)}, f32[24,2,8,128]{3,2,1,0:T(...) custom-call(f32[1280,128]{1,0:T(8,128)S(1)} %bitcast.4, ...), custom_call_target="tpu_custom_call" | custom-call | tf_op jit(solution)/shard_map/pallas_call | solution.py:506
  74.9 29.4 %all_to_all.11 = f32[16,4,8,128]{3,2,1,0:T(8,128)S(1)} all-to-all(f32[16,4,8,128]{3,2,1,0:T(8,128)S(1)} %get-tuple-element.37), channel_id=1, replica_groups=mesh['z'=16,'y'=4,'n'=8] {'z'}, dimensions={0} | all-to-all | bytes 524288 | tf_op jit(solution)/shard_map/all_to_all | solution.py:552
  104.3 15.5 %shard_map.33 = f32[8,8,512]{2,1,0:T(8,128)} custom-call(f32[64,8,128]{2,1,0:T(8,128)S(1)} %bitcast.5, f32[10,2,16,128]{3,2,1,0:T(8,128)S(1)} %get-tuple-element.38.x1h, f32[24,2,8,128]{3,2,1,0:T(8,128)S(1)} %get-tuple-element.39.x2, f32[24,2,8,128]{3,2,1,0:T(8,128)S(1)} %get-tuple-element.40.b2, f32[24,2,8,128]{3,2,1,0:T(8,128)S(1)} %get-tuple-element.41.fx2, ...), custom_call_target="tpu_custom_call" | custom-call | tf_op jit(solution)/shard_map/pallas_call | solution.py:506
Async XLA Ops:
  0.0 0.9 copy-start
  0.9 0.9 copy-start.1
  2.5 11.0 %collective-permute-start = (f32[13,4,8,128]{3,2,1,0:T(8,128)S(1)}, f32[13,4,8,128]{3,2,1,0:T(8,128)S(1)}, u32[]{:S(2)}, u32[]{:S(2)}) collective-permute-start(f32[13,4,8,128]{3,2,1,0:T(8,128)S(1)} %get-tuple-element.32), channel_id=1, source_target_pairs={{0,8},{8,16},{16,24},{24,32},{32,40},{40,48},{48,56},{56,64},{64,7... | collective-permute-start | bytes 638984 | tf_op jit(solution)/shard_map/ppermute | solution.py:526
  6.0 8.7 %collective-permute-start.1 = (f32[13,4,8,128]{3,2,1,0:T(8,128)S(1)}, f32[13,4,8,128]{3,2,1,0:T(8,128)S(1)}, u32[]{:S(2)}, u32[]{:S(2)}) collective-permute-start(f32[13,4,8,128]{3,2,1,0:T(8,128)S(1)} %get-tuple-element.33), channel_id=1, source_target_pairs={{0,504},{8,0},{16,8},{24,16},{32,24},{40,32},{48,40},{56,48},{64,5... | collective-permute-start | bytes 638984 | tf_op jit(solution)/shard_map/ppermute | solution.py:527
  14.7 9.5 %collective-permute-start.3 = (f32[42,4,8,128]{3,2,1,0:T(8,128)S(1)}, f32[42,4,8,128]{3,2,1,0:T(8,128)S(1)}, u32[]{:S(2)}, u32[]{:S(2)}) collective-permute-start(f32[42,4,8,128]{3,2,1,0:T(8,128)S(1)} %shard_map.29.mid), channel_id=1, source_target_pairs={{0,7},{1,0},{2,1},{3,2},{4,3},{5,4},{6,5},{7,6},{8,15},{9,8},{10,9... | collective-permute-start | bytes 2064392 | tf_op jit(solution)/shard_map/ppermute | solution.py:530
  15.8 11.6 %collective-permute-start.2 = (f32[42,4,8,128]{3,2,1,0:T(8,128)S(1)}, f32[42,4,8,128]{3,2,1,0:T(8,128)S(1)}, u32[]{:S(2)}, u32[]{:S(2)}) collective-permute-start(f32[42,4,8,128]{3,2,1,0:T(8,128)S(1)} %shard_map.29.mid), channel_id=1, source_target_pairs={{0,1},{1,2},{2,3},{3,4},{4,5},{5,6},{6,7},{7,0},{8,9},{9,10},{10,1... | collective-permute-start | bytes 2064392 | tf_op jit(solution)/shard_map/ppermute | solution.py:529
  55.0 11.3 %collective-permute-start.4 = (f32[44,8,128]{2,1,0:T(8,128)S(1)}, f32[44,8,128]{2,1,0:T(8,128)S(1)}, u32[]{:S(2)}, u32[]{:S(2)}) collective-permute-start(f32[44,8,128]{2,1,0:T(8,128)S(1)} %get-tuple-element.35), channel_id=1, source_target_pairs={{0,32},{32,64},{64,96},{96,128},{128,160},{160,192},{192,224},{224... | collective-permute-start | bytes 540680 | tf_op jit(solution)/shard_map/ppermute | solution.py:542
  58.9 10.6 %collective-permute-start.5 = (f32[44,8,128]{2,1,0:T(8,128)S(1)}, f32[44,8,128]{2,1,0:T(8,128)S(1)}, u32[]{:S(2)}, u32[]{:S(2)}) collective-permute-start(f32[44,8,128]{2,1,0:T(8,128)S(1)} %get-tuple-element.36), channel_id=1, source_target_pairs={{0,480},{32,0},{64,32},{96,64},{128,96},{160,128},{192,160},{224,1... | collective-permute-start | bytes 540680 | tf_op jit(solution)/shard_map/ppermute | solution.py:543

commit v2 on v1

--- a/solution.py
+++ b/solution.py
@@ -96,11 +96,8 @@
 
 
 def loop(low, high, body):
-    def step(i, carry):
-        body(i)
-        return carry
-
-    lax.fori_loop(low, high, step, 0)
+    for k in range(high - low):
+        body(low + k)
 
 
 def inverse(c, diagonal):
@@ -108,16 +105,26 @@
 
 
 C_LOW, B_LOW = 7, 6
-C_PLANES, B_PLANES = 8 + 2 * C_LOW, 8 + 2 * B_LOW
 SENT = C_LOW + B_LOW
-WIDE_PLANES = C_PLANES + B_PLANES
-
-
-def split_kernel(rhs, beta, own, up, down):
+
+CORNERS = (
+    (0, 1, 0, 0), (0, 2, 0, 0), (0, 3, 7, 2), (0, 4, 6, 3), (0, 5, 0, 0),
+    (1, 1, 6, 2), (1, 2, 0, 0), (1, 3, 5, 3), (1, 4, 0, 0),
+)
+
+
+def split_kernel(rhs_hbm, beta_hbm, own, up, down, rhs, beta, sems):
+    copies = [
+        pltpu.make_async_copy(beta_hbm, beta, sems.at[0]),
+        pltpu.make_async_copy(rhs_hbm, rhs, sems.at[1]),
+    ]
+    for copy in copies:
+        copy.start()
     z = iota((512, 512), 0)
     k = iota((512, 512), 1)
     chooser = ones_where(z == 4 * (k % 128) + k // 128)
     for field, source in enumerate((beta, rhs)):
+        copies[field].wait()
         out = dot_exact(source[...].reshape(64, 512), chooser)
         for x in range(8):
             for q in range(4):
@@ -131,35 +138,70 @@
                     down[start + x, q] = tile
 
 
-def widen_kernel(own, below, above, out, *, wide):
+def side_index(side, field, distance):
+    width, start = (C_LOW, B_LOW)[field], (0, C_LOW)[field]
+    return start + (width - distance if side == 0 else distance - 1)
+
+
+def corner_kernel(below, above, right, left, *, wide):
     index = lax.axis_index("z") * lax.axis_size("y") + lax.axis_index("y")
-    keep_low = jnp.where(index > 0, 1.0, 0.0).astype(F32)
-    keep_high = jnp.where(index < wide - 1, 1.0, 0.0).astype(F32)
-    for j in range(C_LOW):
-        out[j] = below[j] * keep_low
-        out[C_LOW + 8 + j] = above[j] * keep_high
-    for j in range(8):
-        out[C_LOW + j] = own[j]
-        out[C_PLANES + B_LOW + j] = own[8 + j]
-    for j in range(B_LOW):
-        out[C_PLANES + j] = below[C_LOW + j]
-        out[C_PLANES + B_LOW + 8 + j] = above[C_LOW + j]
-
-
-def down_kernel(mid, left, right, packed, x0, b0, fx, fy, fz, dinv, c1, b1, fx1, fy1, fz1, dinv1, diag, first, sums, diag1, first1, x1, *, group):
+    keep = [jnp.where(index > 0, 1.0, 0.0).astype(F32), jnp.where(index < wide - 1, 1.0, 0.0).astype(F32)]
+    row = iota((8, 128), 0)
+    for side, planes in enumerate((below, above)):
+        for t, (field, one, two, rows) in enumerate(CORNERS):
+            place = side * len(CORNERS) + t
+            for q in range(4):
+                tile = planes[side_index(side, field, one), q]
+                to_right = to_left = tile
+                if two:
+                    other = planes[side_index(side, field, two), q]
+                    to_right = jnp.where(row >= rows, tile, pltpu.roll(other, rows, 0))
+                    to_left = jnp.where(row < 8 - rows, tile, pltpu.roll(other, 8 - rows, 0))
+                if field == 0:
+                    to_right, to_left = to_right * keep[side], to_left * keep[side]
+                right[place, q] = to_right
+                left[place, q] = to_left
+
+
+def down_kernel(own, below, above, own_left, own_right, corner_left, corner_right, packed, x0, b0, fx, fy, fz, dinv, c1, x1, r1, fx1, fy1, fz1, dinv1, diag, first, sums, diag1, first1, b1, parts, *, wide, depth):
     n = lax.axis_index("n")
+    index = lax.axis_index("z") * lax.axis_size("y") + lax.axis_index("y")
+    keep_wide = [jnp.where(index > 0, 1.0, 0.0).astype(F32), jnp.where(index < wide - 1, 1.0, 0.0).astype(F32)]
     keep_left = jnp.where(n > 0, 1.0, 0.0).astype(F32)
     keep_right = jnp.where(n < lax.axis_size("n") - 1, 1.0, 0.0).astype(F32)
     lane = iota((24, 128), 1)
     last, begin = lane == 127, lane == 0
 
+    corner = {}
+    for t, (field, one, two, rows) in enumerate(CORNERS):
+        corner[field, one] = (t, 0)
+        if two:
+            corner[field, two] = (t, rows)
+
+    def plane(field, p, keep_0, keep_1):
+        x = p - 8
+        out = []
+        for q in range(4):
+            if 0 <= x < 8:
+                parts = [own_left[8 * field + x, q], own[8 * field + x, q], own_right[8 * field + x, q]]
+            else:
+                side, distance = (0, -x) if x < 0 else (1, x - 7)
+                t, rows = corner[field, distance]
+                place = side * len(CORNERS) + t
+                parts = [corner_left[place, q], (below, above)[side][side_index(side, field, distance), q], corner_right[place, q]]
+                if rows:
+                    parts[0] = pltpu.roll(parts[0], 8 - rows, 0)
+                    parts[2] = pltpu.roll(parts[2], rows, 0)
+                if field == 0:
+                    parts[1] = parts[1] * keep_wide[side]
+            out.append(jnp.concatenate([parts[0] * keep_0, parts[1], parts[2] * keep_1] if field == 0 else parts, axis=0))
+        return out
+
     def cells(p):
-        j = p - 1
-        return [jnp.concatenate([left[j, q] * keep_left, mid[j, q], right[j, q] * keep_right], axis=0) for q in range(4)]
+        return plane(0, p, keep_left, keep_right)
 
     def source(p):
-        j = p - 2 + C_PLANES
-        return [jnp.concatenate([left[j, q], mid[j, q], right[j, q]], axis=0) for q in range(4)]
+        return plane(1, p, None, None)
 
     before, after = cells(1), cells(2)
     for q in range(4):
@@ -234,47 +276,56 @@
 
     loop(2, 8, second_1)
 
-    for x in range(4):
-        for q in range(2):
-            packed[0, x, 4 * q : 4 * q + 4] = x1[3 + x, q, 4:8]
+    y, size = lax.axis_index("y"), lax.axis_size("n")
     for x in range(2):
         total = jnp.zeros((16, 128), F32)
         cell = jnp.zeros((16, 128), F32)
         for p in (3 + 2 * x, 4 + 2 * x):
             near = neighbours(x1, fx1, fz1, fy1, p, 2, 1)
             for q in range(2):
-                total = total + (b1[p, q] + near[q] - diag1[p, q] * x1[p, q])
+                rest = b1[p, q] + near[q] - diag1[p, q] * x1[p, q]
+                r1[p, q] = rest
+                total = total + rest
                 cell = cell + c1[p, q]
+                place = p - 3
+                parts[place // 2, place % 2, 4 * q : 4 * q + 4] = rest[4:8]
+                row = 4 * (place % 2) + 2 * q
+                parts[2, place // 2, row : row + 2] = rest[6:8]
+                parts[3, place // 2, row : row + 2] = rest[4:6]
         total = 0.125 * (total + shift(total, 1, 0))
         cell = 0.125 * (cell + shift(cell, 1, 0))
         for yy in range(2):
-            packed[0, 4, 2 * x + yy : 2 * x + yy + 1] = total[4 + 2 * yy : 5 + 2 * yy]
-            packed[0, 4, 4 + 2 * x + yy : 5 + 2 * x + yy] = cell[4 + 2 * yy : 5 + 2 * yy]
-
-    def copy(s):
-        packed[s] = packed[0]
-
-    loop(1, group, copy)
+            packed[0, 2, 2 * x + yy : 2 * x + yy + 1] = total[4 + 2 * yy : 5 + 2 * yy]
+            packed[0, 2, 4 + 2 * x + yy : 5 + 2 * x + yy] = cell[4 + 2 * yy : 5 + 2 * yy]
+
+    level_two = packed[0, 2]
+    for y_to in range(depth):
+        ahead = (y_to - y + depth) % depth
+        for n_to in range(size):
+            beside = jnp.where(n_to > n, 2, 3)
+            part = jnp.where(ahead == 0, beside, jnp.where(ahead == 1, 1, 0))
+            s = y_to * size + n_to
+            packed[s, 0] = parts[part, 0]
+            packed[s, 1] = parts[part, 1]
+            packed[s, 2] = level_two
 
 
 def edge_kernel(plane, up, down, *, depth):
     n = lax.axis_index("n")
     size = lax.axis_size("n")
 
-    def slab(s):
-        tile = plane[s, 4]
-        up[s] = tile
-        down[s] = tile
-
-    loop(0, depth * size, slab)
+    count = (depth - 1) * size
+    for s in range(count):
+        up[s] = plane[size + s, 2]
+        down[s] = plane[s, 2]
     for k in range(3):
         place = jnp.clip(n + (k - 1), 0, size - 1)
-        for x in range(4):
-            up[depth * size + 4 * k + x] = plane[(depth - 1) * size + place, x]
-            down[depth * size + 4 * k + x] = plane[place, x]
-
-
-def middle_kernel(plane, below, above, sent, x2, b2, fx, fy, fz, dinv, x1, c2, diag, first, *, depth, tall):
+        for j in range(2):
+            up[count + 2 * k + j] = plane[count + place, j]
+            down[count + 2 * k + j] = plane[place, j]
+
+
+def middle_kernel(plane, below, above, r1, sent, x2, r2, fx, fy, fz, dinv, r1h, b2, c2, diag, first, *, depth, tall):
     z, y, n = lax.axis_index("z"), lax.axis_index("y"), lax.axis_index("n")
     size = lax.axis_size("n")
     keep_low = jnp.where(z > 0, 1.0, 0.0).astype(F32)
@@ -285,21 +336,24 @@
             for yy in range(2):
                 r = 2 * x + yy
                 place = 2 * yb + x
-                own = yb * size * 40 + 32 + r
-                edge = yb * size * 8 + r
-                b2[place, yy] = below[pl.ds(edge, 8, stride=8), :]
-                b2[width + place, yy] = plane[pl.ds(own, 8, stride=40), :]
-                b2[2 * width + place, yy] = above[pl.ds(edge, 8, stride=8), :]
-                c2[place, yy] = below[pl.ds(edge + 4, 8, stride=8), :] * keep_low
-                c2[width + place, yy] = plane[pl.ds(own + 4, 8, stride=40), :]
-                c2[2 * width + place, yy] = above[pl.ds(edge + 4, 8, stride=8), :] * keep_high
+                own = yb * size * 24 + 16 + r
+                b2[width + place, yy] = plane[pl.ds(own, 8, stride=24), :]
+                c2[width + place, yy] = plane[pl.ds(own + 4, 8, stride=24), :]
+                if yb > 0:
+                    edge = (yb - 1) * size * 8 + r
+                    b2[place, yy] = below[pl.ds(edge, 8, stride=8), :]
+                    c2[place, yy] = below[pl.ds(edge + 4, 8, stride=8), :] * keep_low
+                if yb < depth - 1:
+                    edge = yb * size * 8 + r
+                    b2[2 * width + place, yy] = above[pl.ds(edge, 8, stride=8), :]
+                    c2[2 * width + place, yy] = above[pl.ds(edge + 4, 8, stride=8), :] * keep_high
 
     scale = 0.5 / 16.0
     shape = (8, 128)
     row, lane = iota(shape, 0), iota(shape, 1)
     last, begin, last_b, begin_b = row == 7, row == 0, lane == 127, lane == 0
     for q in range(2):
-        fx[0, q] = scale * (c2[0, q] + c2[1, q])
+        fx[2, q] = scale * (c2[2, q] + c2[3, q])
 
     def faces_2(p):
         c, c_next = [c2[p, q] for q in range(2)], [c2[p + 1, q] for q in range(2)]
@@ -310,26 +364,26 @@
             dinv[p, q] = inv
             first[p, q] = b2[p, q] * inv * (1.0 / THETA)
 
-    loop(1, 3 * width - 1, faces_2)
+    loop(3, 3 * width - 3, faces_2)
 
     def second_2(p):
         near = neighbours(first, fx, fy, fz, p, 2, 0)
         for q in range(2):
             x2[p, q] = (1.0 + KEEP - GAIN) * first[p, q] + GAIN * (b2[p, q] + near[q]) * dinv[p, q]
 
-    loop(2, 3 * width - 2, second_2)
-
-    totals, cell_sums = [], []
-    for j in range(depth):
-        total = jnp.zeros(shape, F32)
-        cell = jnp.zeros(shape, F32)
-        for p in (width + 2 * j, width + 2 * j + 1):
-            near = neighbours(x2, fx, fy, fz, p, 2, 0)
-            for q in range(2):
-                total = total + (b2[p, q] + near[q] - diag[p, q] * x2[p, q])
-                cell = cell + c2[p, q]
-        totals.append(total)
-        cell_sums.append(cell)
+    loop(4, 3 * width - 4, second_2)
+
+    totals = [jnp.zeros(shape, F32)] * depth
+    cell_sums = [jnp.zeros(shape, F32)] * depth
+    for p in range(5, 3 * width - 5):
+        near = neighbours(x2, fx, fy, fz, p, 2, 0)
+        j = (p - width) // 2
+        for q in range(2):
+            rest = b2[p, q] + near[q] - diag[p, q] * x2[p, q]
+            r2[p, q] = rest
+            if 0 <= j < depth:
+                totals[j] = totals[j] + rest
+                cell_sums[j] = cell_sums[j] + c2[p, q]
     zz, k = iota((128, 128), 0), iota((128, 128), 1)
     low_half = ones_where(k == zz // 2, 0.125)
     high_half = ones_where(k == zz // 2 + 64, 0.125)
@@ -338,37 +392,42 @@
     for s in range(tall):
         sent[s] = coarse
 
-    for x in range(4):
-        for k in range(3):
-            place = jnp.clip(n + (k - 1), 0, size - 1)
-
-            def block(yb):
-                start = pl.multiple_of((yb * size + place) * 40 + 8 * x, 8)
-                return plane[pl.ds(start, 8), :]
-
-            edge = 8 * (depth * size + 4 * k + x)
-            tiles = {
-                -1: jnp.where(y == 0, below[edge : edge + 8], block(jnp.maximum(y - 1, 0))),
-                0: block(y),
-                1: jnp.where(y == depth - 1, above[edge : edge + 8], block(jnp.minimum(y + 1, depth - 1))),
-            }
-            for dx, tile in tiles.items():
-                p = 3 + 4 * dx + x
-                if 0 <= p < 10:
+    for p in range(3, 7):
+        for q in range(2):
+            r1h[p, q] = r1[p, q]
+    edges = 8 * (depth - 1) * size
+    for k in range(3):
+        place = jnp.clip(n + (k - 1), 0, size - 1)
+
+        def block(yb, j):
+            start = pl.multiple_of((yb * size + place) * 24 + 8 * j, 8)
+            return plane[pl.ds(start, 8), :]
+
+        for j in range(2):
+            start = edges + 8 * (2 * k + j)
+            low = jnp.where(y == 0, below[start : start + 8], block(jnp.maximum(y - 1, 0), j))
+            high = jnp.where(y == depth - 1, above[start : start + 8], block(jnp.minimum(y + 1, depth - 1), j))
+            for q in range(2):
+                r1h[1 + j, q, 4 * k : 4 * k + 4] = low[4 * q : 4 * q + 4]
+                r1h[7 + j, q, 4 * k : 4 * k + 4] = high[4 * q : 4 * q + 4]
+                r1h[1 + j, q, 12:16] = jnp.zeros((4, 128), F32)
+                r1h[7 + j, q, 12:16] = jnp.zeros((4, 128), F32)
+            if k != 1:
+                tile = block(y, j)
+                start = 2 if k == 0 else 8
+                for x in range(2):
                     for q in range(2):
-                        x1[p, q, 4 * k : 4 * k + 4] = tile[4 * q : 4 * q + 4]
-    for p in range(10):
-        for q in range(2):
-            x1[p, q, 12:16] = jnp.zeros((4, 128), F32)
-
-
-def sweeps(start, mid, out, source, fx, fa, fb, dinv, low, high, count, axis):
+                        row = 4 * x + 2 * q
+                        r1h[3 + 2 * j + x, q, start : start + 2] = tile[row : row + 2]
+
+
+def sweeps(start, mid, out, source, fx, fa, fb, dinv, low, planes, count, axis):
     def one(p):
         near = neighbours(start, fx, fa, fb, p, count, axis)
         for q in range(count):
             mid[p, q] = (1.0 - 1.0 / THETA) * start[p, q] + (1.0 / THETA) * ((source[p, q] + near[q]) * dinv[p, q])
 
-    loop(low - 1, high + 1, one)
+    loop(-1, planes + 1, lambda k: one(low + k))
 
     def two(p):
         near = neighbours(mid, fx, fa, fb, p, count, axis)
@@ -376,10 +435,10 @@
             value = (1.0 - GAIN + KEEP) * mid[p, q] - KEEP * start[p, q]
             out(p, q, value + GAIN * ((source[p, q] + near[q]) * dinv[p, q]))
 
-    loop(low, high, two)
-
-
-def up_kernel(gathered, x1h, x2, b2, fx2, fy2, fz2, dinv2, c1, b1, fx1, fy1, fz1, dinv1, x0, b0, fx, fy, fz, dinv, result,
+    loop(0, planes, lambda k: two(low + k))
+
+
+def up_kernel(gathered, r1h, x2, r2, fx2, fy2, fz2, dinv2, c1, x1, fx1, fy1, fz1, dinv1, x0, b0, fx, fy, fz, dinv, result,
               c3, p3, r3, x3, i3, fx3, fy3, fz3, d3, s2, m2, f2, s1, m1, f1, s0, m0, f0, *, depth, tall):
     z, y, n = lax.axis_index("z"), lax.axis_index("y"), lax.axis_index("n")
     half = depth * tall // 2
@@ -459,12 +518,12 @@
         add = fine[8 * j : 8 * j + 8]
         for p in (base + 2 * j, base + 2 * j + 1):
             for q in range(2):
-                s2[p, q] = jnp.where(dinv2[p, q] > 0.0, x2[p, q] + add, 0.0)
+                s2[p, q] = jnp.where(dinv2[p, q] > 0.0, add, 0.0)
 
     def keep_2(p, q, value):
-        f2[p, q] = value
-
-    sweeps(s2, m2, keep_2, b2, fx2, fy2, fz2, dinv2, base + 2, base + 8, 2, 0)
+        f2[p, q] = x2[p, q] + value
+
+    sweeps(s2, m2, keep_2, r2, fx2, fy2, fz2, dinv2, base + 2, 6, 2, 0)
 
     wide = jnp.concatenate([jnp.concatenate([f2[base + 2 + k, 0], f2[base + 2 + k, 1]], axis=0) for k in range(6)], axis=1)
     r, k = iota((16, 16), 0), iota((16, 16), 1)
@@ -474,12 +533,12 @@
     for p in range(10):
         k = (p + 1) // 2
         for q in range(2):
-            s1[p, q] = jnp.where(c1[p, q] > 0.0, x1h[p, q] + fine[:, 128 * k : 128 * k + 128], 0.0)
+            s1[p, q] = jnp.where(c1[p, q] > 0.0, fine[:, 128 * k : 128 * k + 128], 0.0)
 
     def keep_1(p, q, value):
-        f1[p, q] = value
-
-    sweeps(s1, m1, keep_1, b1, fx1, fz1, fy1, dinv1, 2, 8, 2, 1)
+        f1[p, q] = x1[p, q] + value
+
+    sweeps(s1, m1, keep_1, r1h, fx1, fz1, fy1, dinv1, 2, 6, 2, 1)
 
     wide = jnp.concatenate([f1[p, q] for p in range(2, 8) for q in range(2)], axis=1)
     r, k = iota((24, 16), 0), iota((24, 16), 1)
@@ -495,7 +554,7 @@
             start = pl.multiple_of(start, 8)
         f0[pl.ds(start, 8), 128 * q : 128 * q + 128] = value[8:16]
 
-    sweeps(s0, m0, keep_0, b0, fx, fz, fy, dinv, 8, 16, 4, 1)
+    sweeps(s0, m0, keep_0, b0, fx, fz, fy, dinv, 8, 8, 4, 1)
     k, z0 = iota((512, 512), 0), iota((512, 512), 1)
     back = ones_where(z0 == 4 * (k % 128) + k // 128)
     result[...] = dot_exact(f0[...], back).reshape(8, 8, 512)
@@ -513,6 +572,18 @@
     )(*operands)
 
 
+def split(rhs_field, beta_cells):
+    outs = [(16, 4, 8, 128), (SENT, 4, 8, 128), (SENT, 4, 8, 128)]
+    return pl.pallas_call(
+        split_kernel,
+        out_shape=[jax.ShapeDtypeStruct(shape, F32) for shape in outs],
+        in_specs=[pl.BlockSpec(memory_space=pltpu.HBM)] * 2,
+        out_specs=[pl.BlockSpec(memory_space=pltpu.VMEM)] * 3,
+        scratch_shapes=[pltpu.VMEM((8, 8, 512), F32)] * 2 + [pltpu.SemaphoreType.DMA((2,))],
+        compiler_params=pltpu.CompilerParams(vmem_limit_bytes=40 * 2**20),
+    )(pltpu.with_memory_space_constraint(rhs_field, pltpu.HBM), pltpu.with_memory_space_constraint(beta_cells, pltpu.HBM))
+
+
 def ring(axis_size, step):
     return [(i, (i + step) % axis_size) for i in range(axis_size)]
 
@@ -520,24 +591,27 @@
 def shards(rhs_field, beta_cells):
     tall, depth, size = lax.axis_size("z"), lax.axis_size("y"), lax.axis_size("n")
     wide, group = tall * depth, depth * size
-    own, up, down = call(
-        split_kernel, [(16, 4, 8, 128), (SENT, 4, 8, 128), (SENT, 4, 8, 128)], rhs_field, beta_cells
-    )
+    own, up, down = split(rhs_field, beta_cells)
+    own_left = lax.ppermute(own, "n", ring(size, 1))
+    own_right = lax.ppermute(own, "n", ring(size, -1))
     below = lax.ppermute(up, ("z", "y"), ring(wide, 1))
     above = lax.ppermute(down, ("z", "y"), ring(wide, -1))
-    (mid,) = call(functools.partial(widen_kernel, wide=wide), [(WIDE_PLANES, 4, 8, 128)], own, below, above)
-    left = lax.ppermute(mid, "n", ring(size, 1))
-    right = lax.ppermute(mid, "n", ring(size, -1))
+    below, above, own_left, own_right = lax.optimization_barrier((below, above, own_left, own_right))
+    corners = (2 * len(CORNERS), 4, 8, 128)
+    to_right, to_left = call(functools.partial(corner_kernel, wide=wide), [corners] * 2, below, above)
+    corner_left = lax.ppermute(to_right, "n", ring(size, 1))
+    corner_right = lax.ppermute(to_left, "n", ring(size, -1))
     fine, coarse = (24, 4, 24, 128), (10, 2, 16, 128)
     outs = call(
-        functools.partial(down_kernel, group=group),
-        [(group, 5, 8, 128)] + [fine] * 6 + [coarse] * 6,
-        mid, left, right,
-        scratch=[fine, fine, (18, 2, 32, 128), coarse, coarse, coarse],
+        functools.partial(down_kernel, wide=wide, depth=depth),
+        [(group, 3, 8, 128)] + [fine] * 6 + [coarse] * 7,
+        own, below, above, own_left, own_right, corner_left, corner_right,
+        scratch=[fine, fine, (18, 2, 32, 128), coarse, coarse, coarse, (4, 2, 8, 128)],
     )
-    packed, level_zero, level_one = outs[0], outs[1:7], outs[7:13]
+    packed, level_zero = outs[0], outs[1:7]
+    c1, x1, r1, *faces_1 = outs[7:14]
     plane = lax.all_to_all(packed, ("y", "n"), 0, 0)
-    edge = group + 12
+    edge = group - size + 6
     up, down = call(functools.partial(edge_kernel, depth=depth), [(edge, 8, 128)] * 2, plane)
     below = lax.ppermute(up, "z", ring(tall, 1))
     above = lax.ppermute(down, "z", ring(tall, -1))
@@ -545,16 +619,16 @@
     outs = call(
         functools.partial(middle_kernel, depth=depth, tall=tall),
         [(tall, depth, 8, 128)] + [slab] * 6 + [coarse],
-        plane.reshape(group * 40, 128), below.reshape(edge * 8, 128), above.reshape(edge * 8, 128),
-        scratch=[slab, slab, slab],
+        plane.reshape(group * 24, 128), below.reshape(edge * 8, 128), above.reshape(edge * 8, 128), r1,
+        scratch=[slab, slab, slab, slab],
     )
-    sent, level_two, x1h = outs[0], outs[1:7], outs[7]
+    sent, level_two, r1h = outs[0], outs[1:7], outs[7]
     gathered = lax.all_to_all(sent, "z", 0, 0)
     packed_3 = (wide // 2 + 2, 1, 8, 128)
     (result,) = call(
         functools.partial(up_kernel, depth=depth, tall=tall),
         [(8, 8, 512)],
-        gathered.reshape(wide, 8, 128), x1h, *level_two, *level_one, *level_zero,
+        gathered.reshape(wide, 8, 128), r1h, *level_two, c1, x1, *faces_1, *level_zero,
         scratch=[packed_3] * 9 + [slab] * 3 + [coarse] * 3 + [fine] * 2 + [(64, 512)],
     )
     return result

time: 120 us -> 94.7 us (0.79)
  the two profiles are of different devices: /device:TPU:32 before, /device:TPU:64 now
where the time goes in v2:
time: 94.7 us; the launch traced here: 94.4 us
  blocking collectives  49 us (52%)
  starting transfers between devices  21.3 us (22%)
  waiting for transfers between devices  13.3 us (14%)
  Pallas kernels  10.8 us (11%)
    all_to_all x1, blocking collectives, shards(): gathered = lax.all_to_all(sent, 'z', 0, 0)  29.8 us
    all_to_all x1, blocking collectives, shards(): plane = lax.all_to_all(packed, ('y', 'n'), 0, 0)  19.2 us
    pallas_call x5, Pallas kernels, call(): pl.pallas_call(kernel, out_shape=shapes, in_specs=[pl.BlockSpec(memory_sp...  9.1 us
    ppermute x1, starting transfers between devices, shards(): below = lax.ppermute(up, 'z', ring(tall, 1))  6.24 us
    ppermute x1, starting transfers between devices, shards(): above = lax.ppermute(down, ('z', 'y'), ring(wide, -1))  4.47 us
    ppermute x1, waiting for transfers between devices, shards(): corner_left = lax.ppermute(to_right, 'n', ring(size, 1))  4.4 us
    ppermute x1, waiting for transfers between devices, shards(): above = lax.ppermute(down, 'z', ring(tall, -1))  4.12 us
    ppermute x1, starting transfers between devices, shards(): below = lax.ppermute(up, ('z', 'y'), ring(wide, 1))  3.47 us
  transfers between devices with their start and end apart: 8, of which 5 were waited for; matrix products, arithmetic and copies ran while one was open for 0% of the time, Pallas kernels for 0%

profile of v2, /device:TPU:64, one launch (start us, length us, event | category | flops | bytes accessed | tf_op | source)
XLA Modules:
  0.0 94.4 jit_solution(16503905471274317348)
XLA Ops:
  0.0 1.7 %shard_map.28 = (f32[16,4,8,128]{3,2,1,0:T(8,128)S(1)}, f32[13,4,8,128]{3,2,1,0:T(8,128)S(1)}, f32[13,4,8,128]{3,2,1,0:T(8,128)S(1)}) custom-call(f32[8,8,512]{2,1,0:T(8,128)} %rhs_hbm.1, f32[8,8,512]{2,1,0:T(8,128)} %beta_hbm.1), custom_call_target="tpu_custom_call" | custom-call | tf_op jit(solution)/shard_map/pallas_call | solution.py:577
  1.7 2.2 %collective-permute-start.3 = (f32[16,4,8,128]{3,2,1,0:T(8,128)S(1)}, f32[16,4,8,128]{3,2,1,0:T(8,128)S(1)}, u32[]{:S(2)}, u32[]{:S(2)}) collective-permute-start(f32[16,4,8,128]{3,2,1,0:T(8,128)S(1)} %get-tuple-element.38.own), channel_id=1, source_target_pairs={{0,7},{1,0},{2,1},{3,2},{4,3},{5,4},{6,5},{7,6},{8,15},{9,8},{10,9... | collective-permute-start | bytes 786440 | tf_op jit(solution)/shard_map/ppermute | solution.py:596
  3.9 0.0 collective-permute-start.2
  3.9 3.5 %collective-permute-start = (f32[13,4,8,128]{3,2,1,0:T(8,128)S(1)}, f32[13,4,8,128]{3,2,1,0:T(8,128)S(1)}, u32[]{:S(2)}, u32[]{:S(2)}) collective-permute-start(f32[13,4,8,128]{3,2,1,0:T(8,128)S(1)} %get-tuple-element.39), channel_id=1, source_target_pairs={{0,8},{8,16},{16,24},{24,32},{32,40},{40,48},{48,56},{56,64},{64,7... | collective-permute-start | bytes 638984 | tf_op jit(solution)/shard_map/ppermute | solution.py:597
  7.4 4.5 %collective-permute-start.1 = (f32[13,4,8,128]{3,2,1,0:T(8,128)S(1)}, f32[13,4,8,128]{3,2,1,0:T(8,128)S(1)}, u32[]{:S(2)}, u32[]{:S(2)}) collective-permute-start(f32[13,4,8,128]{3,2,1,0:T(8,128)S(1)} %get-tuple-element.40), channel_id=1, source_target_pairs={{0,504},{8,0},{16,8},{24,16},{32,24},{40,32},{48,40},{56,48},{64,5... | collective-permute-start | bytes 638984 | tf_op jit(solution)/shard_map/ppermute | solution.py:598
  11.9 2.6 %collective-permute-done.below = f32[13,4,8,128]{3,2,1,0:T(8,128)S(1)} collective-permute-done((f32[13,4,8,128]{3,2,1,0:T(8,128)S(1)}, f32[13,4,8,128]{3,2,1,0:T(8,128)S(1)}, u32[]{:S(2)}, u32[]{:S(2)}) %collective-permute-start) | collective-permute-done | bytes 213024 | tf_op jit(solution)/shard_map/ppermute | solution.py:597
  14.5 1.2 %collective-permute-done.1.above = f32[13,4,8,128]{3,2,1,0:T(8,128)S(1)} collective-permute-done((f32[13,4,8,128]{3,2,1,0:T(8,128)S(1)}, f32[13,4,8,128]{3,2,1,0:T(8,128)S(1)}, u32[]{:S(2)}, u32[]{:S(2)}) %collective-permute-start.1) | collective-permute-done | bytes 213024 | tf_op jit(solution)/shard_map/ppermute | solution.py:598
  15.7 0.0 collective-permute-done.3.own_right
  15.7 0.0 collective-permute-done.2.own_left
  15.8 0.0 collective-permute-start.4
  15.8 2.9 %collective-permute-start.5 = (f32[18,4,8,128]{3,2,1,0:T(8,128)S(1)}, f32[18,4,8,128]{3,2,1,0:T(8,128)S(1)}, u32[]{:S(2)}, u32[]{:S(2)}) collective-permute-start(f32[18,4,8,128]{3,2,1,0:T(8,128)S(1)} %get-tuple-element.46), channel_id=1, source_target_pairs={{0,7},{1,0},{2,1},{3,2},{4,3},{5,4},{6,5},{7,6},{8,15},{9,8},{10,9... | collective-permute-start | bytes 884744 | tf_op jit(solution)/shard_map/ppermute | solution.py:603
  18.7 4.4 %collective-permute-done.4.corner_left = f32[18,4,8,128]{3,2,1,0:T(8,128)S(1)} collective-permute-done((f32[18,4,8,128]{3,2,1,0:T(8,128)S(1)}, f32[18,4,8,128]{3,2,1,0:T(8,128)S(1)}, u32[]{:S(2)}, u32[]{:S(2)}) %collective-permute-start.4) | collective-permute-done | bytes 294944 | tf_op jit(solution)/shard_map/ppermute | solution.py:602
  23.1 0.0 collective-permute-done.5.corner_right
  23.1 2.6 %shard_map.30 = (f32[32,3,8,128]{3,2,1,0:T(8,128)S(1)}, f32[24,4,24,128]{3,2,1,0:T(8,128)S(1)}, f32[24,4,24,128]{3,2,1,0:T(8,128)S(1)}, f32[24,4,24,128]{3,2,1,0...) custom-call(f32[16,4,8,128]{3,2,1,0:T(8,128)S(1)} %get-tuple-element, ...), custom_call_target="tpu_custom_call" | custom-call | tf_op jit(solution)/shard_map/pallas_call | solution.py:565
  25.8 19.2 %all_to_all.10.plane = f32[32,3,8,128]{3,2,1,0:T(8,128)S(1)} all-to-all(f32[32,3,8,128]{3,2,1,0:T(8,128)S(1)} %get-tuple-element.47), channel_id=1, replica_groups=mesh['z'=16,'y'=4,'n'=8] {'y','n'}, dimensions={0} | all-to-all | bytes 786432 | tf_op jit(solution)/shard_map/all_to_all | solution.py:613
  45.0 6.2 %collective-permute-start.6 = (f32[30,8,128]{2,1,0:T(8,128)S(1)}, f32[30,8,128]{2,1,0:T(8,128)S(1)}, u32[]{:S(2)}, u32[]{:S(2)}) collective-permute-start(f32[30,8,128]{2,1,0:T(8,128)S(1)} %get-tuple-element.48), channel_id=1, source_target_pairs={{0,32},{32,64},{64,96},{96,128},{128,160},{160,192},{192,224},{224... | collective-permute-start | bytes 368648 | tf_op jit(solution)/shard_map/ppermute | solution.py:616
  51.3 1.9 %collective-permute-start.7 = (f32[30,8,128]{2,1,0:T(8,128)S(1)}, f32[30,8,128]{2,1,0:T(8,128)S(1)}, u32[]{:S(2)}, u32[]{:S(2)}) collective-permute-start(f32[30,8,128]{2,1,0:T(8,128)S(1)} %get-tuple-element.49), channel_id=1, source_target_pairs={{0,480},{32,0},{64,32},{96,64},{128,96},{160,128},{192,160},{224,1... | collective-permute-start | bytes 368648 | tf_op jit(solution)/shard_map/ppermute | solution.py:617
  53.2 0.9 collective-permute-done.6
  54.1 4.1 %collective-permute-done.7 = f32[30,8,128]{2,1,0:T(8,128)S(1)} collective-permute-done((f32[30,8,128]{2,1,0:T(8,128)S(1)}, f32[30,8,128]{2,1,0:T(8,128)S(1)}, u32[]{:S(2)}, u32[]{:S(2)}) %collective-permute-start.7) | collective-permute-done | bytes 122912 | tf_op jit(solution)/shard_map/ppermute | solution.py:617
  58.2 0.6 shard_map.32
  58.9 29.8 %all_to_all.11 = f32[16,4,8,128]{3,2,1,0:T(8,128)S(1)} all-to-all(f32[16,4,8,128]{3,2,1,0:T(8,128)S(1)} %get-tuple-element.51), channel_id=1, replica_groups=mesh['z'=16,'y'=4,'n'=8] {'z'}, dimensions={0} | all-to-all | bytes 524288 | tf_op jit(solution)/shard_map/all_to_all | solution.py:626
  88.7 5.7 %shard_map.33 = f32[8,8,512]{2,1,0:T(8,128)} custom-call(f32[64,8,128]{2,1,0:T(8,128)S(1)} %bitcast.5, f32[10,2,16,128]{3,2,1,0:T(8,128)S(1)} %get-tuple-element.52.r1h, f32[24,2,8,128]{3,2,1,0:T(8,128)S(1)} %get-tuple-element.53.x2, f32[24,2,8,128]{3,2,1,0:T(8,128)S(1)} %get-tuple-element.54.r2, f32[24,2,8,128]{3,2,1,0:T(8,128)S(1)} %get-tuple-element.55.fx2, ...), custom_call_target="tpu_custom_call" | custom-call | tf_op jit(solution)/shard_map/pallas_call | solution.py:565
  (2 shorter events, 0.1 us)
Async XLA Ops:
  1.7 14.0 %collective-permute-start.3 = (f32[16,4,8,128]{3,2,1,0:T(8,128)S(1)}, f32[16,4,8,128]{3,2,1,0:T(8,128)S(1)}, u32[]{:S(2)}, u32[]{:S(2)}) collective-permute-start(f32[16,4,8,128]{3,2,1,0:T(8,128)S(1)} %get-tuple-element.38.own), channel_id=1, source_target_pairs={{0,7},{1,0},{2,1},{3,2},{4,3},{5,4},{6,5},{7,6},{8,15},{9,8},{10,9... | collective-permute-start | bytes 786440 | tf_op jit(solution)/shard_map/ppermute | solution.py:596
  3.9 11.8 %collective-permute-start.2 = (f32[16,4,8,128]{3,2,1,0:T(8,128)S(1)}, f32[16,4,8,128]{3,2,1,0:T(8,128)S(1)}, u32[]{:S(2)}, u32[]{:S(2)}) collective-permute-start(f32[16,4,8,128]{3,2,1,0:T(8,128)S(1)} %get-tuple-element.38.own), channel_id=1, source_target_pairs={{0,1},{1,2},{2,3},{3,4},{4,5},{5,6},{6,7},{7,0},{8,9},{9,10},{10,1... | collective-permute-start | bytes 786440 | tf_op jit(solution)/shard_map/ppermute | solution.py:595
  3.9 10.6 %collective-permute-start = (f32[13,4,8,128]{3,2,1,0:T(8,128)S(1)}, f32[13,4,8,128]{3,2,1,0:T(8,128)S(1)}, u32[]{:S(2)}, u32[]{:S(2)}) collective-permute-start(f32[13,4,8,128]{3,2,1,0:T(8,128)S(1)} %get-tuple-element.39), channel_id=1, source_target_pairs={{0,8},{8,16},{16,24},{24,32},{32,40},{40,48},{48,56},{56,64},{64,7... | collective-permute-start | bytes 638984 | tf_op jit(solution)/shard_map/ppermute | solution.py:597
  7.4 8.3 %collective-permute-start.1 = (f32[13,4,8,128]{3,2,1,0:T(8,128)S(1)}, f32[13,4,8,128]{3,2,1,0:T(8,128)S(1)}, u32[]{:S(2)}, u32[]{:S(2)}) collective-permute-start(f32[13,4,8,128]{3,2,1,0:T(8,128)S(1)} %get-tuple-element.40), channel_id=1, source_target_pairs={{0,504},{8,0},{16,8},{24,16},{32,24},{40,32},{48,40},{56,48},{64,5... | collective-permute-start | bytes 638984 | tf_op jit(solution)/shard_map/ppermute | solution.py:598
  15.8 7.4 %collective-permute-start.4 = (f32[18,4,8,128]{3,2,1,0:T(8,128)S(1)}, f32[18,4,8,128]{3,2,1,0:T(8,128)S(1)}, u32[]{:S(2)}, u32[]{:S(2)}) collective-permute-start(f32[18,4,8,128]{3,2,1,0:T(8,128)S(1)} %get-tuple-element.45), channel_id=1, source_target_pairs={{0,1},{1,2},{2,3},{3,4},{4,5},{5,6},{6,7},{7,0},{8,9},{9,10},{10,1... | collective-permute-start | bytes 884744 | tf_op jit(solution)/shard_map/ppermute | solution.py:602
  15.8 7.3 %collective-permute-start.5 = (f32[18,4,8,128]{3,2,1,0:T(8,128)S(1)}, f32[18,4,8,128]{3,2,1,0:T(8,128)S(1)}, u32[]{:S(2)}, u32[]{:S(2)}) collective-permute-start(f32[18,4,8,128]{3,2,1,0:T(8,128)S(1)} %get-tuple-element.46), channel_id=1, source_target_pairs={{0,7},{1,0},{2,1},{3,2},{4,3},{5,4},{6,5},{7,6},{8,15},{9,8},{10,9... | collective-permute-start | bytes 884744 | tf_op jit(solution)/shard_map/ppermute | solution.py:603
  45.0 9.1 %collective-permute-start.6 = (f32[30,8,128]{2,1,0:T(8,128)S(1)}, f32[30,8,128]{2,1,0:T(8,128)S(1)}, u32[]{:S(2)}, u32[]{:S(2)}) collective-permute-start(f32[30,8,128]{2,1,0:T(8,128)S(1)} %get-tuple-element.48), channel_id=1, source_target_pairs={{0,32},{32,64},{64,96},{96,128},{128,160},{160,192},{192,224},{224... | collective-permute-start | bytes 368648 | tf_op jit(solution)/shard_map/ppermute | solution.py:616
  51.3 7.0 %collective-permute-start.7 = (f32[30,8,128]{2,1,0:T(8,128)S(1)}, f32[30,8,128]{2,1,0:T(8,128)S(1)}, u32[]{:S(2)}, u32[]{:S(2)}) collective-permute-start(f32[30,8,128]{2,1,0:T(8,128)S(1)} %get-tuple-element.49), channel_id=1, source_target_pairs={{0,480},{32,0},{64,32},{96,64},{128,96},{160,128},{192,160},{224,1... | collective-permute-start | bytes 368648 | tf_op jit(solution)/shard_map/ppermute | solution.py:617

commit v3 on v2

--- a/solution.py
+++ b/solution.py
@@ -25,9 +25,9 @@
     rest = values - high.astype(F32)
     middle = rest.astype(BF16)
     low = (rest - middle.astype(F32)).astype(BF16)
-    out = jnp.dot(high, chooser, preferred_element_type=F32)
-    out = out + jnp.dot(middle, chooser, preferred_element_type=F32)
-    return out + jnp.dot(low, chooser, preferred_element_type=F32)
+    rows = values.shape[0]
+    out = jnp.dot(jnp.concatenate([high, middle, low], axis=0), chooser, preferred_element_type=F32)
+    return out[:rows] + out[rows : 2 * rows] + out[2 * rows :]
 
 
 def chosen_dot(chooser, values):
@@ -143,27 +143,26 @@
     return start + (width - distance if side == 0 else distance - 1)
 
 
-def corner_kernel(below, above, right, left, *, wide):
+def corner_kernel(planes, right, left, *, side, wide):
     index = lax.axis_index("z") * lax.axis_size("y") + lax.axis_index("y")
-    keep = [jnp.where(index > 0, 1.0, 0.0).astype(F32), jnp.where(index < wide - 1, 1.0, 0.0).astype(F32)]
+    inside = index > 0 if side == 0 else index < wide - 1
+    keep = jnp.where(inside, 1.0, 0.0).astype(F32)
     row = iota((8, 128), 0)
-    for side, planes in enumerate((below, above)):
-        for t, (field, one, two, rows) in enumerate(CORNERS):
-            place = side * len(CORNERS) + t
-            for q in range(4):
-                tile = planes[side_index(side, field, one), q]
-                to_right = to_left = tile
-                if two:
-                    other = planes[side_index(side, field, two), q]
-                    to_right = jnp.where(row >= rows, tile, pltpu.roll(other, rows, 0))
-                    to_left = jnp.where(row < 8 - rows, tile, pltpu.roll(other, 8 - rows, 0))
-                if field == 0:
-                    to_right, to_left = to_right * keep[side], to_left * keep[side]
-                right[place, q] = to_right
-                left[place, q] = to_left
-
-
-def down_kernel(own, below, above, own_left, own_right, corner_left, corner_right, packed, x0, b0, fx, fy, fz, dinv, c1, x1, r1, fx1, fy1, fz1, dinv1, diag, first, sums, diag1, first1, b1, parts, *, wide, depth):
+    for t, (field, one, two, rows) in enumerate(CORNERS):
+        for q in range(4):
+            tile = planes[side_index(side, field, one), q]
+            to_right = to_left = tile
+            if two:
+                other = planes[side_index(side, field, two), q]
+                to_right = jnp.where(row >= rows, tile, pltpu.roll(other, rows, 0))
+                to_left = jnp.where(row < 8 - rows, tile, pltpu.roll(other, 8 - rows, 0))
+            if field == 0:
+                to_right, to_left = to_right * keep, to_left * keep
+            right[t, q] = to_right
+            left[t, q] = to_left
+
+
+def down_kernel(own, below, above, own_left, own_right, left_0, right_0, left_1, right_1, packed, x0, b0, fx, fy, fz, dinv, c1, x1, r1, fx1, fy1, fz1, dinv1, diag, first, sums, diag1, first1, b1, parts, *, wide, depth):
     n = lax.axis_index("n")
     index = lax.axis_index("z") * lax.axis_size("y") + lax.axis_index("y")
     keep_wide = [jnp.where(index > 0, 1.0, 0.0).astype(F32), jnp.where(index < wide - 1, 1.0, 0.0).astype(F32)]
@@ -187,8 +186,8 @@
             else:
                 side, distance = (0, -x) if x < 0 else (1, x - 7)
                 t, rows = corner[field, distance]
-                place = side * len(CORNERS) + t
-                parts = [corner_left[place, q], (below, above)[side][side_index(side, field, distance), q], corner_right[place, q]]
+                beside = ((left_0, right_0), (left_1, right_1))[side]
+                parts = [beside[0][t, q], (below, above)[side][side_index(side, field, distance), q], beside[1][t, q]]
                 if rows:
                     parts[0] = pltpu.roll(parts[0], 8 - rows, 0)
                     parts[2] = pltpu.roll(parts[2], rows, 0)
@@ -325,7 +324,7 @@
             down[count + 2 * k + j] = plane[place, j]
 
 
-def middle_kernel(plane, below, above, r1, sent, x2, r2, fx, fy, fz, dinv, r1h, b2, c2, diag, first, *, depth, tall):
+def middle_kernel(plane, below, above, r1, sent, x2, r2, fx, fy, fz, dinv, r1h, b2, c2, diag, first, half, *, depth, tall):
     z, y, n = lax.axis_index("z"), lax.axis_index("y"), lax.axis_index("n")
     size = lax.axis_size("n")
     keep_low = jnp.where(z > 0, 1.0, 0.0).astype(F32)
@@ -388,9 +387,11 @@
     low_half = ones_where(k == zz // 2, 0.125)
     high_half = ones_where(k == zz // 2 + 64, 0.125)
     coarse = dot_exact(jnp.concatenate(totals, axis=0), low_half) + dot_exact(jnp.concatenate(cell_sums, axis=0), high_half)
-    coarse = coarse.reshape(depth, 8, 128)
+    for j in range(depth):
+        half[j // 2, j % 2] = coarse[8 * j : 8 * j + 8]
+    mine = half[n % 2]
     for s in range(tall):
-        sent[s] = coarse
+        sent[s] = mine
 
     for p in range(3, 7):
         for q in range(2):
@@ -447,7 +448,7 @@
     upper = lane >= 64
 
     def unpack(i):
-        one, two = gathered[i], gathered[i + half]
+        one, two = [gathered[j % depth // 2, j // depth, j % 2] for j in (i, i + half)]
         b = jnp.where(upper, pltpu.roll(two, 64, 1), one)
         c3[i + 1, 0] = jnp.where(upper, two, pltpu.roll(one, 64, 1))
         r3[i + 1, 0] = b
@@ -482,7 +483,7 @@
 
     start_norm = spread([r3[i + 1, 0] * r3[i + 1, 0] for i in range(half)])
 
-    def iterate(_, norm):
+    def iterate(norm):
         wrap(p3)
         products = []
         for p in range(1, half + 1):
@@ -503,7 +504,9 @@
             p3[p, 0] = r3[p, 0] + beta * p3[p, 0]
         return new
 
-    lax.fori_loop(0, COARSE_SWEEPS, iterate, start_norm)
+    norm = start_norm
+    for _ in range(COARSE_SWEEPS):
+        norm = iterate(norm)
 
     base = 2 * depth + 2 * y - 4
     tiles = []
@@ -596,16 +599,17 @@
     own_right = lax.ppermute(own, "n", ring(size, -1))
     below = lax.ppermute(up, ("z", "y"), ring(wide, 1))
     above = lax.ppermute(down, ("z", "y"), ring(wide, -1))
-    below, above, own_left, own_right = lax.optimization_barrier((below, above, own_left, own_right))
-    corners = (2 * len(CORNERS), 4, 8, 128)
-    to_right, to_left = call(functools.partial(corner_kernel, wide=wide), [corners] * 2, below, above)
-    corner_left = lax.ppermute(to_right, "n", ring(size, 1))
-    corner_right = lax.ppermute(to_left, "n", ring(size, -1))
+    corners = []
+    for side, planes in enumerate((below, above)):
+        to_right, to_left = call(
+            functools.partial(corner_kernel, side=side, wide=wide), [(len(CORNERS), 4, 8, 128)] * 2, planes
+        )
+        corners += [lax.ppermute(to_right, "n", ring(size, 1)), lax.ppermute(to_left, "n", ring(size, -1))]
     fine, coarse = (24, 4, 24, 128), (10, 2, 16, 128)
     outs = call(
         functools.partial(down_kernel, wide=wide, depth=depth),
         [(group, 3, 8, 128)] + [fine] * 6 + [coarse] * 7,
-        own, below, above, own_left, own_right, corner_left, corner_right,
+        own, below, above, own_left, own_right, *corners,
         scratch=[fine, fine, (18, 2, 32, 128), coarse, coarse, coarse, (4, 2, 8, 128)],
     )
     packed, level_zero = outs[0], outs[1:7]
@@ -618,17 +622,19 @@
     slab = (6 * depth, 2, 8, 128)
     outs = call(
         functools.partial(middle_kernel, depth=depth, tall=tall),
-        [(tall, depth, 8, 128)] + [slab] * 6 + [coarse],
+        [(tall, depth // 2, 8, 128)] + [slab] * 6 + [coarse],
         plane.reshape(group * 24, 128), below.reshape(edge * 8, 128), above.reshape(edge * 8, 128), r1,
-        scratch=[slab, slab, slab, slab],
+        scratch=[slab, slab, slab, slab, (2, depth // 2, 8, 128)],
     )
     sent, level_two, r1h = outs[0], outs[1:7], outs[7]
     gathered = lax.all_to_all(sent, "z", 0, 0)
+    pairs = [[2 * i, 2 * i + 1] for i in range(size // 2)]
+    gathered = lax.all_gather(gathered, "n", axis_index_groups=pairs)
     packed_3 = (wide // 2 + 2, 1, 8, 128)
     (result,) = call(
         functools.partial(up_kernel, depth=depth, tall=tall),
         [(8, 8, 512)],
-        gathered.reshape(wide, 8, 128), r1h, *level_two, c1, x1, *faces_1, *level_zero,
+        gathered, r1h, *level_two, c1, x1, *faces_1, *level_zero,
         scratch=[packed_3] * 9 + [slab] * 3 + [coarse] * 3 + [fine] * 2 + [(64, 512)],
     )
     return result

time: 94.7 us -> 92.6 us (0.978)
  the two profiles are of different devices: /device:TPU:64 before, /device:TPU:1 now
where the time goes in v3:
time: 92.6 us; the launch traced here: 92.3 us
  blocking collectives  40 us (43%)
  starting transfers between devices  32.2 us (35%)
  Pallas kernels  10.1 us (11%)
  waiting for transfers between devices  10 us (11%)
    all_to_all x1, blocking collectives, shards(): gathered = lax.all_to_all(sent, 'z', 0, 0)  19.7 us
    all_to_all x1, blocking collectives, shards(): plane = lax.all_to_all(packed, ('y', 'n'), 0, 0)  14.8 us
    pallas_call x6, Pallas kernels, call(): pl.pallas_call(kernel, out_shape=shapes, in_specs=[pl.BlockSpec(memory_sp...  8.6 us
    ppermute x1, starting transfers between devices, shards(): above = lax.ppermute(down, ('z', 'y'), ring(wide, -1))  8.19 us
    ppermute x2, starting transfers between devices, shards(): lax.ppermute(to_right, 'n', ring(size, 1))  7.28 us
    ppermute x1, starting transfers between devices, shards(): own_right = lax.ppermute(own, 'n', ring(size, -1))  6.89 us
    all_gather x1, blocking collectives, shards(): gathered = lax.all_gather(gathered, 'n', axis_index_groups=pairs)  5.41 us
    ppermute x1, starting transfers between devices, shards(): above = lax.ppermute(down, 'z', ring(tall, -1))  4.57 us
  transfers between devices with their start and end apart: 10, of which 5 were waited for; matrix products, arithmetic and copies ran while one was open for 0% of the time, Pallas kernels for 0%

profile of v3, /device:TPU:1, one launch (start us, length us, event | category | flops | bytes accessed | tf_op | source)
XLA Modules:
  0.0 92.3 jit_solution(8830215596925649988)
XLA Ops:
  0.0 1.5 %shard_map.28 = (f32[16,4,8,128]{3,2,1,0:T(8,128)S(1)}, f32[13,4,8,128]{3,2,1,0:T(8,128)S(1)}, f32[13,4,8,128]{3,2,1,0:T(8,128)S(1)}) custom-call(f32[8,8,512]{2,1,0:T(8,128)} %rhs_hbm.1, f32[8,8,512]{2,1,0:T(8,128)} %beta_hbm.1), custom_call_target="tpu_custom_call" | custom-call | tf_op jit(solution)/shard_map/pallas_call | solution.py:580
  1.5 6.9 %collective-permute-start.3 = (f32[16,4,8,128]{3,2,1,0:T(8,128)S(1)}, f32[16,4,8,128]{3,2,1,0:T(8,128)S(1)}, u32[]{:S(2)}, u32[]{:S(2)}) collective-permute-start(f32[16,4,8,128]{3,2,1,0:T(8,128)S(1)} %get-tuple-element.36.own), channel_id=1, source_target_pairs={{0,7},{1,0},{2,1},{3,2},{4,3},{5,4},{6,5},{7,6},{8,15},{9,8},{10,9... | collective-permute-start | bytes 786440 | tf_op jit(solution)/shard_map/ppermute | solution.py:599
  8.4 8.2 %collective-permute-start.1 = (f32[13,4,8,128]{3,2,1,0:T(8,128)S(1)}, f32[13,4,8,128]{3,2,1,0:T(8,128)S(1)}, u32[]{:S(2)}, u32[]{:S(2)}) collective-permute-start(f32[13,4,8,128]{3,2,1,0:T(8,128)S(1)} %get-tuple-element.38), channel_id=1, source_target_pairs={{0,504},{8,0},{16,8},{24,16},{32,24},{40,32},{48,40},{56,48},{64,5... | collective-permute-start | bytes 638984 | tf_op jit(solution)/shard_map/ppermute | solution.py:601
  16.6 1.9 %collective-permute-start = (f32[13,4,8,128]{3,2,1,0:T(8,128)S(1)}, f32[13,4,8,128]{3,2,1,0:T(8,128)S(1)}, u32[]{:S(2)}, u32[]{:S(2)}) collective-permute-start(f32[13,4,8,128]{3,2,1,0:T(8,128)S(1)} %get-tuple-element.37), channel_id=1, source_target_pairs={{0,8},{8,16},{16,24},{24,32},{32,40},{40,48},{48,56},{56,64},{64,7... | collective-permute-start | bytes 638984 | tf_op jit(solution)/shard_map/ppermute | solution.py:600
  18.5 1.4 %collective-permute-start.2 = (f32[16,4,8,128]{3,2,1,0:T(8,128)S(1)}, f32[16,4,8,128]{3,2,1,0:T(8,128)S(1)}, u32[]{:S(2)}, u32[]{:S(2)}) collective-permute-start(f32[16,4,8,128]{3,2,1,0:T(8,128)S(1)} %get-tuple-element.36.own), channel_id=1, source_target_pairs={{0,1},{1,2},{2,3},{3,4},{4,5},{5,6},{6,7},{7,0},{8,9},{9,10},{10,1... | collective-permute-start | bytes 786440 | tf_op jit(solution)/shard_map/ppermute | solution.py:598
  19.9 0.0 collective-permute-done.1.planes.above
  19.9 3.2 %collective-permute-start.6 = (f32[9,4,8,128]{3,2,1,0:T(8,128)S(1)}, f32[9,4,8,128]{3,2,1,0:T(8,128)S(1)}, u32[]{:S(2)}, u32[]{:S(2)}) collective-permute-start(f32[9,4,8,128]{3,2,1,0:T(8,128)S(1)} %get-tuple-element.41), channel_id=1, source_target_pairs={{0,1},{1,2},{2,3},{3,4},{4,5},{5,6},{6,7},{7,0},{8,9},{9,10},{10,1... | collective-permute-start | bytes 442376 | tf_op jit(solution)/shard_map/ppermute | solution.py:607
  23.1 0.0 collective-permute-start.7
  23.1 3.3 %collective-permute-done.planes.below = f32[13,4,8,128]{3,2,1,0:T(8,128)S(1)} collective-permute-done((f32[13,4,8,128]{3,2,1,0:T(8,128)S(1)}, f32[13,4,8,128]{3,2,1,0:T(8,128)S(1)}, u32[]{:S(2)}, u32[]{:S(2)}) %collective-permute-start) | collective-permute-done | bytes 213024 | tf_op jit(solution)/shard_map/ppermute | solution.py:600
  26.5 4.1 %collective-permute-start.4 = (f32[9,4,8,128]{3,2,1,0:T(8,128)S(1)}, f32[9,4,8,128]{3,2,1,0:T(8,128)S(1)}, u32[]{:S(2)}, u32[]{:S(2)}) collective-permute-start(f32[9,4,8,128]{3,2,1,0:T(8,128)S(1)} %get-tuple-element.39), channel_id=1, source_target_pairs={{0,1},{1,2},{2,3},{3,4},{4,5},{5,6},{6,7},{7,0},{8,9},{9,10},{10,1... | collective-permute-start | bytes 442376 | tf_op jit(solution)/shard_map/ppermute | solution.py:607
  30.6 0.0 collective-permute-done.3.own_right
  30.6 0.0 collective-permute-start.5
  30.6 0.0 collective-permute-done.2.own_left
  30.6 0.0 collective-permute-done.6.left_1
  30.6 0.0 collective-permute-done.7.right_1
  30.6 2.1 %collective-permute-done.4.left_0 = f32[9,4,8,128]{3,2,1,0:T(8,128)S(1)} collective-permute-done((f32[9,4,8,128]{3,2,1,0:T(8,128)S(1)}, f32[9,4,8,128]{3,2,1,0:T(8,128)S(1)}, u32[]{:S(2)}, u32[]{:S(2)}) %collective-permute-start.4) | collective-permute-done | bytes 147488 | tf_op jit(solution)/shard_map/ppermute | solution.py:607
  32.7 2.8 %collective-permute-done.5.right_0 = f32[9,4,8,128]{3,2,1,0:T(8,128)S(1)} collective-permute-done((f32[9,4,8,128]{3,2,1,0:T(8,128)S(1)}, f32[9,4,8,128]{3,2,1,0:T(8,128)S(1)}, u32[]{:S(2)}, u32[]{:S(2)}) %collective-permute-start.5) | collective-permute-done | bytes 147488 | tf_op jit(solution)/shard_map/ppermute | solution.py:607
  35.4 2.6 %shard_map.31 = (f32[32,3,8,128]{3,2,1,0:T(8,128)S(1)}, f32[24,4,24,128]{3,2,1,0:T(8,128)S(1)}, f32[24,4,24,128]{3,2,1,0:T(8,128)S(1)}, f32[24,4,24,128]{3,2,1,0...) custom-call(f32[16,4,8,128]{3,2,1,0:T(8,128)S(1)} %get-tuple-element, ...), custom_call_target="tpu_custom_call" | custom-call | tf_op jit(solution)/shard_map/pallas_call | solution.py:568
  38.1 14.8 %all_to_all.10.plane = f32[32,3,8,128]{3,2,1,0:T(8,128)S(1)} all-to-all(f32[32,3,8,128]{3,2,1,0:T(8,128)S(1)} %get-tuple-element.43), channel_id=1, replica_groups=mesh['z'=16,'y'=4,'n'=8] {'y','n'}, dimensions={0} | all-to-all | bytes 786432 | tf_op jit(solution)/shard_map/all_to_all | solution.py:617
  52.9 1.9 %collective-permute-start.8 = (f32[30,8,128]{2,1,0:T(8,128)S(1)}, f32[30,8,128]{2,1,0:T(8,128)S(1)}, u32[]{:S(2)}, u32[]{:S(2)}) collective-permute-start(f32[30,8,128]{2,1,0:T(8,128)S(1)} %get-tuple-element.44), channel_id=1, source_target_pairs={{0,32},{32,64},{64,96},{96,128},{128,160},{160,192},{192,224},{224... | collective-permute-start | bytes 368648 | tf_op jit(solution)/shard_map/ppermute | solution.py:620
  54.9 4.6 %collective-permute-start.9 = (f32[30,8,128]{2,1,0:T(8,128)S(1)}, f32[30,8,128]{2,1,0:T(8,128)S(1)}, u32[]{:S(2)}, u32[]{:S(2)}) collective-permute-start(f32[30,8,128]{2,1,0:T(8,128)S(1)} %get-tuple-element.45), channel_id=1, source_target_pairs={{0,480},{32,0},{64,32},{96,64},{128,96},{160,128},{192,160},{224,1... | collective-permute-start | bytes 368648 | tf_op jit(solution)/shard_map/ppermute | solution.py:621
  59.5 1.1 %collective-permute-done.8 = f32[30,8,128]{2,1,0:T(8,128)S(1)} collective-permute-done((f32[30,8,128]{2,1,0:T(8,128)S(1)}, f32[30,8,128]{2,1,0:T(8,128)S(1)}, u32[]{:S(2)}, u32[]{:S(2)}) %collective-permute-start.8) | collective-permute-done | bytes 122912 | tf_op jit(solution)/shard_map/ppermute | solution.py:620
  60.6 0.7 collective-permute-done.9
  61.3 0.6 shard_map.33
  61.9 19.7 %all_to_all.11 = f32[16,2,8,128]{3,2,1,0:T(8,128)S(1)} all-to-all(f32[16,2,8,128]{3,2,1,0:T(8,128)S(1)} %get-tuple-element.47), channel_id=1, replica_groups=mesh['z'=16,'y'=4,'n'=8] {'z'}, dimensions={0} | all-to-all | bytes 262144 | tf_op jit(solution)/shard_map/all_to_all | solution.py:630
  81.6 5.4 %all-gather = f32[32,2,8,128]{3,2,1,0:T(8,128)S(1)} all-gather(f32[16,2,8,128]{3,2,1,0:T(8,128)S(1)} %all_to_all.11), channel_id=2, replica_groups={{0,1},{2,3},{4,5},{6,7},{8,9},{10,11},{12,13},{14,15},{16,17},{18,19},{..., dimensions={0}, use_global_device_ids=true | all-gather | bytes 393216 | tf_op jit(solution)/shard_map/all_gather | solution.py:632
  87.0 5.3 %shard_map.34 = f32[8,8,512]{2,1,0:T(8,128)} custom-call(f32[2,16,2,8,128]{4,3,2,1,0:T(8,128)S(1)} %bitcast.5, f32[10,2,16,128]{3,2,1,0:T(8,128)S(1)} %get-tuple-element.48.r1h, f32[24,2,8,128]{3,2,1,0:T(8,128)S(1)} %get-tuple-element.49.x2, f32[24,2,8,128]{3,2,1,0:T(8,128)S(1)} %get-tuple-element.50.r2, f32[24,2,8,128]{3,2,1,0:T(8,128)S(1)} %get-tuple-element.51.fx2, ...), custom_call_target="tpu_custom_call" | custom-call | tf_op jit(solution)/shard_map/pallas_call | solution.py:568
  (3 shorter events, 0.1 us)
Async XLA Ops:
  1.5 29.1 %collective-permute-start.3 = (f32[16,4,8,128]{3,2,1,0:T(8,128)S(1)}, f32[16,4,8,128]{3,2,1,0:T(8,128)S(1)}, u32[]{:S(2)}, u32[]{:S(2)}) collective-permute-start(f32[16,4,8,128]{3,2,1,0:T(8,128)S(1)} %get-tuple-element.36.own), channel_id=1, source_target_pairs={{0,7},{1,0},{2,1},{3,2},{4,3},{5,4},{6,5},{7,6},{8,15},{9,8},{10,9... | collective-permute-start | bytes 786440 | tf_op jit(solution)/shard_map/ppermute | solution.py:599
  8.4 11.5 %collective-permute-start.1 = (f32[13,4,8,128]{3,2,1,0:T(8,128)S(1)}, f32[13,4,8,128]{3,2,1,0:T(8,128)S(1)}, u32[]{:S(2)}, u32[]{:S(2)}) collective-permute-start(f32[13,4,8,128]{3,2,1,0:T(8,128)S(1)} %get-tuple-element.38), channel_id=1, source_target_pairs={{0,504},{8,0},{16,8},{24,16},{32,24},{40,32},{48,40},{56,48},{64,5... | collective-permute-start | bytes 638984 | tf_op jit(solution)/shard_map/ppermute | solution.py:601
  16.6 9.9 %collective-permute-start = (f32[13,4,8,128]{3,2,1,0:T(8,128)S(1)}, f32[13,4,8,128]{3,2,1,0:T(8,128)S(1)}, u32[]{:S(2)}, u32[]{:S(2)}) collective-permute-start(f32[13,4,8,128]{3,2,1,0:T(8,128)S(1)} %get-tuple-element.37), channel_id=1, source_target_pairs={{0,8},{8,16},{16,24},{24,32},{32,40},{40,48},{48,56},{56,64},{64,7... | collective-permute-start | bytes 638984 | tf_op jit(solution)/shard_map/ppermute | solution.py:600
  18.5 12.1 %collective-permute-start.2 = (f32[16,4,8,128]{3,2,1,0:T(8,128)S(1)}, f32[16,4,8,128]{3,2,1,0:T(8,128)S(1)}, u32[]{:S(2)}, u32[]{:S(2)}) collective-permute-start(f32[16,4,8,128]{3,2,1,0:T(8,128)S(1)} %get-tuple-element.36.own), channel_id=1, source_target_pairs={{0,1},{1,2},{2,3},{3,4},{4,5},{5,6},{6,7},{7,0},{8,9},{9,10},{10,1... | collective-permute-start | bytes 786440 | tf_op jit(solution)/shard_map/ppermute | solution.py:598
  19.9 10.7 %collective-permute-start.6 = (f32[9,4,8,128]{3,2,1,0:T(8,128)S(1)}, f32[9,4,8,128]{3,2,1,0:T(8,128)S(1)}, u32[]{:S(2)}, u32[]{:S(2)}) collective-permute-start(f32[9,4,8,128]{3,2,1,0:T(8,128)S(1)} %get-tuple-element.41), channel_id=1, source_target_pairs={{0,1},{1,2},{2,3},{3,4},{4,5},{5,6},{6,7},{7,0},{8,9},{9,10},{10,1... | collective-permute-start | bytes 442376 | tf_op jit(solution)/shard_map/ppermute | solution.py:607
  23.1 7.5 %collective-permute-start.7 = (f32[9,4,8,128]{3,2,1,0:T(8,128)S(1)}, f32[9,4,8,128]{3,2,1,0:T(8,128)S(1)}, u32[]{:S(2)}, u32[]{:S(2)}) collective-permute-start(f32[9,4,8,128]{3,2,1,0:T(8,128)S(1)} %get-tuple-element.42), channel_id=1, source_target_pairs={{0,7},{1,0},{2,1},{3,2},{4,3},{5,4},{6,5},{7,6},{8,15},{9,8},{10,9... | collective-permute-start | bytes 442376 | tf_op jit(solution)/shard_map/ppermute | solution.py:607
  26.5 6.2 %collective-permute-start.4 = (f32[9,4,8,128]{3,2,1,0:T(8,128)S(1)}, f32[9,4,8,128]{3,2,1,0:T(8,128)S(1)}, u32[]{:S(2)}, u32[]{:S(2)}) collective-permute-start(f32[9,4,8,128]{3,2,1,0:T(8,128)S(1)} %get-tuple-element.39), channel_id=1, source_target_pairs={{0,1},{1,2},{2,3},{3,4},{4,5},{5,6},{6,7},{7,0},{8,9},{9,10},{10,1... | collective-permute-start | bytes 442376 | tf_op jit(solution)/shard_map/ppermute | solution.py:607
  30.6 4.9 %collective-permute-start.5 = (f32[9,4,8,128]{3,2,1,0:T(8,128)S(1)}, f32[9,4,8,128]{3,2,1,0:T(8,128)S(1)}, u32[]{:S(2)}, u32[]{:S(2)}) collective-permute-start(f32[9,4,8,128]{3,2,1,0:T(8,128)S(1)} %get-tuple-element.40), channel_id=1, source_target_pairs={{0,7},{1,0},{2,1},{3,2},{4,3},{5,4},{6,5},{7,6},{8,15},{9,8},{10,9... | collective-permute-start | bytes 442376 | tf_op jit(solution)/shard_map/ppermute | solution.py:607
  52.9 7.6 %collective-permute-start.8 = (f32[30,8,128]{2,1,0:T(8,128)S(1)}, f32[30,8,128]{2,1,0:T(8,128)S(1)}, u32[]{:S(2)}, u32[]{:S(2)}) collective-permute-start(f32[30,8,128]{2,1,0:T(8,128)S(1)} %get-tuple-element.44), channel_id=1, source_target_pairs={{0,32},{32,64},{64,96},{96,128},{128,160},{160,192},{192,224},{224... | collective-permute-start | bytes 368648 | tf_op jit(solution)/shard_map/ppermute | solution.py:620
  54.9 6.4 %collective-permute-start.9 = (f32[30,8,128]{2,1,0:T(8,128)S(1)}, f32[30,8,128]{2,1,0:T(8,128)S(1)}, u32[]{:S(2)}, u32[]{:S(2)}) collective-permute-start(f32[30,8,128]{2,1,0:T(8,128)S(1)} %get-tuple-element.45), channel_id=1, source_target_pairs={{0,480},{32,0},{64,32},{96,64},{128,96},{160,128},{192,160},{224,1... | collective-permute-start | bytes 368648 | tf_op jit(solution)/shard_map/ppermute | solution.py:621

commit v4 on v3

--- a/solution.py
+++ b/solution.py
@@ -113,59 +113,51 @@
 )
 
 
-def split_kernel(rhs_hbm, beta_hbm, own, up, down, rhs, beta, sems):
+def split_kernel(rhs_hbm, beta_hbm, own, pair, other, rhs, beta, sems):
     copies = [
         pltpu.make_async_copy(beta_hbm, beta, sems.at[0]),
         pltpu.make_async_copy(rhs_hbm, rhs, sems.at[1]),
     ]
     for copy in copies:
         copy.start()
+    even = lax.axis_index("y") % 2 == 0
     z = iota((512, 512), 0)
     k = iota((512, 512), 1)
     chooser = ones_where(z == 4 * (k % 128) + k // 128)
     for field, source in enumerate((beta, rhs)):
         copies[field].wait()
         out = dot_exact(source[...].reshape(64, 512), chooser)
-        for x in range(8):
-            for q in range(4):
-                tile = out[8 * x : 8 * x + 8, 128 * q : 128 * q + 128]
-                own[8 * field + x, q] = tile
-                width = (C_LOW, B_LOW)[field]
-                start = (0, C_LOW)[field]
-                if x >= 8 - width:
-                    up[start + x - (8 - width), q] = tile
-                if x < width:
-                    down[start + x, q] = tile
-
-
-def side_index(side, field, distance):
-    width, start = (C_LOW, B_LOW)[field], (0, C_LOW)[field]
-    return start + (width - distance if side == 0 else distance - 1)
-
-
-def corner_kernel(planes, right, left, *, side, wide):
-    index = lax.axis_index("z") * lax.axis_size("y") + lax.axis_index("y")
-    inside = index > 0 if side == 0 else index < wide - 1
-    keep = jnp.where(inside, 1.0, 0.0).astype(F32)
+        width, start = (C_LOW, B_LOW)[field], (0, C_LOW)[field]
+        for q in range(4):
+            tiles = [out[8 * x : 8 * x + 8, 128 * q : 128 * q + 128] for x in range(8)]
+            for x in range(8):
+                own[8 * field + x, q] = tiles[x]
+            for d in range(width):
+                pair[start + d, q] = jnp.where(even, tiles[7 - d], tiles[d])
+                other[start + d, q] = jnp.where(even, tiles[d], tiles[7 - d])
+
+
+def place_of(field, distance):
+    return (0, C_LOW)[field] + distance - 1
+
+
+def corner_kernel(planes, right, left):
     row = iota((8, 128), 0)
     for t, (field, one, two, rows) in enumerate(CORNERS):
         for q in range(4):
-            tile = planes[side_index(side, field, one), q]
+            tile = planes[place_of(field, one), q]
             to_right = to_left = tile
             if two:
-                other = planes[side_index(side, field, two), q]
-                to_right = jnp.where(row >= rows, tile, pltpu.roll(other, rows, 0))
-                to_left = jnp.where(row < 8 - rows, tile, pltpu.roll(other, 8 - rows, 0))
-            if field == 0:
-                to_right, to_left = to_right * keep, to_left * keep
+                beside = planes[place_of(field, two), q]
+                to_right = jnp.where(row >= rows, tile, pltpu.roll(beside, rows, 0))
+                to_left = jnp.where(row < 8 - rows, tile, pltpu.roll(beside, 8 - rows, 0))
             right[t, q] = to_right
             left[t, q] = to_left
 
 
-def down_kernel(own, below, above, own_left, own_right, left_0, right_0, left_1, right_1, packed, x0, b0, fx, fy, fz, dinv, c1, x1, r1, fx1, fy1, fz1, dinv1, diag, first, sums, diag1, first1, b1, parts, *, wide, depth):
+def down_kernel(own, pair, other, own_left, own_right, left_pair, right_pair, left_other, right_other, packed, x0, b0, fx, fy, fz, dinv, c1, x1, r1, fx1, fy1, fz1, dinv1, diag, first, sums, diag1, first1, b1, parts, *, depth):
     n = lax.axis_index("n")
-    index = lax.axis_index("z") * lax.axis_size("y") + lax.axis_index("y")
-    keep_wide = [jnp.where(index > 0, 1.0, 0.0).astype(F32), jnp.where(index < wide - 1, 1.0, 0.0).astype(F32)]
+    even = lax.axis_index("y") % 2 == 0
     keep_left = jnp.where(n > 0, 1.0, 0.0).astype(F32)
     keep_right = jnp.where(n < lax.axis_size("n") - 1, 1.0, 0.0).astype(F32)
     lane = iota((24, 128), 1)
@@ -176,6 +168,9 @@
         corner[field, one] = (t, 0)
         if two:
             corner[field, two] = (t, rows)
+
+    def from_side(side, of_pair, of_other):
+        return jnp.where(even, of_other, of_pair) if side == 0 else jnp.where(even, of_pair, of_other)
 
     def plane(field, p, keep_0, keep_1):
         x = p - 8
@@ -186,13 +181,15 @@
             else:
                 side, distance = (0, -x) if x < 0 else (1, x - 7)
                 t, rows = corner[field, distance]
-                beside = ((left_0, right_0), (left_1, right_1))[side]
-                parts = [beside[0][t, q], (below, above)[side][side_index(side, field, distance), q], beside[1][t, q]]
+                at = place_of(field, distance)
+                parts = [
+                    from_side(side, left_pair[t, q], left_other[t, q]),
+                    from_side(side, pair[at, q], other[at, q]),
+                    from_side(side, right_pair[t, q], right_other[t, q]),
+                ]
                 if rows:
                     parts[0] = pltpu.roll(parts[0], 8 - rows, 0)
                     parts[2] = pltpu.roll(parts[2], rows, 0)
-                if field == 0:
-                    parts[1] = parts[1] * keep_wide[side]
             out.append(jnp.concatenate([parts[0] * keep_0, parts[1], parts[2] * keep_1] if field == 0 else parts, axis=0))
         return out
 
@@ -309,26 +306,35 @@
             packed[s, 2] = level_two
 
 
-def edge_kernel(plane, up, down, *, depth):
+def edge_kernel(plane, other, pair, *, depth):
     n = lax.axis_index("n")
+    even = lax.axis_index("z") % 2 == 0
     size = lax.axis_size("n")
 
     count = (depth - 1) * size
+    def send(s, up, down):
+        pair[s] = jnp.where(even, up, down)
+        other[s] = jnp.where(even, down, up)
+
     for s in range(count):
-        up[s] = plane[size + s, 2]
-        down[s] = plane[s, 2]
+        send(s, plane[size + s, 2], plane[s, 2])
     for k in range(3):
         place = jnp.clip(n + (k - 1), 0, size - 1)
         for j in range(2):
-            up[count + 2 * k + j] = plane[count + place, j]
-            down[count + 2 * k + j] = plane[place, j]
-
-
-def middle_kernel(plane, below, above, r1, sent, x2, r2, fx, fy, fz, dinv, r1h, b2, c2, diag, first, half, *, depth, tall):
+            send(count + 2 * k + j, plane[count + place, j], plane[place, j])
+
+
+def middle_kernel(plane, other, pair, r1, sent, x2, r2, fx, fy, fz, dinv, r1h, b2, c2, diag, first, half, *, depth, tall):
     z, y, n = lax.axis_index("z"), lax.axis_index("y"), lax.axis_index("n")
     size = lax.axis_size("n")
-    keep_low = jnp.where(z > 0, 1.0, 0.0).astype(F32)
-    keep_high = jnp.where(z < tall - 1, 1.0, 0.0).astype(F32)
+    even = z % 2 == 0
+
+    def below(rows):
+        return jnp.where(even, other[rows, :], pair[rows, :])
+
+    def above(rows):
+        return jnp.where(even, pair[rows, :], other[rows, :])
+
     width = 2 * depth
     for yb in range(depth):
         for x in range(2):
@@ -340,12 +346,12 @@
                 c2[width + place, yy] = plane[pl.ds(own + 4, 8, stride=24), :]
                 if yb > 0:
                     edge = (yb - 1) * size * 8 + r
-                    b2[place, yy] = below[pl.ds(edge, 8, stride=8), :]
-                    c2[place, yy] = below[pl.ds(edge + 4, 8, stride=8), :] * keep_low
+                    b2[place, yy] = below(pl.ds(edge, 8, stride=8))
+                    c2[place, yy] = below(pl.ds(edge + 4, 8, stride=8))
                 if yb < depth - 1:
                     edge = yb * size * 8 + r
-                    b2[2 * width + place, yy] = above[pl.ds(edge, 8, stride=8), :]
-                    c2[2 * width + place, yy] = above[pl.ds(edge + 4, 8, stride=8), :] * keep_high
+                    b2[2 * width + place, yy] = above(pl.ds(edge, 8, stride=8))
+                    c2[2 * width + place, yy] = above(pl.ds(edge + 4, 8, stride=8))
 
     scale = 0.5 / 16.0
     shape = (8, 128)
@@ -406,8 +412,8 @@
 
         for j in range(2):
             start = edges + 8 * (2 * k + j)
-            low = jnp.where(y == 0, below[start : start + 8], block(jnp.maximum(y - 1, 0), j))
-            high = jnp.where(y == depth - 1, above[start : start + 8], block(jnp.minimum(y + 1, depth - 1), j))
+            low = jnp.where(y == 0, below(pl.ds(start, 8)), block(jnp.maximum(y - 1, 0), j))
+            high = jnp.where(y == depth - 1, above(pl.ds(start, 8)), block(jnp.minimum(y + 1, depth - 1), j))
             for q in range(2):
                 r1h[1 + j, q, 4 * k : 4 * k + 4] = low[4 * q : 4 * q + 4]
                 r1h[7 + j, q, 4 * k : 4 * k + 4] = high[4 * q : 4 * q + 4]
@@ -591,45 +597,51 @@
     return [(i, (i + step) % axis_size) for i in range(axis_size)]
 
 
+def pairs(axis_size):
+    return [(i, i ^ 1) for i in range(axis_size)]
+
+
+def others(axis_size):
+    return [(i, ((i + 1) ^ 1) - 1) for i in range(1, axis_size - 1)]
+
+
 def shards(rhs_field, beta_cells):
     tall, depth, size = lax.axis_size("z"), lax.axis_size("y"), lax.axis_size("n")
     wide, group = tall * depth, depth * size
-    own, up, down = split(rhs_field, beta_cells)
+    own, to_pair, to_other = split(rhs_field, beta_cells)
     own_left = lax.ppermute(own, "n", ring(size, 1))
     own_right = lax.ppermute(own, "n", ring(size, -1))
-    below = lax.ppermute(up, ("z", "y"), ring(wide, 1))
-    above = lax.ppermute(down, ("z", "y"), ring(wide, -1))
+    other = lax.ppermute(to_other, ("z", "y"), others(wide))
+    pair = lax.ppermute(to_pair, ("z", "y"), pairs(wide))
     corners = []
-    for side, planes in enumerate((below, above)):
-        to_right, to_left = call(
-            functools.partial(corner_kernel, side=side, wide=wide), [(len(CORNERS), 4, 8, 128)] * 2, planes
-        )
+    for planes in (pair, other):
+        to_right, to_left = call(corner_kernel, [(len(CORNERS), 4, 8, 128)] * 2, planes)
         corners += [lax.ppermute(to_right, "n", ring(size, 1)), lax.ppermute(to_left, "n", ring(size, -1))]
     fine, coarse = (24, 4, 24, 128), (10, 2, 16, 128)
     outs = call(
-        functools.partial(down_kernel, wide=wide, depth=depth),
+        functools.partial(down_kernel, depth=depth),
         [(group, 3, 8, 128)] + [fine] * 6 + [coarse] * 7,
-        own, below, above, own_left, own_right, *corners,
+        own, pair, other, own_left, own_right, *corners,
         scratch=[fine, fine, (18, 2, 32, 128), coarse, coarse, coarse, (4, 2, 8, 128)],
     )
     packed, level_zero = outs[0], outs[1:7]
     c1, x1, r1, *faces_1 = outs[7:14]
     plane = lax.all_to_all(packed, ("y", "n"), 0, 0)
     edge = group - size + 6
-    up, down = call(functools.partial(edge_kernel, depth=depth), [(edge, 8, 128)] * 2, plane)
-    below = lax.ppermute(up, "z", ring(tall, 1))
-    above = lax.ppermute(down, "z", ring(tall, -1))
+    to_other, to_pair = call(functools.partial(edge_kernel, depth=depth), [(edge, 8, 128)] * 2, plane)
+    other = lax.ppermute(to_other, "z", others(tall))
+    pair = lax.ppermute(to_pair, "z", pairs(tall))
     slab = (6 * depth, 2, 8, 128)
     outs = call(
         functools.partial(middle_kernel, depth=depth, tall=tall),
         [(tall, depth // 2, 8, 128)] + [slab] * 6 + [coarse],
-        plane.reshape(group * 24, 128), below.reshape(edge * 8, 128), above.reshape(edge * 8, 128), r1,
+        plane.reshape(group * 24, 128), other.reshape(edge * 8, 128), pair.reshape(edge * 8, 128), r1,
         scratch=[slab, slab, slab, slab, (2, depth // 2, 8, 128)],
     )
     sent, level_two, r1h = outs[0], outs[1:7], outs[7]
     gathered = lax.all_to_all(sent, "z", 0, 0)
-    pairs = [[2 * i, 2 * i + 1] for i in range(size // 2)]
-    gathered = lax.all_gather(gathered, "n", axis_index_groups=pairs)
+    cores = [[2 * i, 2 * i + 1] for i in range(size // 2)]
+    gathered = lax.all_gather(gathered, "n", axis_index_groups=cores)
     packed_3 = (wide // 2 + 2, 1, 8, 128)
     (result,) = call(
         functools.partial(up_kernel, depth=depth, tall=tall),

time: 92.6 us -> 90.7 us (0.979)
  starting transfers between devices: 32.2 us -> 18.7 us
  blocking collectives: 40 us -> 48.9 us
  waiting for transfers between devices: 10 us -> 12.6 us
    ppermute x2, starting transfers between devices: 7.28 us -> 0.05 us  [shards(): lax.ppermute(to_right, 'n', ring(size, 1))]
    ppermute x4, starting transfers between devices: 16.6 us -> 9.68 us  [the longest x1 6.42 us: shards(): pair = lax.ppermute(to_pair, 'z', pairs(tall))]
    all_to_all x1, blocking collectives: 19.7 us -> 25.6 us  [shards(): gathered = lax.all_to_all(sent, 'z', 0, 0)]
    ppermute x4, waiting for transfers between devices: 5.18 us -> 8.58 us  [the longest x1 5.53 us: shards(): pair = lax.ppermute(to_pair, ('z', 'y'), pairs(wide))]
    all_to_all x1, blocking collectives: 14.8 us -> 17.9 us  [shards(): plane = lax.all_to_all(packed, ('y', 'n'), 0, 0)]
    ppermute x2, starting transfers between devices: 0.01 us -> 1.91 us  [shards(): lax.ppermute(to_left, 'n', ring(size, -1))]
    ppermute x1, starting transfers between devices: 1.41 us -> 0.14 us  [shards(): own_left = lax.ppermute(own, 'n', ring(size, 1))]
  transfers between devices with their start and end apart: 10 -> 10, of which waited for: 5 -> 4; matrix products, arithmetic and copies ran while one was open for 0% -> 0% of each run, Pallas kernels for 0% -> 0%
where the time goes in v4:
time: 90.7 us; the launch traced here: 90.5 us
  blocking collectives  48.9 us (54%)
  starting transfers between devices  18.7 us (21%)
  waiting for transfers between devices  12.6 us (14%)
  Pallas kernels  10.1 us (11%)
    all_to_all x1, blocking collectives, shards(): gathered = lax.all_to_all(sent, 'z', 0, 0)  25.6 us
    all_to_all x1, blocking collectives, shards(): plane = lax.all_to_all(packed, ('y', 'n'), 0, 0)  17.9 us
    pallas_call x6, Pallas kernels, call(): pl.pallas_call(kernel, out_shape=shapes, in_specs=[pl.BlockSpec(memory_sp...  8.66 us
    ppermute x1, starting transfers between devices, shards(): own_right = lax.ppermute(own, 'n', ring(size, -1))  6.89 us
    ppermute x1, starting transfers between devices, shards(): pair = lax.ppermute(to_pair, 'z', pairs(tall))  6.42 us
    ppermute x1, waiting for transfers between devices, shards(): pair = lax.ppermute(to_pair, ('z', 'y'), pairs(wide))  5.53 us
    all_gather x1, blocking collectives, shards(): gathered = lax.all_gather(gathered, 'n', axis_index_groups=cores)  5.4 us
    ppermute x1, waiting for transfers between devices, shards(): pair = lax.ppermute(to_pair, 'z', pairs(tall))  3.05 us
  transfers between devices with their start and end apart: 10, of which 4 were waited for; matrix products, arithmetic and copies ran while one was open for 0% of the time, Pallas kernels for 0%

profile of v4, /device:TPU:1, one launch (start us, length us, event | category | flops | bytes accessed | tf_op | source)
XLA Modules:
  0.0 90.5 jit_solution(7048248807996616067)
XLA Ops:
  0.0 1.5 %shard_map.28 = (f32[16,4,8,128]{3,2,1,0:T(8,128)S(1)}, f32[13,4,8,128]{3,2,1,0:T(8,128)S(1)}, f32[13,4,8,128]{3,2,1,0:T(8,128)S(1)}) custom-call(f32[8,8,512]{2,1,0:T(8,128)} %rhs_hbm.1, f32[8,8,512]{2,1,0:T(8,128)} %beta_hbm.1), custom_call_target="tpu_custom_call" | custom-call | tf_op jit(solution)/shard_map/pallas_call | solution.py:586
  1.5 6.9 %collective-permute-start.3 = (f32[16,4,8,128]{3,2,1,0:T(8,128)S(1)}, f32[16,4,8,128]{3,2,1,0:T(8,128)S(1)}, u32[]{:S(2)}, u32[]{:S(2)}) collective-permute-start(f32[16,4,8,128]{3,2,1,0:T(8,128)S(1)} %get-tuple-element.36.own), channel_id=1, source_target_pairs={{0,7},{1,0},{2,1},{3,2},{4,3},{5,4},{6,5},{7,6},{8,15},{9,8},{10,9... | collective-permute-start | bytes 786440 | tf_op jit(solution)/shard_map/ppermute | solution.py:613
  8.4 0.7 collective-permute-start.1
  9.0 1.9 %collective-permute-start = (f32[13,4,8,128]{3,2,1,0:T(8,128)S(1)}, f32[13,4,8,128]{3,2,1,0:T(8,128)S(1)}, u32[]{:S(2)}, u32[]{:S(2)}) collective-permute-start(f32[13,4,8,128]{3,2,1,0:T(8,128)S(1)} %get-tuple-element.37), channel_id=1, source_target_pairs={{0,8},{8,0},{16,24},{24,16},{32,40},{40,32},{48,56},{56,48},{64,72... | collective-permute-start | bytes 638984 | tf_op jit(solution)/shard_map/ppermute | solution.py:615
  11.0 0.1 collective-permute-start.2
  11.1 0.0 collective-permute-done.1.planes.other
  11.1 0.0 collective-permute-start.6
  11.2 1.1 %collective-permute-start.7 = (f32[9,4,8,128]{3,2,1,0:T(8,128)S(1)}, f32[9,4,8,128]{3,2,1,0:T(8,128)S(1)}, u32[]{:S(2)}, u32[]{:S(2)}) collective-permute-start(f32[9,4,8,128]{3,2,1,0:T(8,128)S(1)} %get-tuple-element.42), channel_id=1, source_target_pairs={{0,7},{1,0},{2,1},{3,2},{4,3},{5,4},{6,5},{7,6},{8,15},{9,8},{10,9... | collective-permute-start | bytes 442376 | tf_op jit(solution)/shard_map/ppermute | solution.py:619
  12.3 5.5 %collective-permute-done.planes.pair = f32[13,4,8,128]{3,2,1,0:T(8,128)S(1)} collective-permute-done((f32[13,4,8,128]{3,2,1,0:T(8,128)S(1)}, f32[13,4,8,128]{3,2,1,0:T(8,128)S(1)}, u32[]{:S(2)}, u32[]{:S(2)}) %collective-permute-start) | collective-permute-done | bytes 213024 | tf_op jit(solution)/shard_map/ppermute | solution.py:615
  17.8 0.0 collective-permute-start.4
  17.8 0.0 collective-permute-done.3.own_right
  17.9 0.8 collective-permute-start.5
  18.7 0.0 collective-permute-done.2.own_left
  18.7 0.0 collective-permute-done.6.left_other
  18.7 0.0 collective-permute-done.7.right_other
  18.7 1.3 %collective-permute-done.4.left_pair = f32[9,4,8,128]{3,2,1,0:T(8,128)S(1)} collective-permute-done((f32[9,4,8,128]{3,2,1,0:T(8,128)S(1)}, f32[9,4,8,128]{3,2,1,0:T(8,128)S(1)}, u32[]{:S(2)}, u32[]{:S(2)}) %collective-permute-start.4) | collective-permute-done | bytes 147488 | tf_op jit(solution)/shard_map/ppermute | solution.py:619
  19.9 2.8 %collective-permute-done.5.right_pair = f32[9,4,8,128]{3,2,1,0:T(8,128)S(1)} collective-permute-done((f32[9,4,8,128]{3,2,1,0:T(8,128)S(1)}, f32[9,4,8,128]{3,2,1,0:T(8,128)S(1)}, u32[]{:S(2)}, u32[]{:S(2)}) %collective-permute-start.5) | collective-permute-done | bytes 147488 | tf_op jit(solution)/shard_map/ppermute | solution.py:619
  22.7 2.7 %shard_map.31 = (f32[32,3,8,128]{3,2,1,0:T(8,128)S(1)}, f32[24,4,24,128]{3,2,1,0:T(8,128)S(1)}, f32[24,4,24,128]{3,2,1,0:T(8,128)S(1)}, f32[24,4,24,128]{3,2,1,0...) custom-call(f32[16,4,8,128]{3,2,1,0:T(8,128)S(1)} %get-tuple-element, ...), custom_call_target="tpu_custom_call" | custom-call | tf_op jit(solution)/shard_map/pallas_call | solution.py:574
  25.4 17.9 %all_to_all.10.plane = f32[32,3,8,128]{3,2,1,0:T(8,128)S(1)} all-to-all(f32[32,3,8,128]{3,2,1,0:T(8,128)S(1)} %get-tuple-element.43), channel_id=1, replica_groups=mesh['z'=16,'y'=4,'n'=8] {'y','n'}, dimensions={0} | all-to-all | bytes 786432 | tf_op jit(solution)/shard_map/all_to_all | solution.py:629
  43.4 0.7 collective-permute-start.8
  44.1 6.4 %collective-permute-start.9 = (f32[30,8,128]{2,1,0:T(8,128)S(1)}, f32[30,8,128]{2,1,0:T(8,128)S(1)}, u32[]{:S(2)}, u32[]{:S(2)}) collective-permute-start(f32[30,8,128]{2,1,0:T(8,128)S(1)} %get-tuple-element.45), channel_id=1, source_target_pairs={{0,32},{32,0},{64,96},{96,64},{128,160},{160,128},{192,224},{224,1... | collective-permute-start | bytes 368648 | tf_op jit(solution)/shard_map/ppermute | solution.py:633
  50.5 0.0 collective-permute-done.8
  50.5 3.0 %collective-permute-done.9 = f32[30,8,128]{2,1,0:T(8,128)S(1)} collective-permute-done((f32[30,8,128]{2,1,0:T(8,128)S(1)}, f32[30,8,128]{2,1,0:T(8,128)S(1)}, u32[]{:S(2)}, u32[]{:S(2)}) %collective-permute-start.9) | collective-permute-done | bytes 122912 | tf_op jit(solution)/shard_map/ppermute | solution.py:633
  53.6 0.6 shard_map.33
  54.2 25.6 %all_to_all.11 = f32[16,2,8,128]{3,2,1,0:T(8,128)S(1)} all-to-all(f32[16,2,8,128]{3,2,1,0:T(8,128)S(1)} %get-tuple-element.47), channel_id=1, replica_groups=mesh['z'=16,'y'=4,'n'=8] {'z'}, dimensions={0} | all-to-all | bytes 262144 | tf_op jit(solution)/shard_map/all_to_all | solution.py:642
  79.8 5.4 %all-gather = f32[32,2,8,128]{3,2,1,0:T(8,128)S(1)} all-gather(f32[16,2,8,128]{3,2,1,0:T(8,128)S(1)} %all_to_all.11), channel_id=2, replica_groups={{0,1},{2,3},{4,5},{6,7},{8,9},{10,11},{12,13},{14,15},{16,17},{18,19},{..., dimensions={0}, use_global_device_ids=true | all-gather | bytes 393216 | tf_op jit(solution)/shard_map/all_gather | solution.py:644
  85.2 5.3 %shard_map.34 = f32[8,8,512]{2,1,0:T(8,128)} custom-call(f32[2,16,2,8,128]{4,3,2,1,0:T(8,128)S(1)} %bitcast.5, f32[10,2,16,128]{3,2,1,0:T(8,128)S(1)} %get-tuple-element.48.r1h, f32[24,2,8,128]{3,2,1,0:T(8,128)S(1)} %get-tuple-element.49.x2, f32[24,2,8,128]{3,2,1,0:T(8,128)S(1)} %get-tuple-element.50.r2, f32[24,2,8,128]{3,2,1,0:T(8,128)S(1)} %get-tuple-element.51.fx2, ...), custom_call_target="tpu_custom_call" | custom-call | tf_op jit(solution)/shard_map/pallas_call | solution.py:574
  (3 shorter events, 0.1 us)
Async XLA Ops:
  1.5 16.4 %collective-permute-start.3 = (f32[16,4,8,128]{3,2,1,0:T(8,128)S(1)}, f32[16,4,8,128]{3,2,1,0:T(8,128)S(1)}, u32[]{:S(2)}, u32[]{:S(2)}) collective-permute-start(f32[16,4,8,128]{3,2,1,0:T(8,128)S(1)} %get-tuple-element.36.own), channel_id=1, source_target_pairs={{0,7},{1,0},{2,1},{3,2},{4,3},{5,4},{6,5},{7,6},{8,15},{9,8},{10,9... | collective-permute-start | bytes 786440 | tf_op jit(solution)/shard_map/ppermute | solution.py:613
  8.4 2.7 %collective-permute-start.1 = (f32[13,4,8,128]{3,2,1,0:T(8,128)S(1)}, f32[13,4,8,128]{3,2,1,0:T(8,128)S(1)}, u32[]{:S(2)}, u32[]{:S(2)}) collective-permute-start(f32[13,4,8,128]{3,2,1,0:T(8,128)S(1)} %get-tuple-element.38), channel_id=1, source_target_pairs={{8,16},{16,8},{24,32},{32,24},{40,48},{48,40},{56,64},{64,56},{72,... | collective-permute-start | bytes 638984 | tf_op jit(solution)/shard_map/ppermute | solution.py:614
  9.0 8.8 %collective-permute-start = (f32[13,4,8,128]{3,2,1,0:T(8,128)S(1)}, f32[13,4,8,128]{3,2,1,0:T(8,128)S(1)}, u32[]{:S(2)}, u32[]{:S(2)}) collective-permute-start(f32[13,4,8,128]{3,2,1,0:T(8,128)S(1)} %get-tuple-element.37), channel_id=1, source_target_pairs={{0,8},{8,0},{16,24},{24,16},{32,40},{40,32},{48,56},{56,48},{64,72... | collective-permute-start | bytes 638984 | tf_op jit(solution)/shard_map/ppermute | solution.py:615
  11.0 7.7 %collective-permute-start.2 = (f32[16,4,8,128]{3,2,1,0:T(8,128)S(1)}, f32[16,4,8,128]{3,2,1,0:T(8,128)S(1)}, u32[]{:S(2)}, u32[]{:S(2)}) collective-permute-start(f32[16,4,8,128]{3,2,1,0:T(8,128)S(1)} %get-tuple-element.36.own), channel_id=1, source_target_pairs={{0,1},{1,2},{2,3},{3,4},{4,5},{5,6},{6,7},{7,0},{8,9},{9,10},{10,1... | collective-permute-start | bytes 786440 | tf_op jit(solution)/shard_map/ppermute | solution.py:612
  11.1 7.5 %collective-permute-start.6 = (f32[9,4,8,128]{3,2,1,0:T(8,128)S(1)}, f32[9,4,8,128]{3,2,1,0:T(8,128)S(1)}, u32[]{:S(2)}, u32[]{:S(2)}) collective-permute-start(f32[9,4,8,128]{3,2,1,0:T(8,128)S(1)} %get-tuple-element.41), channel_id=1, source_target_pairs={{0,1},{1,2},{2,3},{3,4},{4,5},{5,6},{6,7},{7,0},{8,9},{9,10},{10,1... | collective-permute-start | bytes 442376 | tf_op jit(solution)/shard_map/ppermute | solution.py:619
  11.2 7.5 %collective-permute-start.7 = (f32[9,4,8,128]{3,2,1,0:T(8,128)S(1)}, f32[9,4,8,128]{3,2,1,0:T(8,128)S(1)}, u32[]{:S(2)}, u32[]{:S(2)}) collective-permute-start(f32[9,4,8,128]{3,2,1,0:T(8,128)S(1)} %get-tuple-element.42), channel_id=1, source_target_pairs={{0,7},{1,0},{2,1},{3,2},{4,3},{5,4},{6,5},{7,6},{8,15},{9,8},{10,9... | collective-permute-start | bytes 442376 | tf_op jit(solution)/shard_map/ppermute | solution.py:619
  17.8 2.1 %collective-permute-start.4 = (f32[9,4,8,128]{3,2,1,0:T(8,128)S(1)}, f32[9,4,8,128]{3,2,1,0:T(8,128)S(1)}, u32[]{:S(2)}, u32[]{:S(2)}) collective-permute-start(f32[9,4,8,128]{3,2,1,0:T(8,128)S(1)} %get-tuple-element.39), channel_id=1, source_target_pairs={{0,1},{1,2},{2,3},{3,4},{4,5},{5,6},{6,7},{7,0},{8,9},{9,10},{10,1... | collective-permute-start | bytes 442376 | tf_op jit(solution)/shard_map/ppermute | solution.py:619
  17.9 4.9 %collective-permute-start.5 = (f32[9,4,8,128]{3,2,1,0:T(8,128)S(1)}, f32[9,4,8,128]{3,2,1,0:T(8,128)S(1)}, u32[]{:S(2)}, u32[]{:S(2)}) collective-permute-start(f32[9,4,8,128]{3,2,1,0:T(8,128)S(1)} %get-tuple-element.40), channel_id=1, source_target_pairs={{0,7},{1,0},{2,1},{3,2},{4,3},{5,4},{6,5},{7,6},{8,15},{9,8},{10,9... | collective-permute-start | bytes 442376 | tf_op jit(solution)/shard_map/ppermute | solution.py:619
  43.4 7.1 %collective-permute-start.8 = (f32[30,8,128]{2,1,0:T(8,128)S(1)}, f32[30,8,128]{2,1,0:T(8,128)S(1)}, u32[]{:S(2)}, u32[]{:S(2)}) collective-permute-start(f32[30,8,128]{2,1,0:T(8,128)S(1)} %get-tuple-element.44), channel_id=1, source_target_pairs={{32,64},{64,32},{96,128},{128,96},{160,192},{192,160},{224,256},{2... | collective-permute-start | bytes 368648 | tf_op jit(solution)/shard_map/ppermute | solution.py:632
  44.1 9.5 %collective-permute-start.9 = (f32[30,8,128]{2,1,0:T(8,128)S(1)}, f32[30,8,128]{2,1,0:T(8,128)S(1)}, u32[]{:S(2)}, u32[]{:S(2)}) collective-permute-start(f32[30,8,128]{2,1,0:T(8,128)S(1)} %get-tuple-element.45), channel_id=1, source_target_pairs={{0,32},{32,0},{64,96},{96,64},{128,160},{160,128},{192,224},{224,1... | collective-permute-start | bytes 368648 | tf_op jit(solution)/shard_map/ppermute | solution.py:633

commit v5 on v4

--- a/solution.py
+++ b/solution.py
@@ -193,8 +193,12 @@
             out.append(jnp.concatenate([parts[0] * keep_0, parts[1], parts[2] * keep_1] if field == 0 else parts, axis=0))
         return out
 
+    planes = {}
+
     def cells(p):
-        return plane(0, p, keep_left, keep_right)
+        if p not in planes:
+            planes[p] = plane(0, p, keep_left, keep_right)
+        return planes[p]
 
     def source(p):
         return plane(1, p, None, None)
@@ -203,8 +207,16 @@
     for q in range(4):
         fx[1, q] = 0.5 * (before[q] + after[q])
 
+    def cells_1(k):
+        one, two = cells(2 + 2 * k), cells(3 + 2 * k)
+        for q in range(2):
+            sums[8 + k, q, 0:24] = (one[2 * q] + one[2 * q + 1]) + (two[2 * q] + two[2 * q + 1])
+            sums[8 + k, q, 24:32] = jnp.zeros((8, 128), F32)
+
     def faces_0(p):
         c, c_next, b = cells(p), cells(p + 1), source(p)
+        if p % 2:
+            cells_1((p - 3) // 2)
         gx, gz, gy, d = plane_faces(c, c_next, [fx[p - 1, q] for q in range(4)], 0.5, 1, last, begin)
         for q in range(4):
             fx[p, q], fy[p, q], fz[p, q], diag[p, q] = gx[q], gy[q], gz[q], d[q]
@@ -233,14 +245,6 @@
             sums[k, q, 24:32] = jnp.zeros((8, 128), F32)
 
     loop(0, 8, residual_0)
-
-    def cells_1(k):
-        one, two = cells(2 + 2 * k), cells(3 + 2 * k)
-        for q in range(2):
-            sums[8 + k, q, 0:24] = (one[2 * q] + one[2 * q + 1]) + (two[2 * q] + two[2 * q + 1])
-            sums[8 + k, q, 24:32] = jnp.zeros((8, 128), F32)
-
-    loop(0, 10, cells_1)
 
     def halve(k, q):
         return 0.125 * (sums[k, q, pl.ds(0, 16, stride=2), :] + sums[k, q, pl.ds(1, 16, stride=2), :])

time: 90.7 us -> 90.6 us (level)
  no operation moved by 1% of the time
where the time goes in v5:
time: 90.6 us; the launch traced here: 90.3 us
  blocking collectives  48.9 us (54%)
  starting transfers between devices  18.7 us (21%)
  waiting for transfers between devices  12.6 us (14%)
  Pallas kernels  10 us (11%)
    all_to_all x1, blocking collectives, shards(): gathered = lax.all_to_all(sent, 'z', 0, 0)  25.6 us
    all_to_all x1, blocking collectives, shards(): plane = lax.all_to_all(packed, ('y', 'n'), 0, 0)  17.9 us
    pallas_call x6, Pallas kernels, call(): pl.pallas_call(kernel, out_shape=shapes, in_specs=[pl.BlockSpec(memory_sp...  8.54 us
    ppermute x1, starting transfers between devices, shards(): own_right = lax.ppermute(own, 'n', ring(size, -1))  6.89 us
    ppermute x1, starting transfers between devices, shards(): pair = lax.ppermute(to_pair, 'z', pairs(tall))  6.42 us
    ppermute x1, waiting for transfers between devices, shards(): pair = lax.ppermute(to_pair, ('z', 'y'), pairs(wide))  5.53 us
    all_gather x1, blocking collectives, shards(): gathered = lax.all_gather(gathered, 'n', axis_index_groups=cores)  5.4 us
    ppermute x1, waiting for transfers between devices, shards(): pair = lax.ppermute(to_pair, 'z', pairs(tall))  3.05 us
  transfers between devices with their start and end apart: 10, of which 4 were waited for; matrix products, arithmetic and copies ran while one was open for 0% of the time, Pallas kernels for 0%

profile of v5, /device:TPU:1, one launch (start us, length us, event | category | flops | bytes accessed | tf_op | source)
XLA Modules:
  0.0 90.3 jit_solution(9508731231891750281)
XLA Ops:
  0.0 1.5 %shard_map.28 = (f32[16,4,8,128]{3,2,1,0:T(8,128)S(1)}, f32[13,4,8,128]{3,2,1,0:T(8,128)S(1)}, f32[13,4,8,128]{3,2,1,0:T(8,128)S(1)}) custom-call(f32[8,8,512]{2,1,0:T(8,128)} %rhs_hbm.1, f32[8,8,512]{2,1,0:T(8,128)} %beta_hbm.1), custom_call_target="tpu_custom_call" | custom-call | tf_op jit(solution)/shard_map/pallas_call | solution.py:590
  1.5 6.9 %collective-permute-start.3 = (f32[16,4,8,128]{3,2,1,0:T(8,128)S(1)}, f32[16,4,8,128]{3,2,1,0:T(8,128)S(1)}, u32[]{:S(2)}, u32[]{:S(2)}) collective-permute-start(f32[16,4,8,128]{3,2,1,0:T(8,128)S(1)} %get-tuple-element.36.own), channel_id=1, source_target_pairs={{0,7},{1,0},{2,1},{3,2},{4,3},{5,4},{6,5},{7,6},{8,15},{9,8},{10,9... | collective-permute-start | bytes 786440 | tf_op jit(solution)/shard_map/ppermute | solution.py:617
  8.4 0.7 collective-permute-start.1
  9.0 1.9 %collective-permute-start = (f32[13,4,8,128]{3,2,1,0:T(8,128)S(1)}, f32[13,4,8,128]{3,2,1,0:T(8,128)S(1)}, u32[]{:S(2)}, u32[]{:S(2)}) collective-permute-start(f32[13,4,8,128]{3,2,1,0:T(8,128)S(1)} %get-tuple-element.37), channel_id=1, source_target_pairs={{0,8},{8,0},{16,24},{24,16},{32,40},{40,32},{48,56},{56,48},{64,72... | collective-permute-start | bytes 638984 | tf_op jit(solution)/shard_map/ppermute | solution.py:619
  11.0 0.1 collective-permute-start.2
  11.1 0.0 collective-permute-done.1.planes.other
  11.1 0.0 collective-permute-start.6
  11.2 1.1 %collective-permute-start.7 = (f32[9,4,8,128]{3,2,1,0:T(8,128)S(1)}, f32[9,4,8,128]{3,2,1,0:T(8,128)S(1)}, u32[]{:S(2)}, u32[]{:S(2)}) collective-permute-start(f32[9,4,8,128]{3,2,1,0:T(8,128)S(1)} %get-tuple-element.42), channel_id=1, source_target_pairs={{0,7},{1,0},{2,1},{3,2},{4,3},{5,4},{6,5},{7,6},{8,15},{9,8},{10,9... | collective-permute-start | bytes 442376 | tf_op jit(solution)/shard_map/ppermute | solution.py:623
  12.3 5.5 %collective-permute-done.planes.pair = f32[13,4,8,128]{3,2,1,0:T(8,128)S(1)} collective-permute-done((f32[13,4,8,128]{3,2,1,0:T(8,128)S(1)}, f32[13,4,8,128]{3,2,1,0:T(8,128)S(1)}, u32[]{:S(2)}, u32[]{:S(2)}) %collective-permute-start) | collective-permute-done | bytes 213024 | tf_op jit(solution)/shard_map/ppermute | solution.py:619
  17.8 0.0 collective-permute-start.4
  17.8 0.0 collective-permute-done.3.own_right
  17.9 0.8 collective-permute-start.5
  18.7 0.0 collective-permute-done.2.own_left
  18.7 0.0 collective-permute-done.6.left_other
  18.7 0.0 collective-permute-done.7.right_other
  18.7 1.3 %collective-permute-done.4.left_pair = f32[9,4,8,128]{3,2,1,0:T(8,128)S(1)} collective-permute-done((f32[9,4,8,128]{3,2,1,0:T(8,128)S(1)}, f32[9,4,8,128]{3,2,1,0:T(8,128)S(1)}, u32[]{:S(2)}, u32[]{:S(2)}) %collective-permute-start.4) | collective-permute-done | bytes 147488 | tf_op jit(solution)/shard_map/ppermute | solution.py:623
  19.9 2.8 %collective-permute-done.5.right_pair = f32[9,4,8,128]{3,2,1,0:T(8,128)S(1)} collective-permute-done((f32[9,4,8,128]{3,2,1,0:T(8,128)S(1)}, f32[9,4,8,128]{3,2,1,0:T(8,128)S(1)}, u32[]{:S(2)}, u32[]{:S(2)}) %collective-permute-start.5) | collective-permute-done | bytes 147488 | tf_op jit(solution)/shard_map/ppermute | solution.py:623
  22.7 2.6 %shard_map.31 = (f32[32,3,8,128]{3,2,1,0:T(8,128)S(1)}, f32[24,4,24,128]{3,2,1,0:T(8,128)S(1)}, f32[24,4,24,128]{3,2,1,0:T(8,128)S(1)}, f32[24,4,24,128]{3,2,1,0...) custom-call(f32[16,4,8,128]{3,2,1,0:T(8,128)S(1)} %get-tuple-element, ...), custom_call_target="tpu_custom_call" | custom-call | tf_op jit(solution)/shard_map/pallas_call | solution.py:578
  25.3 17.9 %all_to_all.10.plane = f32[32,3,8,128]{3,2,1,0:T(8,128)S(1)} all-to-all(f32[32,3,8,128]{3,2,1,0:T(8,128)S(1)} %get-tuple-element.43), channel_id=1, replica_groups=mesh['z'=16,'y'=4,'n'=8] {'y','n'}, dimensions={0} | all-to-all | bytes 786432 | tf_op jit(solution)/shard_map/all_to_all | solution.py:633
  43.3 0.7 collective-permute-start.8
  43.9 6.4 %collective-permute-start.9 = (f32[30,8,128]{2,1,0:T(8,128)S(1)}, f32[30,8,128]{2,1,0:T(8,128)S(1)}, u32[]{:S(2)}, u32[]{:S(2)}) collective-permute-start(f32[30,8,128]{2,1,0:T(8,128)S(1)} %get-tuple-element.45), channel_id=1, source_target_pairs={{0,32},{32,0},{64,96},{96,64},{128,160},{160,128},{192,224},{224,1... | collective-permute-start | bytes 368648 | tf_op jit(solution)/shard_map/ppermute | solution.py:637
  50.4 0.0 collective-permute-done.8
  50.4 3.0 %collective-permute-done.9 = f32[30,8,128]{2,1,0:T(8,128)S(1)} collective-permute-done((f32[30,8,128]{2,1,0:T(8,128)S(1)}, f32[30,8,128]{2,1,0:T(8,128)S(1)}, u32[]{:S(2)}, u32[]{:S(2)}) %collective-permute-start.9) | collective-permute-done | bytes 122912 | tf_op jit(solution)/shard_map/ppermute | solution.py:637
  53.4 0.6 shard_map.33
  54.1 25.6 %all_to_all.11 = f32[16,2,8,128]{3,2,1,0:T(8,128)S(1)} all-to-all(f32[16,2,8,128]{3,2,1,0:T(8,128)S(1)} %get-tuple-element.47), channel_id=1, replica_groups=mesh['z'=16,'y'=4,'n'=8] {'z'}, dimensions={0} | all-to-all | bytes 262144 | tf_op jit(solution)/shard_map/all_to_all | solution.py:646
  79.7 5.4 %all-gather = f32[32,2,8,128]{3,2,1,0:T(8,128)S(1)} all-gather(f32[16,2,8,128]{3,2,1,0:T(8,128)S(1)} %all_to_all.11), channel_id=2, replica_groups={{0,1},{2,3},{4,5},{6,7},{8,9},{10,11},{12,13},{14,15},{16,17},{18,19},{..., dimensions={0}, use_global_device_ids=true | all-gather | bytes 393216 | tf_op jit(solution)/shard_map/all_gather | solution.py:648
  85.1 5.3 %shard_map.34 = f32[8,8,512]{2,1,0:T(8,128)} custom-call(f32[2,16,2,8,128]{4,3,2,1,0:T(8,128)S(1)} %bitcast.5, f32[10,2,16,128]{3,2,1,0:T(8,128)S(1)} %get-tuple-element.48.r1h, f32[24,2,8,128]{3,2,1,0:T(8,128)S(1)} %get-tuple-element.49.x2, f32[24,2,8,128]{3,2,1,0:T(8,128)S(1)} %get-tuple-element.50.r2, f32[24,2,8,128]{3,2,1,0:T(8,128)S(1)} %get-tuple-element.51.fx2, ...), custom_call_target="tpu_custom_call" | custom-call | tf_op jit(solution)/shard_map/pallas_call | solution.py:578
  (3 shorter events, 0.1 us)
Async XLA Ops:
  1.5 16.4 %collective-permute-start.3 = (f32[16,4,8,128]{3,2,1,0:T(8,128)S(1)}, f32[16,4,8,128]{3,2,1,0:T(8,128)S(1)}, u32[]{:S(2)}, u32[]{:S(2)}) collective-permute-start(f32[16,4,8,128]{3,2,1,0:T(8,128)S(1)} %get-tuple-element.36.own), channel_id=1, source_target_pairs={{0,7},{1,0},{2,1},{3,2},{4,3},{5,4},{6,5},{7,6},{8,15},{9,8},{10,9... | collective-permute-start | bytes 786440 | tf_op jit(solution)/shard_map/ppermute | solution.py:617
  8.4 2.7 %collective-permute-start.1 = (f32[13,4,8,128]{3,2,1,0:T(8,128)S(1)}, f32[13,4,8,128]{3,2,1,0:T(8,128)S(1)}, u32[]{:S(2)}, u32[]{:S(2)}) collective-permute-start(f32[13,4,8,128]{3,2,1,0:T(8,128)S(1)} %get-tuple-element.38), channel_id=1, source_target_pairs={{8,16},{16,8},{24,32},{32,24},{40,48},{48,40},{56,64},{64,56},{72,... | collective-permute-start | bytes 638984 | tf_op jit(solution)/shard_map/ppermute | solution.py:618
  9.0 8.8 %collective-permute-start = (f32[13,4,8,128]{3,2,1,0:T(8,128)S(1)}, f32[13,4,8,128]{3,2,1,0:T(8,128)S(1)}, u32[]{:S(2)}, u32[]{:S(2)}) collective-permute-start(f32[13,4,8,128]{3,2,1,0:T(8,128)S(1)} %get-tuple-element.37), channel_id=1, source_target_pairs={{0,8},{8,0},{16,24},{24,16},{32,40},{40,32},{48,56},{56,48},{64,72... | collective-permute-start | bytes 638984 | tf_op jit(solution)/shard_map/ppermute | solution.py:619
  11.0 7.7 %collective-permute-start.2 = (f32[16,4,8,128]{3,2,1,0:T(8,128)S(1)}, f32[16,4,8,128]{3,2,1,0:T(8,128)S(1)}, u32[]{:S(2)}, u32[]{:S(2)}) collective-permute-start(f32[16,4,8,128]{3,2,1,0:T(8,128)S(1)} %get-tuple-element.36.own), channel_id=1, source_target_pairs={{0,1},{1,2},{2,3},{3,4},{4,5},{5,6},{6,7},{7,0},{8,9},{9,10},{10,1... | collective-permute-start | bytes 786440 | tf_op jit(solution)/shard_map/ppermute | solution.py:616
  11.1 7.5 %collective-permute-start.6 = (f32[9,4,8,128]{3,2,1,0:T(8,128)S(1)}, f32[9,4,8,128]{3,2,1,0:T(8,128)S(1)}, u32[]{:S(2)}, u32[]{:S(2)}) collective-permute-start(f32[9,4,8,128]{3,2,1,0:T(8,128)S(1)} %get-tuple-element.41), channel_id=1, source_target_pairs={{0,1},{1,2},{2,3},{3,4},{4,5},{5,6},{6,7},{7,0},{8,9},{9,10},{10,1... | collective-permute-start | bytes 442376 | tf_op jit(solution)/shard_map/ppermute | solution.py:623
  11.2 7.5 %collective-permute-start.7 = (f32[9,4,8,128]{3,2,1,0:T(8,128)S(1)}, f32[9,4,8,128]{3,2,1,0:T(8,128)S(1)}, u32[]{:S(2)}, u32[]{:S(2)}) collective-permute-start(f32[9,4,8,128]{3,2,1,0:T(8,128)S(1)} %get-tuple-element.42), channel_id=1, source_target_pairs={{0,7},{1,0},{2,1},{3,2},{4,3},{5,4},{6,5},{7,6},{8,15},{9,8},{10,9... | collective-permute-start | bytes 442376 | tf_op jit(solution)/shard_map/ppermute | solution.py:623
  17.8 2.1 %collective-permute-start.4 = (f32[9,4,8,128]{3,2,1,0:T(8,128)S(1)}, f32[9,4,8,128]{3,2,1,0:T(8,128)S(1)}, u32[]{:S(2)}, u32[]{:S(2)}) collective-permute-start(f32[9,4,8,128]{3,2,1,0:T(8,128)S(1)} %get-tuple-element.39), channel_id=1, source_target_pairs={{0,1},{1,2},{2,3},{3,4},{4,5},{5,6},{6,7},{7,0},{8,9},{9,10},{10,1... | collective-permute-start | bytes 442376 | tf_op jit(solution)/shard_map/ppermute | solution.py:623
  17.9 4.9 %collective-permute-start.5 = (f32[9,4,8,128]{3,2,1,0:T(8,128)S(1)}, f32[9,4,8,128]{3,2,1,0:T(8,128)S(1)}, u32[]{:S(2)}, u32[]{:S(2)}) collective-permute-start(f32[9,4,8,128]{3,2,1,0:T(8,128)S(1)} %get-tuple-element.40), channel_id=1, source_target_pairs={{0,7},{1,0},{2,1},{3,2},{4,3},{5,4},{6,5},{7,6},{8,15},{9,8},{10,9... | collective-permute-start | bytes 442376 | tf_op jit(solution)/shard_map/ppermute | solution.py:623
  43.3 7.1 %collective-permute-start.8 = (f32[30,8,128]{2,1,0:T(8,128)S(1)}, f32[30,8,128]{2,1,0:T(8,128)S(1)}, u32[]{:S(2)}, u32[]{:S(2)}) collective-permute-start(f32[30,8,128]{2,1,0:T(8,128)S(1)} %get-tuple-element.44), channel_id=1, source_target_pairs={{32,64},{64,32},{96,128},{128,96},{160,192},{192,160},{224,256},{2... | collective-permute-start | bytes 368648 | tf_op jit(solution)/shard_map/ppermute | solution.py:636
  43.9 9.5 %collective-permute-start.9 = (f32[30,8,128]{2,1,0:T(8,128)S(1)}, f32[30,8,128]{2,1,0:T(8,128)S(1)}, u32[]{:S(2)}, u32[]{:S(2)}) collective-permute-start(f32[30,8,128]{2,1,0:T(8,128)S(1)} %get-tuple-element.45), channel_id=1, source_target_pairs={{0,32},{32,0},{64,96},{96,64},{128,160},{160,128},{192,224},{224,1... | collective-permute-start | bytes 368648 | tf_op jit(solution)/shard_map/ppermute | solution.py:637

commit v6 on v5

--- a/solution.py
+++ b/solution.py
@@ -108,8 +108,8 @@
 SENT = C_LOW + B_LOW
 
 CORNERS = (
-    (0, 1, 0, 0), (0, 2, 0, 0), (0, 3, 7, 2), (0, 4, 6, 3), (0, 5, 0, 0),
-    (1, 1, 6, 2), (1, 2, 0, 0), (1, 3, 5, 3), (1, 4, 0, 0),
+    (0, 1, 0, 0, 0), (0, 2, 0, 0, 0), (0, 3, 0, 7, 2), (0, 4, 0, 6, 3), (0, 5, 1, 4, 4),
+    (1, 1, 1, 6, 2), (1, 2, 0, 0, 0), (1, 3, 1, 5, 3),
 )
 
 
@@ -143,12 +143,12 @@
 
 def corner_kernel(planes, right, left):
     row = iota((8, 128), 0)
-    for t, (field, one, two, rows) in enumerate(CORNERS):
+    for t, (field, one, field_two, two, rows) in enumerate(CORNERS):
         for q in range(4):
             tile = planes[place_of(field, one), q]
             to_right = to_left = tile
             if two:
-                beside = planes[place_of(field, two), q]
+                beside = planes[place_of(field_two, two), q]
                 to_right = jnp.where(row >= rows, tile, pltpu.roll(beside, rows, 0))
                 to_left = jnp.where(row < 8 - rows, tile, pltpu.roll(beside, 8 - rows, 0))
             right[t, q] = to_right
@@ -164,10 +164,11 @@
     last, begin = lane == 127, lane == 0
 
     corner = {}
-    for t, (field, one, two, rows) in enumerate(CORNERS):
+    for t, (field, one, field_two, two, rows) in enumerate(CORNERS):
         corner[field, one] = (t, 0)
         if two:
-            corner[field, two] = (t, rows)
+            corner[field_two, two] = (t, rows)
+    tile_row = iota((8, 128), 0)
 
     def from_side(side, of_pair, of_other):
         return jnp.where(even, of_other, of_pair) if side == 0 else jnp.where(even, of_pair, of_other)
@@ -187,6 +188,9 @@
                     from_side(side, pair[at, q], other[at, q]),
                     from_side(side, right_pair[t, q], right_other[t, q]),
                 ]
+                if (field, distance) == (0, 5):
+                    parts[0] = jnp.where(tile_row >= 4, parts[0], 0.0)
+                    parts[2] = jnp.where(tile_row < 4, parts[2], 0.0)
                 if rows:
                     parts[0] = pltpu.roll(parts[0], 8 - rows, 0)
                     parts[2] = pltpu.roll(parts[2], rows, 0)

time: 90.6 us -> 90.4 us (level)
  no operation moved by 1% of the time
where the time goes in v6:
time: 90.4 us; the launch traced here: 90.2 us
  blocking collectives  48.9 us (54%)
  starting transfers between devices  18.7 us (21%)
  waiting for transfers between devices  12.5 us (14%)
  Pallas kernels  10 us (11%)
    all_to_all x1, blocking collectives, shards(): gathered = lax.all_to_all(sent, 'z', 0, 0)  25.6 us
    all_to_all x1, blocking collectives, shards(): plane = lax.all_to_all(packed, ('y', 'n'), 0, 0)  17.9 us
    pallas_call x6, Pallas kernels, call(): pl.pallas_call(kernel, out_shape=shapes, in_specs=[pl.BlockSpec(memory_sp...  8.55 us
    ppermute x1, starting transfers between devices, shards(): own_right = lax.ppermute(own, 'n', ring(size, -1))  6.89 us
    ppermute x1, starting transfers between devices, shards(): pair = lax.ppermute(to_pair, 'z', pairs(tall))  6.42 us
    ppermute x1, waiting for transfers between devices, shards(): pair = lax.ppermute(to_pair, ('z', 'y'), pairs(wide))  5.53 us
    all_gather x1, blocking collectives, shards(): gathered = lax.all_gather(gathered, 'n', axis_index_groups=cores)  5.4 us
    ppermute x1, waiting for transfers between devices, shards(): pair = lax.ppermute(to_pair, 'z', pairs(tall))  3.05 us
  transfers between devices with their start and end apart: 10, of which 4 were waited for; matrix products, arithmetic and copies ran while one was open for 0% of the time, Pallas kernels for 0%

profile of v6, /device:TPU:1, one launch (start us, length us, event | category | flops | bytes accessed | tf_op | source)
XLA Modules:
  0.0 90.2 jit_solution(10112699784894074466)
XLA Ops:
  0.0 1.5 %shard_map.28 = (f32[16,4,8,128]{3,2,1,0:T(8,128)S(1)}, f32[13,4,8,128]{3,2,1,0:T(8,128)S(1)}, f32[13,4,8,128]{3,2,1,0:T(8,128)S(1)}) custom-call(f32[8,8,512]{2,1,0:T(8,128)} %rhs_hbm.1, f32[8,8,512]{2,1,0:T(8,128)} %beta_hbm.1), custom_call_target="tpu_custom_call" | custom-call | tf_op jit(solution)/shard_map/pallas_call | solution.py:594
  1.5 6.9 %collective-permute-start.3 = (f32[16,4,8,128]{3,2,1,0:T(8,128)S(1)}, f32[16,4,8,128]{3,2,1,0:T(8,128)S(1)}, u32[]{:S(2)}, u32[]{:S(2)}) collective-permute-start(f32[16,4,8,128]{3,2,1,0:T(8,128)S(1)} %get-tuple-element.36.own), channel_id=1, source_target_pairs={{0,7},{1,0},{2,1},{3,2},{4,3},{5,4},{6,5},{7,6},{8,15},{9,8},{10,9... | collective-permute-start | bytes 786440 | tf_op jit(solution)/shard_map/ppermute | solution.py:621
  8.4 0.7 collective-permute-start.1
  9.0 1.9 %collective-permute-start = (f32[13,4,8,128]{3,2,1,0:T(8,128)S(1)}, f32[13,4,8,128]{3,2,1,0:T(8,128)S(1)}, u32[]{:S(2)}, u32[]{:S(2)}) collective-permute-start(f32[13,4,8,128]{3,2,1,0:T(8,128)S(1)} %get-tuple-element.37), channel_id=1, source_target_pairs={{0,8},{8,0},{16,24},{24,16},{32,40},{40,32},{48,56},{56,48},{64,72... | collective-permute-start | bytes 638984 | tf_op jit(solution)/shard_map/ppermute | solution.py:623
  11.0 0.1 collective-permute-start.2
  11.1 0.0 collective-permute-done.1.planes.other
  11.1 0.0 collective-permute-start.6
  11.2 1.1 %collective-permute-start.7 = (f32[8,4,8,128]{3,2,1,0:T(8,128)S(1)}, f32[8,4,8,128]{3,2,1,0:T(8,128)S(1)}, u32[]{:S(2)}, u32[]{:S(2)}) collective-permute-start(f32[8,4,8,128]{3,2,1,0:T(8,128)S(1)} %get-tuple-element.42), channel_id=1, source_target_pairs={{0,7},{1,0},{2,1},{3,2},{4,3},{5,4},{6,5},{7,6},{8,15},{9,8},{10,9... | collective-permute-start | bytes 393224 | tf_op jit(solution)/shard_map/ppermute | solution.py:627
  12.3 5.5 %collective-permute-done.planes.pair = f32[13,4,8,128]{3,2,1,0:T(8,128)S(1)} collective-permute-done((f32[13,4,8,128]{3,2,1,0:T(8,128)S(1)}, f32[13,4,8,128]{3,2,1,0:T(8,128)S(1)}, u32[]{:S(2)}, u32[]{:S(2)}) %collective-permute-start) | collective-permute-done | bytes 213024 | tf_op jit(solution)/shard_map/ppermute | solution.py:623
  17.8 0.0 collective-permute-start.4
  17.8 0.0 collective-permute-done.3.own_right
  17.9 0.8 collective-permute-start.5
  18.7 0.0 collective-permute-done.2.own_left
  18.7 0.0 collective-permute-done.6.left_other
  18.7 0.0 collective-permute-done.7.right_other
  18.7 1.1 %collective-permute-done.4.left_pair = f32[8,4,8,128]{3,2,1,0:T(8,128)S(1)} collective-permute-done((f32[8,4,8,128]{3,2,1,0:T(8,128)S(1)}, f32[8,4,8,128]{3,2,1,0:T(8,128)S(1)}, u32[]{:S(2)}, u32[]{:S(2)}) %collective-permute-start.4) | collective-permute-done | bytes 131104 | tf_op jit(solution)/shard_map/ppermute | solution.py:627
  19.8 2.8 %collective-permute-done.5.right_pair = f32[8,4,8,128]{3,2,1,0:T(8,128)S(1)} collective-permute-done((f32[8,4,8,128]{3,2,1,0:T(8,128)S(1)}, f32[8,4,8,128]{3,2,1,0:T(8,128)S(1)}, u32[]{:S(2)}, u32[]{:S(2)}) %collective-permute-start.5) | collective-permute-done | bytes 131104 | tf_op jit(solution)/shard_map/ppermute | solution.py:627
  22.6 2.6 %shard_map.31 = (f32[32,3,8,128]{3,2,1,0:T(8,128)S(1)}, f32[24,4,24,128]{3,2,1,0:T(8,128)S(1)}, f32[24,4,24,128]{3,2,1,0:T(8,128)S(1)}, f32[24,4,24,128]{3,2,1,0...) custom-call(f32[16,4,8,128]{3,2,1,0:T(8,128)S(1)} %get-tuple-element, ...), custom_call_target="tpu_custom_call" | custom-call | tf_op jit(solution)/shard_map/pallas_call | solution.py:582
  25.1 17.9 %all_to_all.10.plane = f32[32,3,8,128]{3,2,1,0:T(8,128)S(1)} all-to-all(f32[32,3,8,128]{3,2,1,0:T(8,128)S(1)} %get-tuple-element.43), channel_id=1, replica_groups=mesh['z'=16,'y'=4,'n'=8] {'y','n'}, dimensions={0} | all-to-all | bytes 786432 | tf_op jit(solution)/shard_map/all_to_all | solution.py:637
  43.1 0.7 collective-permute-start.8
  43.8 6.4 %collective-permute-start.9 = (f32[30,8,128]{2,1,0:T(8,128)S(1)}, f32[30,8,128]{2,1,0:T(8,128)S(1)}, u32[]{:S(2)}, u32[]{:S(2)}) collective-permute-start(f32[30,8,128]{2,1,0:T(8,128)S(1)} %get-tuple-element.45), channel_id=1, source_target_pairs={{0,32},{32,0},{64,96},{96,64},{128,160},{160,128},{192,224},{224,1... | collective-permute-start | bytes 368648 | tf_op jit(solution)/shard_map/ppermute | solution.py:641
  50.2 0.0 collective-permute-done.8
  50.2 3.0 %collective-permute-done.9 = f32[30,8,128]{2,1,0:T(8,128)S(1)} collective-permute-done((f32[30,8,128]{2,1,0:T(8,128)S(1)}, f32[30,8,128]{2,1,0:T(8,128)S(1)}, u32[]{:S(2)}, u32[]{:S(2)}) %collective-permute-start.9) | collective-permute-done | bytes 122912 | tf_op jit(solution)/shard_map/ppermute | solution.py:641
  53.3 0.6 shard_map.33
  53.9 25.6 %all_to_all.11 = f32[16,2,8,128]{3,2,1,0:T(8,128)S(1)} all-to-all(f32[16,2,8,128]{3,2,1,0:T(8,128)S(1)} %get-tuple-element.47), channel_id=1, replica_groups=mesh['z'=16,'y'=4,'n'=8] {'z'}, dimensions={0} | all-to-all | bytes 262144 | tf_op jit(solution)/shard_map/all_to_all | solution.py:650
  79.5 5.4 %all-gather = f32[32,2,8,128]{3,2,1,0:T(8,128)S(1)} all-gather(f32[16,2,8,128]{3,2,1,0:T(8,128)S(1)} %all_to_all.11), channel_id=2, replica_groups={{0,1},{2,3},{4,5},{6,7},{8,9},{10,11},{12,13},{14,15},{16,17},{18,19},{..., dimensions={0}, use_global_device_ids=true | all-gather | bytes 393216 | tf_op jit(solution)/shard_map/all_gather | solution.py:652
  84.9 5.3 %shard_map.34 = f32[8,8,512]{2,1,0:T(8,128)} custom-call(f32[2,16,2,8,128]{4,3,2,1,0:T(8,128)S(1)} %bitcast.5, f32[10,2,16,128]{3,2,1,0:T(8,128)S(1)} %get-tuple-element.48.r1h, f32[24,2,8,128]{3,2,1,0:T(8,128)S(1)} %get-tuple-element.49.x2, f32[24,2,8,128]{3,2,1,0:T(8,128)S(1)} %get-tuple-element.50.r2, f32[24,2,8,128]{3,2,1,0:T(8,128)S(1)} %get-tuple-element.51.fx2, ...), custom_call_target="tpu_custom_call" | custom-call | tf_op jit(solution)/shard_map/pallas_call | solution.py:582
  (3 shorter events, 0.1 us)
Async XLA Ops:
  1.5 16.4 %collective-permute-start.3 = (f32[16,4,8,128]{3,2,1,0:T(8,128)S(1)}, f32[16,4,8,128]{3,2,1,0:T(8,128)S(1)}, u32[]{:S(2)}, u32[]{:S(2)}) collective-permute-start(f32[16,4,8,128]{3,2,1,0:T(8,128)S(1)} %get-tuple-element.36.own), channel_id=1, source_target_pairs={{0,7},{1,0},{2,1},{3,2},{4,3},{5,4},{6,5},{7,6},{8,15},{9,8},{10,9... | collective-permute-start | bytes 786440 | tf_op jit(solution)/shard_map/ppermute | solution.py:621
  8.4 2.7 %collective-permute-start.1 = (f32[13,4,8,128]{3,2,1,0:T(8,128)S(1)}, f32[13,4,8,128]{3,2,1,0:T(8,128)S(1)}, u32[]{:S(2)}, u32[]{:S(2)}) collective-permute-start(f32[13,4,8,128]{3,2,1,0:T(8,128)S(1)} %get-tuple-element.38), channel_id=1, source_target_pairs={{8,16},{16,8},{24,32},{32,24},{40,48},{48,40},{56,64},{64,56},{72,... | collective-permute-start | bytes 638984 | tf_op jit(solution)/shard_map/ppermute | solution.py:622
  9.0 8.8 %collective-permute-start = (f32[13,4,8,128]{3,2,1,0:T(8,128)S(1)}, f32[13,4,8,128]{3,2,1,0:T(8,128)S(1)}, u32[]{:S(2)}, u32[]{:S(2)}) collective-permute-start(f32[13,4,8,128]{3,2,1,0:T(8,128)S(1)} %get-tuple-element.37), channel_id=1, source_target_pairs={{0,8},{8,0},{16,24},{24,16},{32,40},{40,32},{48,56},{56,48},{64,72... | collective-permute-start | bytes 638984 | tf_op jit(solution)/shard_map/ppermute | solution.py:623
  11.0 7.7 %collective-permute-start.2 = (f32[16,4,8,128]{3,2,1,0:T(8,128)S(1)}, f32[16,4,8,128]{3,2,1,0:T(8,128)S(1)}, u32[]{:S(2)}, u32[]{:S(2)}) collective-permute-start(f32[16,4,8,128]{3,2,1,0:T(8,128)S(1)} %get-tuple-element.36.own), channel_id=1, source_target_pairs={{0,1},{1,2},{2,3},{3,4},{4,5},{5,6},{6,7},{7,0},{8,9},{9,10},{10,1... | collective-permute-start | bytes 786440 | tf_op jit(solution)/shard_map/ppermute | solution.py:620
  11.1 7.5 %collective-permute-start.6 = (f32[8,4,8,128]{3,2,1,0:T(8,128)S(1)}, f32[8,4,8,128]{3,2,1,0:T(8,128)S(1)}, u32[]{:S(2)}, u32[]{:S(2)}) collective-permute-start(f32[8,4,8,128]{3,2,1,0:T(8,128)S(1)} %get-tuple-element.41), channel_id=1, source_target_pairs={{0,1},{1,2},{2,3},{3,4},{4,5},{5,6},{6,7},{7,0},{8,9},{9,10},{10,1... | collective-permute-start | bytes 393224 | tf_op jit(solution)/shard_map/ppermute | solution.py:627
  11.2 7.5 %collective-permute-start.7 = (f32[8,4,8,128]{3,2,1,0:T(8,128)S(1)}, f32[8,4,8,128]{3,2,1,0:T(8,128)S(1)}, u32[]{:S(2)}, u32[]{:S(2)}) collective-permute-start(f32[8,4,8,128]{3,2,1,0:T(8,128)S(1)} %get-tuple-element.42), channel_id=1, source_target_pairs={{0,7},{1,0},{2,1},{3,2},{4,3},{5,4},{6,5},{7,6},{8,15},{9,8},{10,9... | collective-permute-start | bytes 393224 | tf_op jit(solution)/shard_map/ppermute | solution.py:627
  17.8 2.0 %collective-permute-start.4 = (f32[8,4,8,128]{3,2,1,0:T(8,128)S(1)}, f32[8,4,8,128]{3,2,1,0:T(8,128)S(1)}, u32[]{:S(2)}, u32[]{:S(2)}) collective-permute-start(f32[8,4,8,128]{3,2,1,0:T(8,128)S(1)} %get-tuple-element.39), channel_id=1, source_target_pairs={{0,1},{1,2},{2,3},{3,4},{4,5},{5,6},{6,7},{7,0},{8,9},{9,10},{10,1... | collective-permute-start | bytes 393224 | tf_op jit(solution)/shard_map/ppermute | solution.py:627
  17.9 4.7 %collective-permute-start.5 = (f32[8,4,8,128]{3,2,1,0:T(8,128)S(1)}, f32[8,4,8,128]{3,2,1,0:T(8,128)S(1)}, u32[]{:S(2)}, u32[]{:S(2)}) collective-permute-start(f32[8,4,8,128]{3,2,1,0:T(8,128)S(1)} %get-tuple-element.40), channel_id=1, source_target_pairs={{0,7},{1,0},{2,1},{3,2},{4,3},{5,4},{6,5},{7,6},{8,15},{9,8},{10,9... | collective-permute-start | bytes 393224 | tf_op jit(solution)/shard_map/ppermute | solution.py:627
  43.1 7.1 %collective-permute-start.8 = (f32[30,8,128]{2,1,0:T(8,128)S(1)}, f32[30,8,128]{2,1,0:T(8,128)S(1)}, u32[]{:S(2)}, u32[]{:S(2)}) collective-permute-start(f32[30,8,128]{2,1,0:T(8,128)S(1)} %get-tuple-element.44), channel_id=1, source_target_pairs={{32,64},{64,32},{96,128},{128,96},{160,192},{192,160},{224,256},{2... | collective-permute-start | bytes 368648 | tf_op jit(solution)/shard_map/ppermute | solution.py:640
  43.8 9.5 %collective-permute-start.9 = (f32[30,8,128]{2,1,0:T(8,128)S(1)}, f32[30,8,128]{2,1,0:T(8,128)S(1)}, u32[]{:S(2)}, u32[]{:S(2)}) collective-permute-start(f32[30,8,128]{2,1,0:T(8,128)S(1)} %get-tuple-element.45), channel_id=1, source_target_pairs={{0,32},{32,0},{64,96},{96,64},{128,160},{160,128},{192,224},{224,1... | collective-permute-start | bytes 368648 | tf_op jit(solution)/shard_map/ppermute | solution.py:641
